TPU v7x, 32 devices: a whole 2x2x4 slice. The times are simulated.
32 devices in a mesh: parts: 2 (over y), ffn: 4 (over z), pair: 2 (over x), rep: 2 (over core).
Axes of the slice: x: 2, y: 2, z: 4, core: 2. Of those that a mesh axis runs over, the one named last changes fastest.
Arguments:
- residual: float32 [2, 8, 16, 8192], P(None, ('parts', 'pair', 'rep'), 'ffn'), parts along dimension 1, may hold values from -6 to 6
- query: bfloat16 [2, 8, 16, 8192], P(None, ('parts', 'pair', 'rep'), 'ffn'), parts along dimension 1, may hold values from -6 to 6
- key_cache: bfloat16 [2, 8, 16, 128, 1024], P(None, ('parts', 'pair', 'rep'), 'ffn'), parts along dimension 1, may hold values from -6 to 6
- value_cache: bfloat16 [2, 8, 16, 128, 1024], P(None, ('parts', 'pair', 'rep'), 'ffn'), parts along dimension 1, may hold values from -6 to 6
- cache_len: int32 [2, 8, 16], P(None, ('parts', 'pair', 'rep'), 'ffn'), parts along dimension 1, may hold values from 32 to 128, as said below
- partner_table: int32 [4, 4], P('parts'), parts along dimension 0, may hold values from 0 to 3, each once within a row
- norm_gain: float32 [8192], replicated, may hold values from 0.1 to 1.9
- gate_weight: bfloat16 [8192, 14336], P(('pair', 'rep'), 'ffn'), may hold values from -0.0625 to 0.0625
- up_weight: bfloat16 [8192, 14336], P(('pair', 'rep'), 'ffn'), may hold values from -0.0625 to 0.0625
- down_weight: bfloat16 [14336, 8192], P('ffn', ('pair', 'rep')), may hold values from -0.046875 to 0.046875
Outputs:
- new_residual: float32 [2, 8, 16, 8192], P(None, ('parts', 'pair', 'rep'), 'ffn'), parts along dimension 1
- served_hidden: bfloat16 [2, 8, 16, 14336], P(None, ('parts', 'pair', 'rep'), None, 'ffn'), parts along dimension 1
There are 2 independent parts, one for each index of `parts`. A program takes and returns all parts, laid end to end along the dimension named above; an argument that names none is the same for every part. Nothing has to cross between parts.
Inputs may be any that keep to these rules, and one draw needn't show every extreme that they name: `cache_len`: one entry of each sequence's new token; some sequence has exactly 128. `partner_table`: each row names every column once.
All inputs are finite; a program needn't handle non-finite values.
Results may differ from a plain program's by a relative error of at most 0.0085.
Values may be sent and summed in bfloat16 or wider, within the bound.
No kernel may reach another device: no remote copies, remote signals or barrier semaphores. Data moves between devices by JAX's collectives and lax.ppermute only.
A program may use at most 128 MiB of HBM per device.

v0:
```python
import math

import jax
import jax.numpy as jnp
from jax import lax
from jax.sharding import PartitionSpec as P

HEADS = 64
KVH = 8
HD = 128


def attend_local(query, key_cache, value_cache, cache_len):
    batches = query.shape[0]
    rows = query.shape[2]
    cache = key_cache.shape[3]
    scale = 1.0 / math.sqrt(HD)
    queries = query.reshape(batches, rows, KVH, HEADS // KVH, HD)
    keys = key_cache.reshape(batches, rows, cache, KVH, HD)
    values = value_cache.reshape(batches, rows, cache, KVH, HD)
    scores = (
        jnp.einsum("brkgd,brlkd->brkgl", queries, keys, preferred_element_type=jnp.float32) * scale
    )
    valid = (jnp.arange(cache)[None, None, :] < cache_len[:, 0, :, None])[:, :, None, None, :]
    scores = jnp.where(valid, scores, -1e30)
    peak = jnp.max(scores, axis=-1, keepdims=True)
    raised = jnp.exp(scores - peak)
    attn_probs = (raised / jnp.sum(raised, axis=-1, keepdims=True)).astype(jnp.bfloat16)
    mixed = jnp.einsum("brkgl,brlkd->brkgd", attn_probs, values, preferred_element_type=jnp.float32)
    return mixed.astype(jnp.bfloat16).reshape(batches, rows, HEADS * HD)


def activate(sums, width):
    return (jax.nn.silu(sums[..., :width]) * sums[..., width:]).astype(jnp.bfloat16)


def layer_step(
    residual,
    query,
    key_cache,
    value_cache,
    cache_len,
    partner_table,
    norm_gain,
    gate_up,
    down_weight,
):
    column = lax.axis_index(("pair", "rep"))
    width = down_weight.shape[0]
    attn = attend_local(query, key_cache, value_cache, cache_len)
    stream = residual[:, 0] + attn.astype(jnp.float32)
    normed = (
        stream * lax.rsqrt(jnp.mean(stream * stream, axis=-1, keepdims=True) + 1e-05) * norm_gain
    ).astype(jnp.bfloat16)
    routed = lax.all_to_all(
        normed[:, None], ("pair", "rep"), split_axis=3, concat_axis=1, tiled=True
    )
    partial_value = jnp.einsum(
        "bgrd,df->bgrf",
        lax.all_gather(routed, "ffn", axis=2, tiled=True),
        gate_up,
        preferred_element_type=jnp.float32,
    )
    summed = lax.psum(partial_value, ("pair", "rep"))
    hidden = activate(summed, width)
    owner = (partner_table == column).astype(jnp.bfloat16)
    served = jnp.einsum("ba,barf->brf", owner, hidden, preferred_element_type=jnp.float32).astype(
        jnp.bfloat16
    )[:, None]
    rows_first = jnp.transpose(hidden, (2, 0, 1, 3))
    shares = lax.psum_scatter(
        jnp.einsum("rbgf,fd->rbgd", rows_first, down_weight, preferred_element_type=jnp.float32),
        "ffn",
        scatter_dimension=0,
        tiled=True,
    )
    change = shares.astype(jnp.bfloat16)
    arrived = lax.all_to_all(change, ("pair", "rep"), split_axis=2, concat_axis=3, tiled=True)
    updated = stream + jnp.transpose(arrived[:, :, 0], (1, 0, 2)).astype(jnp.float32)
    return (updated[:, None], served)


def per_device(
    residual,
    query,
    key_cache,
    value_cache,
    cache_len,
    partner_table,
    norm_gain,
    gate_weight,
    up_weight,
    down_weight,
):
    gate_up = jnp.concatenate([gate_weight, up_weight], axis=1)
    updated_list = []
    served_list = []
    for micro in range(residual.shape[0]):
        updated, served = layer_step(
            residual[micro : micro + 1],
            query[micro : micro + 1],
            key_cache[micro : micro + 1],
            value_cache[micro : micro + 1],
            cache_len[micro : micro + 1],
            partner_table[micro : micro + 1],
            norm_gain,
            gate_up,
            down_weight,
        )
        updated_list.append(updated)
        served_list.append(served)
    return (jnp.concatenate(updated_list, axis=0), jnp.concatenate(served_list, axis=0))


def solution(mesh):
    placed = (
        P(None, ("parts", "pair", "rep"), "ffn", None),
        P(None, ("parts", "pair", "rep"), "ffn", None),
        P(None, ("parts", "pair", "rep"), "ffn", None, None),
        P(None, ("parts", "pair", "rep"), "ffn", None, None),
        P(None, ("parts", "pair", "rep"), "ffn"),
        P("parts", None),
        P(),
        P(("pair", "rep"), "ffn"),
        P(("pair", "rep"), "ffn"),
        P("ffn", ("pair", "rep")),
    )
    return jax.shard_map(
        per_device,
        mesh=mesh,
        in_specs=placed,
        out_specs=(
            P(None, ("parts", "pair", "rep"), "ffn", None),
            P(None, ("parts", "pair", "rep"), None, "ffn"),
        ),
        check_vma=False,
    )
```

profile of v0, /device:TPU:0, one launch (start us, length us, event | category | flops | bytes accessed | tf_op | source)
XLA Modules:
  0.0 398.4 jit_solution(7050041935214680735)
XLA Ops:
  27.0 6.8 %copy.98 = bf16[1,1,4,8192]{2,1,0,3:T(2,128)(2,1)} copy(bf16[1,1,4,8192]{3,2,1,0:T(4,128)(2,1)S(1)} %get-tuple-element.16) | data formatting | bytes 131072 | tf_op jit(solution)/shard_map/convert_element_type | solution.py:54
  34.4 45.2 %reduce.11 = bf16[8192,4]{1,0:T(8,128)(2,1)S(1)} reduce(bf16[8192,1,1,4]{3,2,1,0:T(2,128)(2,1)} %bitcast.140, bf16[]{:T(256)} %broadcast.121), dimensions={1,2}, to_apply=%bitcast.124.reduce_sub_computation | reduce | bytes 131074
  79.6 4.6 %reshape.418 = bf16[4,2,4096]{2,1,0:T(2,128)(2,1)} reshape(bf16[8192,4]{1,0:T(8,128)(2,1)S(1)} %reduce.11) | data formatting | bytes 131072
  84.2 4.2 %all-to-all-start = ((bf16[4,2,4096]{2,1,0:T(2,128)(2,1)}), bf16[4,2,4096]{2,1,0:T(2,128)(2,1)S(1)}, u32[]{:S(2)}, u32[]{:S(2)}) async-start(bf16[4,2,4096]{2,1,0:T(2,128)(2,1)} %reshape.418), calls=%async_computation | async-start | bytes 131072 | tf_op jit(solution)/shard_map/all_to_all | solution.py:55
  88.4 6.8 %copy.108 = bf16[1,1,4,8192]{2,1,0,3:T(2,128)(2,1)} copy(bf16[1,1,4,8192]{3,2,1,0:T(4,128)(2,1)S(1)} %get-tuple-element.17) | data formatting | bytes 131072 | tf_op jit(solution)/shard_map/convert_element_type | solution.py:54
  95.2 45.2 %reduce.10 = bf16[8192,4]{1,0:T(8,128)(2,1)S(1)} reduce(bf16[8192,1,1,4]{3,2,1,0:T(2,128)(2,1)} %bitcast.141, bf16[]{:T(256)} %broadcast.121), dimensions={1,2}, to_apply=%bitcast.122.reduce_sub_computation | reduce | bytes 131074
  140.4 4.6 %reshape.416 = bf16[4,2,4096]{2,1,0:T(2,128)(2,1)} reshape(bf16[8192,4]{1,0:T(8,128)(2,1)S(1)} %reduce.10) | data formatting | bytes 131072
  145.0 3.5 all-to-all-start.2
  148.5 6.0 %reshape.419 = bf16[8192,1,1,4]{3,2,1,0:T(2,128)(2,1)} reshape(bf16[4,2,4096]{2,1,0:T(2,128)(2,1)S(1)} %all-to-all-done) | data formatting | bytes 131072
  154.6 8.1 %copy.99 = bf16[1,1,4,8192]{3,2,1,0:T(4,128)(2,1)S(1)} copy(bf16[1,1,4,8192]{2,1,0,3:T(2,128)(2,1)} %bitcast.142) | data formatting | bytes 131072 | tf_op jit(solution)/shard_map/all_to_all | solution.py:55
  162.7 14.8 %all-gather = bf16[1,4,1,16,2048]{4,1,2,0,3:T(4,128)(2,1)S(1)} all-gather(bf16[1,4,1,4,2048]{4,1,2,0,3:T(4,128)(2,1)S(1)} %bitcast.152), channel_id=2, replica_groups=mesh['parts'=2,'ffn'=4,'pair'=2,'rep'=2] {'ffn'}, dimensions={3}, use_global_device_ids=true | all-gather | bytes 327680 | tf_op jit(solution)/shard_map/all_gather | solution.py:60
  177.5 6.0 %reshape.417 = bf16[8192,1,1,4]{3,2,1,0:T(2,128)(2,1)} reshape(bf16[4,2,4096]{2,1,0:T(2,128)(2,1)S(1)} %all-to-all-done.2) | data formatting | bytes 131072
  183.6 8.1 %copy.109 = bf16[1,1,4,8192]{3,2,1,0:T(4,128)(2,1)S(1)} copy(bf16[1,1,4,8192]{2,1,0,3:T(2,128)(2,1)} %bitcast.143) | data formatting | bytes 131072 | tf_op jit(solution)/shard_map/all_to_all | solution.py:55
  191.7 14.6 %all-gather.1 = bf16[1,4,1,16,2048]{4,1,2,0,3:T(4,128)(2,1)S(1)} all-gather(bf16[1,4,1,4,2048]{4,1,2,0,3:T(4,128)(2,1)S(1)} %bitcast.153), channel_id=3, replica_groups=mesh['parts'=2,'ffn'=4,'pair'=2,'rep'=2] {'ffn'}, dimensions={3}, use_global_device_ids=true | all-gather | bytes 327680 | tf_op jit(solution)/shard_map/all_gather | solution.py:60
  206.4 12.7 %fusion.8 = f32[1,4,16,7168]{3,2,1,0:T(8,128)} fusion(bf16[2048,3584]{1,0:T(8,128)(2,1)} %param.18, bf16[2048,3584]{1,0:T(8,128)(2,1)} %param.17, bf16[1,4,1,16,2048]{4,1,2,0,3:T(4,128)(2,1)S(1)} %all-gather), kind=kOutput, calls=%fused_computation.9 | convolution fusion | flops 1937768448 | bytes 31457280 | tf_op jit(solution)/shard_map/bgrd,df->bgrf/dot_general | solution.py:58
  219.1 12.7 %fusion.9 = f32[1,4,16,7168]{3,2,1,0:T(8,128)} fusion(bf16[2048,3584]{1,0:T(8,128)(2,1)} %param.18, bf16[2048,3584]{1,0:T(8,128)(2,1)} %param.17, bf16[1,4,1,16,2048]{4,1,2,0,3:T(4,128)(2,1)S(1)} %all-gather.1), kind=kOutput, calls=%fused_computation.10 | convolution fusion | flops 1937768448 | bytes 31457280 | tf_op jit(solution)/shard_map/bgrd,df->bgrf/dot_general | solution.py:58
  233.1 77.5 %all-reduce.7.cloned.1.call-done = (f32[1,4,16,7168]{3,2,1,0:T(8,128)}, f32[1,4,16,7168]{3,2,1,0:T(8,128)}) async-done(((f32[1,4,16,7168]{3,2,1,0:T(8,128)}, f32[1,4,16,7168]{3,2,1,0:T(8,128)}), (f32[1,4,16,7168]{3,2,1,0:T(8,128)}, f32[1,4,16,7168]{3,2,1,0:T(8,128)})) %all-reduce.7.cloned.1.call-update) | async-done | bytes 3670032 | tf_op jit(solution)/shard_map/psum | solution.py:64
  314.1 8.4 %fusion.10 = f32[16,1,4,2048]{3,0,2,1:T(8,128)S(1)} fusion(bf16[3584,2048]{1,0:T(8,128)(2,1)} %param.19, f32[1,4,16,7168]{3,2,1,0:T(8,128)} %get-tuple-element.9), kind=kOutput, calls=%fused_computation.11 | convolution fusion | flops 940900352 | bytes 17039360 | tf_op jit(solution)/shard_map/rbgf,fd->rbgd/dot_general | solution.py:72
  322.5 7.9 %fusion.13 = f32[16,1,4,2048]{3,0,2,1:T(8,128)S(1)} fusion(bf16[3584,2048]{1,0:T(8,128)(2,1)} %param.19, f32[1,4,16,7168]{3,2,1,0:T(8,128)S(1)} %copy-done), kind=kOutput, calls=%fused_computation.12 | convolution fusion | flops 940900352 | bytes 17039360 | tf_op jit(solution)/shard_map/rbgf,fd->rbgd/dot_general | solution.py:72
  331.4 43.8 %all-reduce.8 = (bf16[16,1,4,2048]{3,0,2,1:T(8,128)(2,1)S(1)}, bf16[16,1,4,2048]{3,0,2,1:T(8,128)(2,1)S(1)}) all-reduce(f32[16,1,4,2048]{3,0,2,1:T(8,128)S(1)} %fusion.13, f32[16,1,4,2048]{3,0,2,1:T(8,128)S(1)} %fusion.10), channel_id=5, replica_groups=mesh['parts'=2,'ffn'=4,'pair'=2,'rep'=2] {'ffn'}, use_global_device_ids=true, to_apply=%region_9.10.clone | all-reduce | flops 262144 | bytes 1572864
  375.9 3.3 all-to-all-start.1
  379.9 3.4 all-to-all-done.1
  383.3 3.3 all-to-all-start.3
  387.3 3.4 all-to-all-done.3
  (50 shorter events, 28.4 us)
Async XLA Ops:
  7.2 17.8 %copy-start.1 = (f32[2,1,4,8192]{3,2,1,0:T(4,128)S(1)}, f32[2,1,4,8192]{3,2,1,0:T(4,128)}, u32[]{:S(2)}) copy-start(f32[2,1,4,8192]{3,2,1,0:T(4,128)} %param.10) | copy-start | bytes 786436
  84.2 60.8 %all-to-all-start = ((bf16[4,2,4096]{2,1,0:T(2,128)(2,1)}), bf16[4,2,4096]{2,1,0:T(2,128)(2,1)S(1)}, u32[]{:S(2)}, u32[]{:S(2)}) async-start(bf16[4,2,4096]{2,1,0:T(2,128)(2,1)} %reshape.418), calls=%async_computation | async-start | bytes 131072 | tf_op jit(solution)/shard_map/all_to_all | solution.py:55
  145.0 32.6 %all-to-all-start.2 = ((bf16[4,2,4096]{2,1,0:T(2,128)(2,1)}), bf16[4,2,4096]{2,1,0:T(2,128)(2,1)S(1)}, u32[]{:S(2)}, u32[]{:S(2)}) async-start(bf16[4,2,4096]{2,1,0:T(2,128)(2,1)} %reshape.416), calls=%async_computation.2 | async-start | bytes 131072 | tf_op jit(solution)/shard_map/all_to_all | solution.py:55
  148.5 162.0 %all-reduce.7.cloned.1.call-start = ((), (), s32[]{:S(2)}) async-start(), calls=%async_computation.4 | async-start | bytes 7340032 | tf_op jit(solution)/shard_map/psum | solution.py:64
  219.1 12.7 %copy-start.3 = (u32[32]{0:T(128)S(1)}, u32[32]{0:T(128)}, u32[]{:S(2)}) copy-start(u32[32]{0:T(128)} %constant.33) | copy-start | bytes 388
  310.6 12.0 %copy-start = (f32[1,4,16,7168]{3,2,1,0:T(8,128)S(1)}, f32[1,4,16,7168]{3,2,1,0:T(8,128)}, u32[]{:S(2)}) copy-start(f32[1,4,16,7168]{3,2,1,0:T(8,128)} %get-tuple-element.8) | copy-start | bytes 5505028
  314.1 16.3 %copy-start.2 = (s32[2,4]{1,0:T(2,128)S(1)}, s32[2,4]{1,0:T(2,128)}, u32[]{:S(2)}) copy-start(s32[2,4]{1,0:T(2,128)} %param.15) | copy-start | bytes 100
  375.9 7.4 %all-to-all-start.1 = ((bf16[4,1,4,2048]{3,0,1,2:T(4,128)(2,1)}), bf16[4,1,4,2048]{3,0,1,2:T(4,128)(2,1)S(1)}, u32[]{:S(2)}, u32[]{:S(2)}) async-start(bf16[4,1,4,2048]{3,0,1,2:T(4,128)(2,1)} %fusion.42), calls=%async_computation.1 | async-start | bytes 131072 | tf_op jit(solution)/shard_map/all_to_all | solution.py:78
  383.3 7.4 %all-to-all-start.3 = ((bf16[4,1,4,2048]{3,0,1,2:T(4,128)(2,1)}), bf16[4,1,4,2048]{3,0,1,2:T(4,128)(2,1)S(1)}, u32[]{:S(2)}, u32[]{:S(2)}) async-start(bf16[4,1,4,2048]{3,0,1,2:T(4,128)(2,1)} %fusion.43), calls=%async_computation.3 | async-start | bytes 131072 | tf_op jit(solution)/shard_map/all_to_all | solution.py:78
Sparse Core Ops, SparseCore 0:
  231.9 78.5 all-reduce.6
where the time goes:
time: 400 us; the launch traced here: 398 us
  other arithmetic  98.5 us (25%)
  waiting for transfers between devices  84.3 us (21%)
  blocking collectives  73.3 us (18%)
  local copies, waits for them, and re-layouts  66.8 us (17%)
  matrix products  46.3 us (12%)
  between operations  14.9 us (4%)
  starting transfers between devices  14.3 us (4%)
    unnamed x2, other arithmetic  90.4 us
    psum x1, waiting for transfers between devices, layer_step(): summed = lax.psum(partial_value, ('pair', 'rep'))  77.5 us
    unnamed x1, blocking collectives  43.8 us
    all_gather x2, blocking collectives, layer_step(): lax.all_gather(routed, 'ffn', axis=2, tiled=True)  29.4 us
    unnamed x19, local copies, waits for them, and re-layouts  27.5 us
    dot_general x2, matrix products, layer_step(): jnp.einsum('bgrd,df->bgrf', lax.all_gather(routed, 'ffn', axis=2, tiled=T...  25.4 us
    all_to_all x4, local copies, waits for them, and re-layouts, layer_step(): lax.all_to_all(normed[:, None], ('pair', 'rep'), split_axis=3, concat_axi...  16.3 us
    dot_general x2, matrix products, layer_step(): jnp.einsum('rbgf,fd->rbgd', rows_first, down_weight, preferred_element_ty...  16.3 us
  transfers between devices with their start and end apart: 5, of which 3 were waited for; matrix products, arithmetic and copies ran while one was open for 18% of the time, Pallas kernels for 0%

commit v1 on v0

v1 whole, which is shorter than its diff:
```python
import functools
import math

import jax
import jax.numpy as jnp
from jax import lax
from jax.experimental import pallas as pl
from jax.experimental.pallas import tpu as pltpu
from jax.sharding import PartitionSpec as P

HD = 128
F32 = jnp.float32
BF16 = jnp.bfloat16
SMEM = pltpu.MemorySpace.SMEM
VMEM = pltpu.MemorySpace.VMEM


def attend_kernel(
    cols, kvh, heads_per_step, len_ref, query_ref, key_ref, value_ref, residual_ref, gain_ref, *refs
):
    pairs, reps = cols
    stream_ref = refs[0]
    piece_refs = refs[1 : 1 + pairs * reps]
    bias_ref, = refs[1 + pairs * reps :]
    step = pl.program_id(0)
    batches, rows, wide = query_ref.shape
    seqs = batches * rows
    cache = key_ref.shape[0] // seqs
    group = wide // (heads_per_step * HD)
    scale = 1.0 / math.sqrt(HD)

    @pl.when(step == 0)
    def _():
        shape = (group * seqs, seqs * cache)
        row = lax.rem(lax.broadcasted_iota(jnp.int32, shape, 0), seqs)
        place = lax.broadcasted_iota(jnp.int32, shape, 1) - row * cache
        limit = jnp.zeros(shape, jnp.int32)
        for seq in range(seqs):
            limit = jnp.where(row == seq, len_ref[seq // rows, seq % rows], limit)
        bias_ref[...] = jnp.where((place >= 0) & (place < limit), 0.0, -1e30)

    queries = jnp.concatenate([query_ref[b].astype(F32) for b in range(batches)], axis=0)
    residual = jnp.concatenate([residual_ref[b] for b in range(batches)], axis=0)
    mixed = []
    for k in range(heads_per_step):
        stacked = jnp.concatenate(
            [queries[:, (k * group + h) * HD : (k * group + h + 1) * HD] for h in range(group)],
            axis=0,
        ).astype(BF16)
        scores = lax.dot_general(
            stacked,
            key_ref[:, k * HD : (k + 1) * HD],
            (((1,), (1,)), ((), ())),
            preferred_element_type=F32,
        )
        scores = scores * scale + bias_ref[...]
        peak = jnp.max(scores, axis=-1, keepdims=True)
        raised = jnp.exp(scores - peak)
        probs = (raised / jnp.sum(raised, axis=-1, keepdims=True)).astype(BF16)
        out = jnp.dot(probs, value_ref[:, k * HD : (k + 1) * HD], preferred_element_type=F32)
        out = out.astype(BF16).astype(F32)
        mixed += [out[h * seqs : (h + 1) * seqs] for h in range(group)]
    start = pl.multiple_of(step * wide, wide)
    stream_ref[:, pl.ds(start, wide)] = residual + jnp.concatenate(mixed, axis=1)

    @pl.when(step == kvh // heads_per_step - 1)
    def _():
        stream = stream_ref[...]
        width = stream.shape[1] // (pairs * reps)
        factor = lax.rsqrt(jnp.mean(stream * stream, axis=-1, keepdims=True) + 1e-05)
        pair = lax.axis_index("pair")
        rep = lax.axis_index("rep")
        for index, piece_ref in enumerate(piece_refs):
            dr, dp = divmod(index, pairs)
            column = lax.rem(pair + dp, pairs) * reps + lax.rem(rep + dr, reps)
            own = pl.ds(pl.multiple_of(column * width, width), width)
            piece_ref[...] = (stream_ref[:, own] * factor * gain_ref[:, own]).astype(BF16)


def attend(cols, cache_len, query, key_cache, value_cache, residual, norm_gain):
    batches, _, rows, depth = query.shape
    seqs = batches * rows
    cache, kv = key_cache.shape[3:]
    kvh = kv // HD
    heads_per_step = 2
    wide = depth // kvh * heads_per_step
    columns = cols[0] * cols[1]
    by_head = pl.BlockSpec((batches, rows, wide), lambda i: (0, 0, i))
    cached = pl.BlockSpec((seqs * cache, heads_per_step * HD), lambda i: (0, i))
    return pl.pallas_call(
        functools.partial(attend_kernel, cols, kvh, heads_per_step),
        grid=(kvh // heads_per_step,),
        out_shape=[jax.ShapeDtypeStruct((seqs, depth), F32)]
        + [jax.ShapeDtypeStruct((seqs, depth // columns), BF16)] * columns,
        in_specs=[
            pl.BlockSpec(memory_space=SMEM),
            by_head,
            cached,
            cached,
            by_head,
            pl.BlockSpec((1, depth), lambda i: (0, 0)),
        ],
        out_specs=[pl.BlockSpec((seqs, depth), lambda i: (0, 0))]
        + [pl.BlockSpec((seqs, depth // columns), lambda i: (0, 0))] * columns,
        scratch_shapes=[pltpu.VMEM((depth // kvh // HD * seqs, seqs * cache), F32)],
        compiler_params=pltpu.CompilerParams(vmem_limit_bytes=16 * 1024 * 1024),
        cost_estimate=pl.CostEstimate(flops=10**9, bytes_accessed=10**7, transcendentals=10**6),
        name="attend",
    )(
        cache_len.reshape(batches, rows),
        query.reshape(batches, rows, depth),
        key_cache.reshape(seqs * cache, kv),
        value_cache.reshape(seqs * cache, kv),
        residual.reshape(batches, rows, depth),
        norm_gain.reshape(1, depth),
    )


def owner_of(table_ref, micro, column, columns):
    found = jnp.int32(0)
    for group in range(columns):
        found = found + jnp.where(table_ref[micro, group] == column, group, 0)
    return found


def gate_up_kernel(cols, batches, ffn, table_ref, *refs):
    pairs, reps = cols
    columns = pairs * reps
    pieces = refs[:ffn]
    gate_ref, up_ref, keep_ref, send_ref, rows_ref = refs[ffn:]
    seqs = pieces[0].shape[1]
    rows = seqs // batches
    half = rows_ref.shape[0] // reps

    @pl.when(pl.program_id(0) == 0)
    def _():
        pair = lax.axis_index("pair")
        rep = lax.axis_index("rep")
        first = lax.broadcasted_iota(jnp.int32, pieces[0].shape[1:], 0) < rows
        for index in range(columns):
            dr, dp = divmod(index, pairs)
            column = lax.rem(pair + dp, pairs) * reps + lax.rem(rep + dr, reps)
            for micro in range(batches):
                group = owner_of(table_ref, micro, column, columns)
                from_pair = lax.rem(pair - group // reps + pairs, pairs)
                from_rep = lax.rem(rep - lax.rem(group, reps) + reps, reps)
                slot = from_rep * pairs + from_pair
                for shift in range(0, ffn, 2):
                    a = pieces[shift][slot].astype(F32)
                    b = pieces[shift + 1][slot].astype(F32)
                    if micro == 0:
                        b = pltpu.roll(b, rows, 0)
                    else:
                        a = pltpu.roll(a, rows, 0)
                    base = ((index * batches + micro) * ffn + shift) * rows
                    rows_ref[base : base + 2 * rows, :] = jnp.where(first, a, b).astype(BF16)

    for place, weight_ref in enumerate((gate_ref, up_ref)):
        sums = jnp.dot(rows_ref[...], weight_ref[...], preferred_element_type=F32)
        keep_ref[place] = sums[:half]
        send_ref[place] = sums[half:].astype(BF16)


def gate_up(cols, batches, table, pieces, gate_weight, up_weight, chunk, chunks):
    ffn = len(pieces)
    columns, seqs, depth = pieces[0].shape
    width = gate_weight.shape[1] // chunks
    tile = math.gcd(width, 256)
    steps = width // tile
    total = columns * seqs * ffn
    half = total // cols[1]
    weight = pl.BlockSpec((depth, tile), lambda i: (0, chunk * steps + i))
    whole = pl.BlockSpec((columns, seqs, depth), lambda i: (0, 0, 0))
    out = pl.BlockSpec((2, half, tile), lambda i: (0, 0, i))
    return pl.pallas_call(
        functools.partial(gate_up_kernel, cols, batches, ffn),
        grid=(steps,),
        out_shape=[
            jax.ShapeDtypeStruct((2, half, width), F32),
            jax.ShapeDtypeStruct((2, total - half, width), BF16),
        ],
        in_specs=[pl.BlockSpec(memory_space=SMEM)] + [whole] * ffn + [weight, weight],
        out_specs=[out, pl.BlockSpec((2, total - half, tile), lambda i: (0, 0, i))],
        scratch_shapes=[pltpu.VMEM((total, depth), BF16)],
        compiler_params=pltpu.CompilerParams(vmem_limit_bytes=32 * 1024 * 1024),
        cost_estimate=pl.CostEstimate(
            flops=4 * total * depth * width, bytes_accessed=4 * depth * width, transcendentals=0
        ),
        name=f"gate_up_{chunk}",
    )(table, *pieces, gate_weight, up_weight)


def join_kernel(pairs, keep_ref, came_ref, own_ref, *send_refs):
    rows = own_ref.shape[1]
    own_ref[...] = keep_ref[:, :rows] + came_ref[:, :rows].astype(F32)
    for dp in range(1, pairs):
        part = slice(dp * rows, (dp + 1) * rows)
        send_refs[dp - 1][...] = (keep_ref[:, part] + came_ref[:, part].astype(F32)).astype(BF16)


def join(pairs, keep, came):
    two, total, width = keep.shape
    rows = total // pairs
    tile = math.gcd(width, 896)

    def block(count):
        return pl.BlockSpec((two, count, tile), lambda i: (0, 0, i))

    return pl.pallas_call(
        functools.partial(join_kernel, pairs),
        grid=(width // tile,),
        out_shape=[jax.ShapeDtypeStruct((two, rows, width), F32)]
        + [jax.ShapeDtypeStruct((two, rows, width), BF16)] * (pairs - 1),
        in_specs=[block(total)] * 2,
        out_specs=[block(rows)] * pairs,
        compiler_params=pltpu.CompilerParams(vmem_limit_bytes=16 * 1024 * 1024),
        cost_estimate=pl.CostEstimate(flops=keep.size, bytes_accessed=6 * keep.size, transcendentals=0),
        name="join",
    )(keep, came)


def act_kernel(own_ref, *refs):
    sums = own_ref[...]
    for ref in refs[:-1]:
        sums = sums + ref[...].astype(F32)
    gate = sums[0]
    refs[-1][...] = (gate / (1.0 + jnp.exp(-gate)) * sums[1]).astype(BF16)


def activate(own, arrived):
    two, rows, width = own.shape
    tile = math.gcd(width, 896)
    block = pl.BlockSpec((two, rows, tile), lambda i: (0, 0, i))
    return pl.pallas_call(
        act_kernel,
        grid=(width // tile,),
        out_shape=jax.ShapeDtypeStruct((rows, width), BF16),
        in_specs=[block] * (1 + len(arrived)),
        out_specs=pl.BlockSpec((rows, tile), lambda i: (0, i)),
        compiler_params=pltpu.CompilerParams(vmem_limit_bytes=16 * 1024 * 1024),
        cost_estimate=pl.CostEstimate(flops=own.size, bytes_accessed=6 * own.size, transcendentals=own.size),
        name="activate",
    )(own, *arrived)


def served_kernel(batches, rows, *refs):
    out_ref = refs[-1]
    turn = lax.axis_index("ffn") * rows
    start = 0
    for ref in refs[:-1]:
        held = ref[...].astype(F32)
        each = held.shape[0] // batches
        for micro in range(batches):
            part = pltpu.roll(held[micro * each : (micro + 1) * each], turn, 0)
            out_ref[micro, 0, :, start : start + held.shape[1]] = part.astype(BF16)
        start += held.shape[1]


def serve(batches, rows, hidden):
    total = hidden[0].shape[0]
    width = sum(h.shape[1] for h in hidden)
    return pl.pallas_call(
        functools.partial(served_kernel, batches, rows),
        out_shape=jax.ShapeDtypeStruct((batches, 1, total // batches, width), BF16),
        in_specs=[pl.BlockSpec(memory_space=VMEM)] * len(hidden),
        out_specs=pl.BlockSpec(memory_space=VMEM),
        compiler_params=pltpu.CompilerParams(vmem_limit_bytes=16 * 1024 * 1024),
        name="serve",
    )(*hidden)


def down_kernel(count, has_sum, hidden_count, *refs):
    hidden_refs = refs[:hidden_count]
    weight_ref = refs[hidden_count]
    out_ref = refs[-2]
    rows_ref = refs[-1]

    @pl.when(pl.program_id(0) == 0)
    def _():
        rows_ref[...] = jnp.concatenate([ref[...] for ref in hidden_refs], axis=0)

    sums = jnp.dot(rows_ref[...], weight_ref[...], preferred_element_type=F32)
    if has_sum:
        sums = sums + refs[hidden_count + 1][...]
    out_ref[...] = sums


def down(hidden, weight, chunk, chunks, before):
    width = weight.shape[0] // chunks
    depth = weight.shape[1]
    tile = math.gcd(depth, 256)
    total = sum(h.shape[0] for h in hidden)
    part = pl.BlockSpec((total, tile), lambda i: (0, i))
    return pl.pallas_call(
        functools.partial(down_kernel, chunks, before is not None, len(hidden)),
        grid=(depth // tile,),
        out_shape=jax.ShapeDtypeStruct((total, depth), F32),
        in_specs=[pl.BlockSpec(h.shape, lambda i: (0, 0)) for h in hidden]
        + [pl.BlockSpec((width, tile), lambda i: (chunk, i))]
        + [part] * (before is not None),
        out_specs=part,
        scratch_shapes=[pltpu.VMEM((total, width), BF16)],
        compiler_params=pltpu.CompilerParams(vmem_limit_bytes=32 * 1024 * 1024),
        cost_estimate=pl.CostEstimate(
            flops=2 * total * depth * width, bytes_accessed=2 * depth * width, transcendentals=0
        ),
        name=f"down_{chunk}",
    )(*hidden, weight, *([before] * (before is not None)))


def arrange_kernel(cols, batches, ffn, rows, table_ref, sums_ref, *out_refs):
    pairs, reps = cols
    columns = pairs * reps
    pair = lax.axis_index("pair")
    rep = lax.axis_index("rep")
    seqs = batches * rows
    first = lax.broadcasted_iota(jnp.int32, (seqs, sums_ref.shape[1]), 0) < rows
    for index in range(columns):
        dr, dp = divmod(index, pairs)
        group = lax.rem(pair + dp, pairs) * reps + lax.rem(rep + dr, reps)
        bases = []
        for micro in range(batches):
            column = table_ref[micro, group]
            to_pair = lax.rem(column // reps - pair + pairs, pairs)
            to_rep = lax.rem(lax.rem(column, reps) - rep + reps, reps)
            bases.append(((to_rep * pairs + to_pair) * batches + micro) * ffn * rows)
        for shift in range(ffn):
            low = shift // 2 * 2 * rows
            a, b = (
                sums_ref[pl.ds(pl.multiple_of(base + low, 2 * rows), 2 * rows), :] for base in bases
            )
            if shift % 2 == 0:
                b = pltpu.roll(b, rows, 0)
            else:
                a = pltpu.roll(a, rows, 0)
            out_refs[shift][index] = jnp.where(first, a, b).astype(BF16)


def arrange(cols, batches, ffn, rows, table, sums):
    columns = cols[0] * cols[1]
    depth = sums.shape[1]
    return pl.pallas_call(
        functools.partial(arrange_kernel, cols, batches, ffn, rows),
        out_shape=[jax.ShapeDtypeStruct((columns, batches * rows, depth), BF16)] * ffn,
        in_specs=[pl.BlockSpec(memory_space=SMEM), pl.BlockSpec(memory_space=VMEM)],
        out_specs=[pl.BlockSpec(memory_space=VMEM)] * ffn,
        compiler_params=pltpu.CompilerParams(vmem_limit_bytes=16 * 1024 * 1024),
        name="arrange",
    )(table, sums)


def total_kernel(*refs):
    count = len(refs) // 2
    ins = [r for r in refs if r.ndim == 3]
    outs = [r for r in refs if r.ndim == 2]
    for index, out_ref in enumerate(outs):
        sums = ins[0][index].astype(F32)
        for ref in ins[1:]:
            sums = sums + ref[index].astype(F32)
        out_ref[...] = sums.astype(BF16)


def total(parts):
    columns, seqs, depth = parts[0].shape
    return pl.pallas_call(
        total_kernel,
        out_shape=[jax.ShapeDtypeStruct((seqs, depth), BF16)] * columns,
        in_specs=[pl.BlockSpec(memory_space=VMEM)] * len(parts),
        out_specs=[pl.BlockSpec(memory_space=VMEM)] * columns,
        compiler_params=pltpu.CompilerParams(vmem_limit_bytes=16 * 1024 * 1024),
        name="total",
    )(*parts)


def finish_kernel(cols, stream_ref, *refs):
    pairs, reps = cols
    pair = lax.axis_index("pair")
    rep = lax.axis_index("rep")
    out_ref = refs[-1]
    batches, _, rows, _ = out_ref.shape
    width = refs[0].shape[1]
    for index, ref in enumerate(refs[:-1]):
        dr, dp = divmod(index, pairs)
        column = lax.rem(pair - dp + pairs, pairs) * reps + lax.rem(rep - dr + reps, reps)
        own = pl.ds(pl.multiple_of(column * width, width), width)
        sums = stream_ref[:, own] + ref[...].astype(F32)
        for micro in range(batches):
            out_ref[micro, 0, :, own] = sums[micro * rows : (micro + 1) * rows]


def finish(cols, batches, stream, changes):
    seqs, depth = stream.shape
    return pl.pallas_call(
        functools.partial(finish_kernel, cols),
        out_shape=jax.ShapeDtypeStruct((batches, 1, seqs // batches, depth), F32),
        in_specs=[pl.BlockSpec(memory_space=VMEM)] * (1 + len(changes)),
        out_specs=pl.BlockSpec(memory_space=VMEM),
        compiler_params=pltpu.CompilerParams(vmem_limit_bytes=16 * 1024 * 1024),
        name="finish",
    )(stream, *changes)


def to_column(cols, value, dr, dp):
    pairs, reps = cols
    route = [
        (p * reps + r, (p + dp) % pairs * reps + (r + dr) % reps)
        for p in range(pairs)
        for r in range(reps)
    ]
    return lax.ppermute(value, ("pair", "rep"), route)


def exchange(cols, values):
    return [values[0]] + [
        to_column(cols, value, *divmod(index, cols[0]))
        for index, value in enumerate(values)
        if index > 0
    ]


def per_device(
    cols,
    ffn,
    residual,
    query,
    key_cache,
    value_cache,
    cache_len,
    partner_table,
    norm_gain,
    gate_weight,
    up_weight,
    down_weight,
):
    pairs, reps = cols
    batches, _, rows, _ = query.shape
    units = gate_weight.shape[1] // 128
    chunks = 2 if units % 2 == 0 else 1
    stream, *normed = attend(
        cols, cache_len, query, key_cache, value_cache, residual, norm_gain
    )
    mine = jnp.stack(exchange(cols, normed))
    pieces = [mine] + [
        lax.ppermute(mine, "ffn", [(i, (i - s) % ffn) for i in range(ffn)]) for s in range(1, ffn)
    ]
    hidden = []
    sums = None
    for chunk in range(chunks):
        keep, send = gate_up(
            cols, batches, partner_table, pieces, gate_weight, up_weight, chunk, chunks
        )
        came = to_column(cols, send, 1, 0)
        own, *others = join(pairs, keep, came)
        arrived = [to_column(cols, other, 0, dp + 1) for dp, other in enumerate(others)]
        hidden.append(activate(own, arrived))
    for chunk, part in enumerate(hidden):
        block = [part] + [to_column(cols, part, 0, pairs - dp) for dp in range(1, pairs)]
        block += [to_column(cols, item, 1, 0) for item in block]
        sums = down(block, down_weight, chunk, chunks, sums)
    served = serve(batches, rows, hidden)
    shares = arrange(cols, batches, ffn, rows, partner_table, sums)
    gathered = [shares[0]] + [
        lax.ppermute(shares[s], "ffn", [(i, (i + s) % ffn) for i in range(ffn)])
        for s in range(1, ffn)
    ]
    changes = exchange(cols, total(gathered))
    updated = finish(cols, batches, stream, changes)
    return (updated, served)


def solution(mesh):
    sizes = dict(mesh.shape)
    cols = (sizes["pair"], sizes["rep"])
    rows = P(None, ("parts", "pair", "rep"), "ffn", None)
    caches = P(None, ("parts", "pair", "rep"), "ffn", None, None)
    placed = (
        rows,
        rows,
        caches,
        caches,
        P(None, ("parts", "pair", "rep"), "ffn"),
        P("parts", None),
        P(),
        P(("pair", "rep"), "ffn"),
        P(("pair", "rep"), "ffn"),
        P("ffn", ("pair", "rep")),
    )
    return jax.shard_map(
        functools.partial(per_device, cols, sizes["ffn"]),
        mesh=mesh,
        in_specs=placed,
        out_specs=(rows, P(None, ("parts", "pair", "rep"), None, "ffn")),
        check_vma=False,
    )
```

time: 400 us -> 103 us (0.26)
  other arithmetic: 98.5 us -> 0.02 us
  blocking collectives: 73.3 us -> 0 us
  local copies, waits for them, and re-layouts: 66.8 us -> 12.3 us
  waiting for transfers between devices: 84.3 us -> 37.8 us
  matrix products: 46.3 us -> 0 us
  Pallas kernels: 0 us -> 32.9 us
  between operations: 14.9 us -> 0.84 us
  starting transfers between devices: 14.3 us -> 18.7 us
    unnamed x2 -> x1, other arithmetic: 90.4 us -> 0.01 us
    psum x1 -> x0, waiting for transfers between devices: 77.5 us -> none  [layer_step(): summed = lax.psum(partial_value, ('pair', 'rep'))]
    dot_general x10 -> x0, matrix products: 46.3 us -> none  [the longest x2 25.4 us: layer_step(): jnp.einsum('bgrd,df->bgrf', lax.all_gather(routed, 'ffn', axis=2, tiled=T...]
    unnamed x1 -> x0, blocking collectives: 43.8 us -> none
    ppermute x0 -> x22, waiting for transfers between devices: none -> 37.8 us  [the longest x16 19.9 us: to_column(): return lax.ppermute(value, ('pair', 'rep'), route)]
    pallas_call x0 -> x13, Pallas kernels: none -> 32.9 us  [the longest x2 17 us: gate_up(): pl.pallas_call(functools.partial(gate_up_kernel, cols, batches, ffn), gri...]
    all_gather x2 -> x0, blocking collectives: 29.4 us -> none  [layer_step(): lax.all_gather(routed, 'ffn', axis=2, tiled=True)]
    ppermute x0 -> x22, starting transfers between devices: none -> 18.7 us  [the longest x16 8.8 us: to_column(): return lax.ppermute(value, ('pair', 'rep'), route)]
  transfers between devices with their start and end apart: 5 -> 22, of which waited for: 3 -> 13; matrix products, arithmetic and copies ran while one was open for 18% -> 0% of each run, Pallas kernels for 0% -> 14%
where the time goes in v1:
time: 103 us
  waiting for transfers between devices  37.8 us (37%)
  Pallas kernels  32.9 us (32%)
  starting transfers between devices  18.7 us (18%)
  local copies, waits for them, and re-layouts  12.3 us (12%)
    ppermute x16, waiting for transfers between devices, to_column(): return lax.ppermute(value, ('pair', 'rep'), route)  19.9 us
    pallas_call x2, Pallas kernels, gate_up(): pl.pallas_call(functools.partial(gate_up_kernel, cols, batches, ffn), gri...  17 us
    unnamed x26, local copies, waits for them, and re-layouts  12.3 us
    ppermute x3, waiting for transfers between devices, per_device(): lax.ppermute(mine, 'ffn', [(i, (i - s) % ffn) for i in range(ffn)])  9.79 us
    ppermute x16, starting transfers between devices, to_column(): return lax.ppermute(value, ('pair', 'rep'), route)  8.8 us
    ppermute x3, waiting for transfers between devices, per_device(): lax.ppermute(shares[s], 'ffn', [(i, (i + s) % ffn) for i in range(ffn)])  8.06 us
    pallas_call x2, Pallas kernels, down(): pl.pallas_call(functools.partial(down_kernel, chunks, before is not None,...  7.33 us
    pallas_call x1, Pallas kernels, attend(): pl.pallas_call(functools.partial(attend_kernel, cols, kvh, heads_per_step...  5.29 us
  transfers between devices with their start and end apart: 22, of which 13 were waited for; matrix products, arithmetic and copies ran while one was open for 0% of the time, Pallas kernels for 14%

profile of v1, /device:TPU:0, one launch (start us, length us, event | category | flops | bytes accessed | tf_op | source)
XLA Modules:
  0.0 102.5 jit_solution(16321699280526743543)
XLA Ops:
  0.6 1.6 %copy-done.1 = bf16[2,1,4,128,1024]{4,3,2,1,0:T(8,128)(2,1)S(1)} copy-done((bf16[2,1,4,128,1024]{4,3,2,1,0:T(8,128)(2,1)S(1)}, bf16[2,1,4,128,1024]{4,3,2,1,0:T(8,128)(2,1)}, u32[]{:S(2)}) %copy-start.1) | copy-done | bytes 2097176
  2.2 1.6 %copy-done.2 = bf16[2,1,4,128,1024]{4,3,2,1,0:T(8,128)(2,1)S(1)} copy-done((bf16[2,1,4,128,1024]{4,3,2,1,0:T(8,128)(2,1)S(1)}, bf16[2,1,4,128,1024]{4,3,2,1,0:T(8,128)(2,1)}, u32[]{:S(2)}) %copy-start.2) | copy-done | bytes 2097176
  7.1 5.3 %attend.1 = (f32[8,8192]{1,0:T(8,128)S(1)}, bf16[8,2048]{1,0:T(8,128)(2,1)S(1)}, bf16[8,2048]{1,0:T(8,128)(2,1)S(1)}, bf16[8,2048]{1,0:T(8,128)(2,1)S(1)}, bf16[8,2048]{1,0:T(8,128)(2,1)S(1)}) custom-call(s32[2,4]{1,0:T(2,128)S(1)} %bitcast.18, bf16[2,4,8192]{2,1,0:T(4,128)(2,1)S(1)} %bitcast.15, bf16[1024,1024]{1,0:T(8,128)(2,1)S(1)} %bitcast.12, ...), custom_call_target="tpu_custom_call" | custom-call | flops 1000000000 | bytes 10000000 | tf_op jit(solution)/shard_map/attend/pallas_call | solution.py:90
  12.4 2.4 %collective-permute-start.2 = (bf16[8,2048]{1,0:T(8,128)(2,1)S(1)}, bf16[8,2048]{1,0:T(8,128)(2,1)S(1)}, u32[]{:S(2)}, u32[]{:S(2)}) collective-permute-start(bf16[8,2048]{1,0:T(8,128)(2,1)S(1)} %get-tuple-element.27), channel_id=1, source_target_pairs={{0,3},{1,2},{2,1},{3,0},{4,7},{5,6},{6,5},{7,4},{8,11},{9,10},{10,... | collective-permute-start | bytes 98312 | tf_op jit(solution)/shard_map/ppermute | solution.py:410
  15.6 1.1 %collective-permute-done.2 = bf16[8,2048]{1,0:T(8,128)(2,1)S(1)} collective-permute-done((bf16[8,2048]{1,0:T(8,128)(2,1)S(1)}, bf16[8,2048]{1,0:T(8,128)(2,1)S(1)}, u32[]{:S(2)}, u32[]{:S(2)}) %collective-permute-start.2) | collective-permute-done | bytes 32800 | tf_op jit(solution)/shard_map/ppermute | solution.py:410
  16.6 2.8 %collective-permute-done = bf16[8,2048]{1,0:T(8,128)(2,1)S(1)} collective-permute-done((bf16[8,2048]{1,0:T(8,128)(2,1)S(1)}, bf16[8,2048]{1,0:T(8,128)(2,1)S(1)}, u32[]{:S(2)}, u32[]{:S(2)}) %collective-permute-start) | collective-permute-done | bytes 32800 | tf_op jit(solution)/shard_map/ppermute | solution.py:410
  19.5 3.7 %collective-permute-start.3 = (bf16[4,8,2048]{2,1,0:T(8,128)(2,1)S(1)}, bf16[4,8,2048]{2,1,0:T(8,128)(2,1)S(1)}, u32[]{:S(2)}, u32[]{:S(2)}) collective-permute-start(bf16[4,8,2048]{2,1,0:T(8,128)(2,1)S(1)} %pad_maximum_fusion.refs_0_), channel_id=1, source_target_pairs={{0,12},{4,0},{8,4},{12,8},{1,13},{5,1},{9,5},{13,9},{2,14},{6,2},{... | collective-permute-start | bytes 393224 | tf_op jit(solution)/shard_map/ppermute | solution.py:444
  24.1 2.9 %collective-permute-done.3.refs_1_ = bf16[4,8,2048]{2,1,0:T(8,128)(2,1)S(1)} collective-permute-done((bf16[4,8,2048]{2,1,0:T(8,128)(2,1)S(1)}, bf16[4,8,2048]{2,1,0:T(8,128)(2,1)S(1)}, u32[]{:S(2)}, u32[]{:S(2)}) %collective-permute-start.3) | collective-permute-done | bytes 131104 | tf_op jit(solution)/shard_map/ppermute | solution.py:444
  27.1 6.8 %collective-permute-done.4.refs_2_ = bf16[4,8,2048]{2,1,0:T(8,128)(2,1)S(1)} collective-permute-done((bf16[4,8,2048]{2,1,0:T(8,128)(2,1)S(1)}, bf16[4,8,2048]{2,1,0:T(8,128)(2,1)S(1)}, u32[]{:S(2)}, u32[]{:S(2)}) %collective-permute-start.4) | collective-permute-done | bytes 131104 | tf_op jit(solution)/shard_map/ppermute | solution.py:444
  33.9 5.2 %copy-done = bf16[2048,3584]{1,0:T(8,128)(2,1)S(1)} copy-done((bf16[2048,3584]{1,0:T(8,128)(2,1)S(1)}, bf16[2048,3584]{1,0:T(8,128)(2,1)}, u32[]{:S(2)}) %copy-start) | copy-done | bytes 14680088
  39.8 8.0 %gate_up_0.1 = (f32[2,64,1792]{2,1,0:T(8,128)S(1)}, bf16[2,64,1792]{2,1,0:T(8,128)(2,1)}) custom-call(s32[2,4]{1,0:T(2,128)S(1)} %copy-done.6, bf16[4,8,2048]{2,1,0:T(8,128)(2,1)S(1)} %pad_maximum_fusion.refs_0_, bf16[4,8,2048]{2,1,0:T(8,128)(2,1)S(1)} %collective-permute-done.3.refs_1_, bf16[4,8,2048]{2,1,0:T(8,128)(2,1)S(1)} %collective-permute-done.4.refs_2_, ...), custom_call_target="tpu_custom_call" | custom-call | flops 1879048192 | bytes 14680064 | tf_op jit(solution)/shard_map/gate_up_0/pallas_call | solution.py:175
  47.9 9.0 %gate_up_1.1 = (f32[2,64,1792]{2,1,0:T(8,128)S(1)}, bf16[2,64,1792]{2,1,0:T(8,128)(2,1)S(1)}) custom-call(s32[2,4]{1,0:T(2,128)S(1)} %copy-done.6, bf16[4,8,2048]{2,1,0:T(8,128)(2,1)S(1)} %pad_maximum_fusion.refs_0_, bf16[4,8,2048]{2,1,0:T(8,128)(2,1)S(1)} %collective-permute-done.3.refs_1_, bf16[4,8,2048]{2,1,0:T(8,128)(2,1)S(1)} %collective-permute-done.4.refs_2_, ...), custom_call_target="tpu_custom_call" | custom-call | flops 1879048192 | bytes 14680064 | tf_op jit(solution)/shard_map/gate_up_1/pallas_call | solution.py:175
  59.9 6.0 %collective-permute-done.12.refs_0_ = bf16[2,32,1792]{2,1,0:T(8,128)(2,1)S(1)} collective-permute-done((bf16[2,32,1792]{2,1,0:T(8,128)(2,1)S(1)}, bf16[2,32,1792]{2,1,0:T(8,128)(2,1)S(1)}, u32[]{:S(2)}, u32[]{:S(2)}) %collective-permute-start.12) | collective-permute-done | bytes 229408 | tf_op jit(solution)/shard_map/ppermute | solution.py:410
  66.8 4.1 %collective-permute-done.7.refs_0_ = bf16[2,32,1792]{2,1,0:T(8,128)(2,1)S(1)} collective-permute-done((bf16[2,32,1792]{2,1,0:T(8,128)(2,1)S(1)}, bf16[2,32,1792]{2,1,0:T(8,128)(2,1)S(1)}, u32[]{:S(2)}, u32[]{:S(2)}) %collective-permute-start.7) | collective-permute-done | bytes 229408 | tf_op jit(solution)/shard_map/ppermute | solution.py:410
  71.7 1.0 collective-permute-done.13.refs_1_
  73.2 2.8 %collective-permute-done.8.refs_1_ = bf16[32,1792]{1,0:T(8,128)(2,1)S(1)} collective-permute-done((bf16[32,1792]{1,0:T(8,128)(2,1)S(1)}, bf16[32,1792]{1,0:T(8,128)(2,1)S(1)}, u32[]{:S(2)}, u32[]{:S(2)}) %collective-permute-start.8) | collective-permute-done | bytes 114720 | tf_op jit(solution)/shard_map/ppermute | solution.py:410
  76.1 3.6 %down_0.1.refs_5_ = f32[128,2048]{1,0:T(8,128)S(1)} custom-call(bf16[32,1792]{1,0:T(8,128)(2,1)S(1)} %activate.3.refs_0_, bf16[32,1792]{1,0:T(8,128)(2,1)S(1)} %collective-permute-done.13.refs_1_, bf16[32,1792]{1,0:T(8,128)(2,1)S(1)} %collective-permute-done.14.refs_2_, bf16[32,1792]{1,0:T(8,128)(2,1)S(1)} %collective-permute-done.15.refs_3_, ...), custom_call_target="tpu_custom_call" | custom-call | flops 939524096 | bytes 7340032 | tf_op jit(solution)/shard_map/down_0/pallas_call | solution.py:294
  79.7 3.7 %down_1.1.sums_ref = f32[128,2048]{1,0:T(8,128)S(1)} custom-call(bf16[32,1792]{1,0:T(8,128)(2,1)S(1)} %activate.2.refs_0_.refs_1_, bf16[32,1792]{1,0:T(8,128)(2,1)S(1)} %collective-permute-done.8.refs_1_, bf16[32,1792]{1,0:T(8,128)(2,1)S(1)} %collective-permute-done.9.refs_2_, bf16[32,1792]{1,0:T(8,128)(2,1)S(1)} %collective-permute-done.10.refs_3_, ...), custom_call_target="tpu_custom_call" | custom-call | flops 939524096 | bytes 7340032 | tf_op jit(solution)/shard_map/down_1/pallas_call | solution.py:294
  84.5 2.0 %collective-permute-start.17 = (bf16[4,8,2048]{2,1,0:T(8,128)(2,1)S(1)}, bf16[4,8,2048]{2,1,0:T(8,128)(2,1)S(1)}, u32[]{:S(2)}, u32[]{:S(2)}) collective-permute-start(bf16[4,8,2048]{2,1,0:T(8,128)(2,1)S(1)} %get-tuple-element.38), channel_id=1, source_target_pairs={{0,8},{4,12},{8,0},{12,4},{1,9},{5,13},{9,1},{13,5},{2,10},{6,14},... | collective-permute-start | bytes 393224 | tf_op jit(solution)/shard_map/ppermute | solution.py:463
  86.5 2.8 %collective-permute-start.18 = (bf16[4,8,2048]{2,1,0:T(8,128)(2,1)S(1)}, bf16[4,8,2048]{2,1,0:T(8,128)(2,1)S(1)}, u32[]{:S(2)}, u32[]{:S(2)}) collective-permute-start(bf16[4,8,2048]{2,1,0:T(8,128)(2,1)S(1)} %get-tuple-element.39), channel_id=1, source_target_pairs={{0,12},{4,0},{8,4},{12,8},{1,13},{5,1},{9,5},{13,9},{2,14},{6,2},{... | collective-permute-start | bytes 393224 | tf_op jit(solution)/shard_map/ppermute | solution.py:463
  89.3 3.1 %collective-permute-done.16.refs_1_ = bf16[4,8,2048]{2,1,0:T(8,128)(2,1)S(1)} collective-permute-done((bf16[4,8,2048]{2,1,0:T(8,128)(2,1)S(1)}, bf16[4,8,2048]{2,1,0:T(8,128)(2,1)S(1)}, u32[]{:S(2)}, u32[]{:S(2)}) %collective-permute-start.16) | collective-permute-done | bytes 131104 | tf_op jit(solution)/shard_map/ppermute | solution.py:463
  92.4 4.9 %collective-permute-done.17.refs_2_ = bf16[4,8,2048]{2,1,0:T(8,128)(2,1)S(1)} collective-permute-done((bf16[4,8,2048]{2,1,0:T(8,128)(2,1)S(1)}, bf16[4,8,2048]{2,1,0:T(8,128)(2,1)S(1)}, u32[]{:S(2)}, u32[]{:S(2)}) %collective-permute-start.17) | collective-permute-done | bytes 131104 | tf_op jit(solution)/shard_map/ppermute | solution.py:463
  98.2 1.4 %collective-permute-start.21 = (bf16[8,2048]{1,0:T(8,128)(2,1)S(1)}, bf16[8,2048]{1,0:T(8,128)(2,1)S(1)}, u32[]{:S(2)}, u32[]{:S(2)}) collective-permute-start(bf16[8,2048]{1,0:T(8,128)(2,1)S(1)} %get-tuple-element.43), channel_id=1, source_target_pairs={{0,3},{1,2},{2,1},{3,0},{4,7},{5,6},{6,5},{7,4},{8,11},{9,10},{10,... | collective-permute-start | bytes 98312 | tf_op jit(solution)/shard_map/ppermute | solution.py:410
  100.4 1.2 %collective-permute-done.19.refs_1_ = bf16[8,2048]{1,0:T(8,128)(2,1)S(1)} collective-permute-done((bf16[8,2048]{1,0:T(8,128)(2,1)S(1)}, bf16[8,2048]{1,0:T(8,128)(2,1)S(1)}, u32[]{:S(2)}, u32[]{:S(2)}) %collective-permute-start.19) | collective-permute-done | bytes 32800 | tf_op jit(solution)/shard_map/ppermute | solution.py:410
  (61 shorter events, 14.5 us)
Async XLA Ops:
  12.4 4.2 %collective-permute-start.2 = (bf16[8,2048]{1,0:T(8,128)(2,1)S(1)}, bf16[8,2048]{1,0:T(8,128)(2,1)S(1)}, u32[]{:S(2)}, u32[]{:S(2)}) collective-permute-start(bf16[8,2048]{1,0:T(8,128)(2,1)S(1)} %get-tuple-element.27), channel_id=1, source_target_pairs={{0,3},{1,2},{2,1},{3,0},{4,7},{5,6},{6,5},{7,4},{8,11},{9,10},{10,... | collective-permute-start | bytes 98312 | tf_op jit(solution)/shard_map/ppermute | solution.py:410
  14.8 1.8 %collective-permute-start.1 = (bf16[8,2048]{1,0:T(8,128)(2,1)S(1)}, bf16[8,2048]{1,0:T(8,128)(2,1)S(1)}, u32[]{:S(2)}, u32[]{:S(2)}) collective-permute-start(bf16[8,2048]{1,0:T(8,128)(2,1)S(1)} %get-tuple-element.26), channel_id=1, source_target_pairs={{0,1},{1,0},{2,3},{3,2},{4,5},{5,4},{6,7},{7,6},{8,9},{9,8},{10,11... | collective-permute-start | bytes 98312 | tf_op jit(solution)/shard_map/ppermute | solution.py:410
  15.5 3.9 %collective-permute-start = (bf16[8,2048]{1,0:T(8,128)(2,1)S(1)}, bf16[8,2048]{1,0:T(8,128)(2,1)S(1)}, u32[]{:S(2)}, u32[]{:S(2)}) collective-permute-start(bf16[8,2048]{1,0:T(8,128)(2,1)S(1)} %get-tuple-element.25), channel_id=1, source_target_pairs={{0,2},{1,3},{2,0},{3,1},{4,6},{5,7},{6,4},{7,5},{8,10},{9,11},{10,... | collective-permute-start | bytes 98312 | tf_op jit(solution)/shard_map/ppermute | solution.py:410
  19.5 7.6 %collective-permute-start.3 = (bf16[4,8,2048]{2,1,0:T(8,128)(2,1)S(1)}, bf16[4,8,2048]{2,1,0:T(8,128)(2,1)S(1)}, u32[]{:S(2)}, u32[]{:S(2)}) collective-permute-start(bf16[4,8,2048]{2,1,0:T(8,128)(2,1)S(1)} %pad_maximum_fusion.refs_0_), channel_id=1, source_target_pairs={{0,12},{4,0},{8,4},{12,8},{1,13},{5,1},{9,5},{13,9},{2,14},{6,2},{... | collective-permute-start | bytes 393224 | tf_op jit(solution)/shard_map/ppermute | solution.py:444
  23.1 10.8 %collective-permute-start.4 = (bf16[4,8,2048]{2,1,0:T(8,128)(2,1)S(1)}, bf16[4,8,2048]{2,1,0:T(8,128)(2,1)S(1)}, u32[]{:S(2)}, u32[]{:S(2)}) collective-permute-start(bf16[4,8,2048]{2,1,0:T(8,128)(2,1)S(1)} %pad_maximum_fusion.refs_0_), channel_id=1, source_target_pairs={{0,8},{4,12},{8,0},{12,4},{1,9},{5,13},{9,1},{13,5},{2,10},{6,14},... | collective-permute-start | bytes 393224 | tf_op jit(solution)/shard_map/ppermute | solution.py:444
  23.1 10.8 %collective-permute-start.5 = (bf16[4,8,2048]{2,1,0:T(8,128)(2,1)S(1)}, bf16[4,8,2048]{2,1,0:T(8,128)(2,1)S(1)}, u32[]{:S(2)}, u32[]{:S(2)}) collective-permute-start(bf16[4,8,2048]{2,1,0:T(8,128)(2,1)S(1)} %pad_maximum_fusion.refs_0_), channel_id=1, source_target_pairs={{0,4},{4,8},{8,12},{12,0},{1,5},{5,9},{9,13},{13,1},{2,6},{6,10},{... | collective-permute-start | bytes 393224 | tf_op jit(solution)/shard_map/ppermute | solution.py:444
  47.8 28.3 %slice-start.2 = ((s8[14680064]{0:T(1024)(128)(4,1)}), s8[4194304]{0:T(1024)(128)(4,1)S(1)}, s32[]{:S(2)}) async-start(s8[14680064]{0:T(1024)(128)(4,1)} %bitcast.10), calls=%async_computation.2 | async-start | bytes 8388608
  47.8 28.3 %slice-start.3 = ((s8[14680064]{0:T(1024)(128)(4,1)}), s8[2097152]{0:T(1024)(128)(4,1)S(1)}, s32[]{:S(2)}) async-start(s8[14680064]{0:T(1024)(128)(4,1)} %bitcast.10), calls=%async_computation.3 | async-start | bytes 4194304
  47.8 9.4 %collective-permute-start.11 = (bf16[2,64,1792]{2,1,0:T(8,128)(2,1)}, bf16[2,64,1792]{2,1,0:T(8,128)(2,1)S(1)}, u32[]{:S(2)}, u32[]{:S(2)}) collective-permute-start(bf16[2,64,1792]{2,1,0:T(8,128)(2,1)} %get-tuple-element.33), channel_id=1, source_target_pairs={{0,1},{1,0},{2,3},{3,2},{4,5},{5,4},{6,7},{7,6},{8,9},{9,8},{10,11... | collective-permute-start | bytes 1376264 | tf_op jit(solution)/shard_map/ppermute | solution.py:410
  56.9 1.9 %collective-permute-start.6 = (bf16[2,64,1792]{2,1,0:T(8,128)(2,1)S(1)}, bf16[2,64,1792]{2,1,0:T(8,128)(2,1)S(1)}, u32[]{:S(2)}, u32[]{:S(2)}) collective-permute-start(bf16[2,64,1792]{2,1,0:T(8,128)(2,1)S(1)} %get-tuple-element.29), channel_id=1, source_target_pairs={{0,1},{1,0},{2,3},{3,2},{4,5},{5,4},{6,7},{7,6},{8,9},{9,8},{10,11... | collective-permute-start | bytes 1376264 | tf_op jit(solution)/shard_map/ppermute | solution.py:410
  57.5 8.5 %collective-permute-start.12 = (bf16[2,32,1792]{2,1,0:T(8,128)(2,1)S(1)}, bf16[2,32,1792]{2,1,0:T(8,128)(2,1)S(1)}, u32[]{:S(2)}, u32[]{:S(2)}) collective-permute-start(bf16[2,32,1792]{2,1,0:T(8,128)(2,1)S(1)} %get-tuple-element.35), channel_id=1, source_target_pairs={{0,2},{1,3},{2,0},{3,1},{4,6},{5,7},{6,4},{7,5},{8,10},{9,11},{10,... | collective-permute-start | bytes 688136 | tf_op jit(solution)/shard_map/ppermute | solution.py:410
  59.1 11.8 %collective-permute-start.7 = (bf16[2,32,1792]{2,1,0:T(8,128)(2,1)S(1)}, bf16[2,32,1792]{2,1,0:T(8,128)(2,1)S(1)}, u32[]{:S(2)}, u32[]{:S(2)}) collective-permute-start(bf16[2,32,1792]{2,1,0:T(8,128)(2,1)S(1)} %get-tuple-element.31), channel_id=1, source_target_pairs={{0,2},{1,3},{2,0},{3,1},{4,6},{5,7},{6,4},{7,5},{8,10},{9,11},{10,... | collective-permute-start | bytes 688136 | tf_op jit(solution)/shard_map/ppermute | solution.py:410
  66.2 6.5 %collective-permute-start.13 = (bf16[32,1792]{1,0:T(8,128)(2,1)S(1)}, bf16[32,1792]{1,0:T(8,128)(2,1)S(1)}, u32[]{:S(2)}, u32[]{:S(2)}) collective-permute-start(bf16[32,1792]{1,0:T(8,128)(2,1)S(1)} %activate.3.refs_0_), channel_id=1, source_target_pairs={{0,2},{1,3},{2,0},{3,1},{4,6},{5,7},{6,4},{7,5},{8,10},{9,11},{10,... | collective-permute-start | bytes 344072 | tf_op jit(solution)/shard_map/ppermute | solution.py:410
  71.2 4.9 %collective-permute-start.8 = (bf16[32,1792]{1,0:T(8,128)(2,1)S(1)}, bf16[32,1792]{1,0:T(8,128)(2,1)S(1)}, u32[]{:S(2)}, u32[]{:S(2)}) collective-permute-start(bf16[32,1792]{1,0:T(8,128)(2,1)S(1)} %activate.2.refs_0_.refs_1_), channel_id=1, source_target_pairs={{0,2},{1,3},{2,0},{3,1},{4,6},{5,7},{6,4},{7,5},{8,10},{9,11},{10,... | collective-permute-start | bytes 344072 | tf_op jit(solution)/shard_map/ppermute | solution.py:410
  71.7 4.3 %collective-permute-start.14 = (bf16[32,1792]{1,0:T(8,128)(2,1)S(1)}, bf16[32,1792]{1,0:T(8,128)(2,1)S(1)}, u32[]{:S(2)}, u32[]{:S(2)}) collective-permute-start(bf16[32,1792]{1,0:T(8,128)(2,1)S(1)} %activate.3.refs_0_), channel_id=1, source_target_pairs={{0,1},{1,0},{2,3},{3,2},{4,5},{5,4},{6,7},{7,6},{8,9},{9,8},{10,11... | collective-permute-start | bytes 344072 | tf_op jit(solution)/shard_map/ppermute | solution.py:410
  72.7 3.3 %collective-permute-start.15 = (bf16[32,1792]{1,0:T(8,128)(2,1)S(1)}, bf16[32,1792]{1,0:T(8,128)(2,1)S(1)}, u32[]{:S(2)}, u32[]{:S(2)}) collective-permute-start(bf16[32,1792]{1,0:T(8,128)(2,1)S(1)} %collective-permute-done.13.refs_1_), channel_id=1, source_target_pairs={{0,1},{1,0},{2,3},{3,2},{4,5},{5,4},{6,7},{7,6},{8,9},{9,8},{10,11... | collective-permute-start | bytes 344072 | tf_op jit(solution)/shard_map/ppermute | solution.py:410
  72.7 7.0 %collective-permute-start.9 = (bf16[32,1792]{1,0:T(8,128)(2,1)S(1)}, bf16[32,1792]{1,0:T(8,128)(2,1)S(1)}, u32[]{:S(2)}, u32[]{:S(2)}) collective-permute-start(bf16[32,1792]{1,0:T(8,128)(2,1)S(1)} %activate.2.refs_0_.refs_1_), channel_id=1, source_target_pairs={{0,1},{1,0},{2,3},{3,2},{4,5},{5,4},{6,7},{7,6},{8,9},{9,8},{10,11... | collective-permute-start | bytes 344072 | tf_op jit(solution)/shard_map/ppermute | solution.py:410
  76.0 3.7 %collective-permute-start.10 = (bf16[32,1792]{1,0:T(8,128)(2,1)S(1)}, bf16[32,1792]{1,0:T(8,128)(2,1)S(1)}, u32[]{:S(2)}, u32[]{:S(2)}) collective-permute-start(bf16[32,1792]{1,0:T(8,128)(2,1)S(1)} %collective-permute-done.8.refs_1_), channel_id=1, source_target_pairs={{0,1},{1,0},{2,3},{3,2},{4,5},{5,4},{6,7},{7,6},{8,9},{9,8},{10,11... | collective-permute-start | bytes 344072 | tf_op jit(solution)/shard_map/ppermute | solution.py:410
  84.1 8.3 %collective-permute-start.16 = (bf16[4,8,2048]{2,1,0:T(8,128)(2,1)S(1)}, bf16[4,8,2048]{2,1,0:T(8,128)(2,1)S(1)}, u32[]{:S(2)}, u32[]{:S(2)}) collective-permute-start(bf16[4,8,2048]{2,1,0:T(8,128)(2,1)S(1)} %get-tuple-element.37), channel_id=1, source_target_pairs={{0,4},{4,8},{8,12},{12,0},{1,5},{5,9},{9,13},{13,1},{2,6},{6,10},{... | collective-permute-start | bytes 393224 | tf_op jit(solution)/shard_map/ppermute | solution.py:463
  84.5 12.9 %collective-permute-start.17 = (bf16[4,8,2048]{2,1,0:T(8,128)(2,1)S(1)}, bf16[4,8,2048]{2,1,0:T(8,128)(2,1)S(1)}, u32[]{:S(2)}, u32[]{:S(2)}) collective-permute-start(bf16[4,8,2048]{2,1,0:T(8,128)(2,1)S(1)} %get-tuple-element.38), channel_id=1, source_target_pairs={{0,8},{4,12},{8,0},{12,4},{1,9},{5,13},{9,1},{13,5},{2,10},{6,14},... | collective-permute-start | bytes 393224 | tf_op jit(solution)/shard_map/ppermute | solution.py:463
  86.5 10.9 %collective-permute-start.18 = (bf16[4,8,2048]{2,1,0:T(8,128)(2,1)S(1)}, bf16[4,8,2048]{2,1,0:T(8,128)(2,1)S(1)}, u32[]{:S(2)}, u32[]{:S(2)}) collective-permute-start(bf16[4,8,2048]{2,1,0:T(8,128)(2,1)S(1)} %get-tuple-element.39), channel_id=1, source_target_pairs={{0,12},{4,0},{8,4},{12,8},{1,13},{5,1},{9,5},{13,9},{2,14},{6,2},{... | collective-permute-start | bytes 393224 | tf_op jit(solution)/shard_map/ppermute | solution.py:463
  97.4 4.2 %collective-permute-start.19 = (bf16[8,2048]{1,0:T(8,128)(2,1)S(1)}, bf16[8,2048]{1,0:T(8,128)(2,1)S(1)}, u32[]{:S(2)}, u32[]{:S(2)}) collective-permute-start(bf16[8,2048]{1,0:T(8,128)(2,1)S(1)} %get-tuple-element.41), channel_id=1, source_target_pairs={{0,2},{1,3},{2,0},{3,1},{4,6},{5,7},{6,4},{7,5},{8,10},{9,11},{10,... | collective-permute-start | bytes 98312 | tf_op jit(solution)/shard_map/ppermute | solution.py:410
  98.2 3.4 %collective-permute-start.20 = (bf16[8,2048]{1,0:T(8,128)(2,1)S(1)}, bf16[8,2048]{1,0:T(8,128)(2,1)S(1)}, u32[]{:S(2)}, u32[]{:S(2)}) collective-permute-start(bf16[8,2048]{1,0:T(8,128)(2,1)S(1)} %get-tuple-element.42), channel_id=1, source_target_pairs={{0,1},{1,0},{2,3},{3,2},{4,5},{5,4},{6,7},{7,6},{8,9},{9,8},{10,11... | collective-permute-start | bytes 98312 | tf_op jit(solution)/shard_map/ppermute | solution.py:410
  98.2 3.5 %collective-permute-start.21 = (bf16[8,2048]{1,0:T(8,128)(2,1)S(1)}, bf16[8,2048]{1,0:T(8,128)(2,1)S(1)}, u32[]{:S(2)}, u32[]{:S(2)}) collective-permute-start(bf16[8,2048]{1,0:T(8,128)(2,1)S(1)} %get-tuple-element.43), channel_id=1, source_target_pairs={{0,3},{1,2},{2,1},{3,0},{4,7},{5,6},{6,5},{7,4},{8,11},{9,10},{10,... | collective-permute-start | bytes 98312 | tf_op jit(solution)/shard_map/ppermute | solution.py:410
  (11 other events, 81.1 us)

commit v2 on v1

--- a/solution.py
+++ b/solution.py
@@ -13,6 +13,10 @@
 BF16 = jnp.bfloat16
 SMEM = pltpu.MemorySpace.SMEM
 VMEM = pltpu.MemorySpace.VMEM
+
+
+def in_hbm(value):
+    return pltpu.with_memory_space_constraint(value, pltpu.MemorySpace.HBM)
 
 
 def attend_kernel(
@@ -103,16 +107,16 @@
         out_specs=[pl.BlockSpec((seqs, depth), lambda i: (0, 0))]
         + [pl.BlockSpec((seqs, depth // columns), lambda i: (0, 0))] * columns,
         scratch_shapes=[pltpu.VMEM((depth // kvh // HD * seqs, seqs * cache), F32)],
-        compiler_params=pltpu.CompilerParams(vmem_limit_bytes=16 * 1024 * 1024),
-        cost_estimate=pl.CostEstimate(flops=10**9, bytes_accessed=10**7, transcendentals=10**6),
+        compiler_params=pltpu.CompilerParams(vmem_limit_bytes=8 * 1024 * 1024),
+        cost_estimate=pl.CostEstimate(flops=10**11, bytes_accessed=10**8, transcendentals=10**8),
         name="attend",
     )(
         cache_len.reshape(batches, rows),
-        query.reshape(batches, rows, depth),
-        key_cache.reshape(seqs * cache, kv),
-        value_cache.reshape(seqs * cache, kv),
-        residual.reshape(batches, rows, depth),
-        norm_gain.reshape(1, depth),
+        in_hbm(query.reshape(batches, rows, depth)),
+        in_hbm(key_cache.reshape(seqs * cache, kv)),
+        in_hbm(value_cache.reshape(seqs * cache, kv)),
+        in_hbm(residual.reshape(batches, rows, depth)),
+        in_hbm(norm_gain.reshape(1, depth)),
     )
 
 
@@ -123,7 +127,7 @@
     return found
 
 
-def gate_up_kernel(cols, batches, ffn, table_ref, *refs):
+def gate_up_kernel(cols, batches, ffn, start, table_ref, *refs):
     pairs, reps = cols
     columns = pairs * reps
     pieces = refs[:ffn]
@@ -132,8 +136,7 @@
     rows = seqs // batches
     half = rows_ref.shape[0] // reps
 
-    @pl.when(pl.program_id(0) == 0)
-    def _():
+    def order():
         pair = lax.axis_index("pair")
         rep = lax.axis_index("rep")
         first = lax.broadcasted_iota(jnp.int32, pieces[0].shape[1:], 0) < rows
@@ -155,36 +158,40 @@
                     base = ((index * batches + micro) * ffn + shift) * rows
                     rows_ref[base : base + 2 * rows, :] = jnp.where(first, a, b).astype(BF16)
 
+    order()
+    width = keep_ref.shape[2]
+    tile = math.gcd(width, 256)
     for place, weight_ref in enumerate((gate_ref, up_ref)):
-        sums = jnp.dot(rows_ref[...], weight_ref[...], preferred_element_type=F32)
-        keep_ref[place] = sums[:half]
-        send_ref[place] = sums[half:].astype(BF16)
+        for low in range(0, width, tile):
+            part = slice(low, low + tile)
+            sums = jnp.dot(
+                rows_ref[...],
+                weight_ref[:, start + low : start + low + tile],
+                preferred_element_type=F32,
+            )
+            keep_ref[place, :, part] = sums[:half]
+            send_ref[place, :, part] = sums[half:].astype(BF16)
 
 
 def gate_up(cols, batches, table, pieces, gate_weight, up_weight, chunk, chunks):
     ffn = len(pieces)
     columns, seqs, depth = pieces[0].shape
     width = gate_weight.shape[1] // chunks
-    tile = math.gcd(width, 256)
-    steps = width // tile
     total = columns * seqs * ffn
     half = total // cols[1]
-    weight = pl.BlockSpec((depth, tile), lambda i: (0, chunk * steps + i))
-    whole = pl.BlockSpec((columns, seqs, depth), lambda i: (0, 0, 0))
-    out = pl.BlockSpec((2, half, tile), lambda i: (0, 0, i))
-    return pl.pallas_call(
-        functools.partial(gate_up_kernel, cols, batches, ffn),
-        grid=(steps,),
+    whole = pl.BlockSpec(memory_space=VMEM)
+    return pl.pallas_call(
+        functools.partial(gate_up_kernel, cols, batches, ffn, chunk * width),
         out_shape=[
             jax.ShapeDtypeStruct((2, half, width), F32),
             jax.ShapeDtypeStruct((2, total - half, width), BF16),
         ],
-        in_specs=[pl.BlockSpec(memory_space=SMEM)] + [whole] * ffn + [weight, weight],
-        out_specs=[out, pl.BlockSpec((2, total - half, tile), lambda i: (0, 0, i))],
+        in_specs=[pl.BlockSpec(memory_space=SMEM)] + [whole] * (ffn + 2),
+        out_specs=[whole, whole],
         scratch_shapes=[pltpu.VMEM((total, depth), BF16)],
-        compiler_params=pltpu.CompilerParams(vmem_limit_bytes=32 * 1024 * 1024),
+        compiler_params=pltpu.CompilerParams(vmem_limit_bytes=8 * 1024 * 1024),
         cost_estimate=pl.CostEstimate(
-            flops=4 * total * depth * width, bytes_accessed=4 * depth * width, transcendentals=0
+            flops=10**11, bytes_accessed=10**8, transcendentals=0
         ),
         name=f"gate_up_{chunk}",
     )(table, *pieces, gate_weight, up_weight)
@@ -213,7 +220,7 @@
         + [jax.ShapeDtypeStruct((two, rows, width), BF16)] * (pairs - 1),
         in_specs=[block(total)] * 2,
         out_specs=[block(rows)] * pairs,
-        compiler_params=pltpu.CompilerParams(vmem_limit_bytes=16 * 1024 * 1024),
+        compiler_params=pltpu.CompilerParams(vmem_limit_bytes=8 * 1024 * 1024),
         cost_estimate=pl.CostEstimate(flops=keep.size, bytes_accessed=6 * keep.size, transcendentals=0),
         name="join",
     )(keep, came)
@@ -237,7 +244,7 @@
         out_shape=jax.ShapeDtypeStruct((rows, width), BF16),
         in_specs=[block] * (1 + len(arrived)),
         out_specs=pl.BlockSpec((rows, tile), lambda i: (0, i)),
-        compiler_params=pltpu.CompilerParams(vmem_limit_bytes=16 * 1024 * 1024),
+        compiler_params=pltpu.CompilerParams(vmem_limit_bytes=8 * 1024 * 1024),
         cost_estimate=pl.CostEstimate(flops=own.size, bytes_accessed=6 * own.size, transcendentals=own.size),
         name="activate",
     )(own, *arrived)
@@ -264,43 +271,39 @@
         out_shape=jax.ShapeDtypeStruct((batches, 1, total // batches, width), BF16),
         in_specs=[pl.BlockSpec(memory_space=VMEM)] * len(hidden),
         out_specs=pl.BlockSpec(memory_space=VMEM),
-        compiler_params=pltpu.CompilerParams(vmem_limit_bytes=16 * 1024 * 1024),
+        compiler_params=pltpu.CompilerParams(vmem_limit_bytes=8 * 1024 * 1024),
         name="serve",
     )(*hidden)
 
 
-def down_kernel(count, has_sum, hidden_count, *refs):
+def down_kernel(start, has_sum, hidden_count, *refs):
     hidden_refs = refs[:hidden_count]
     weight_ref = refs[hidden_count]
-    out_ref = refs[-2]
-    rows_ref = refs[-1]
-
-    @pl.when(pl.program_id(0) == 0)
-    def _():
-        rows_ref[...] = jnp.concatenate([ref[...] for ref in hidden_refs], axis=0)
-
-    sums = jnp.dot(rows_ref[...], weight_ref[...], preferred_element_type=F32)
-    if has_sum:
-        sums = sums + refs[hidden_count + 1][...]
-    out_ref[...] = sums
+    out_ref = refs[-1]
+    rows = jnp.concatenate([ref[...] for ref in hidden_refs], axis=0)
+    depth = out_ref.shape[1]
+    tile = math.gcd(depth, 256)
+    for low in range(0, depth, tile):
+        part = slice(low, low + tile)
+        sums = jnp.dot(
+            rows, weight_ref[start : start + rows.shape[1], part], preferred_element_type=F32
+        )
+        if has_sum:
+            sums = sums + refs[hidden_count + 1][:, part]
+        out_ref[:, part] = sums
 
 
 def down(hidden, weight, chunk, chunks, before):
     width = weight.shape[0] // chunks
     depth = weight.shape[1]
-    tile = math.gcd(depth, 256)
     total = sum(h.shape[0] for h in hidden)
-    part = pl.BlockSpec((total, tile), lambda i: (0, i))
-    return pl.pallas_call(
-        functools.partial(down_kernel, chunks, before is not None, len(hidden)),
-        grid=(depth // tile,),
+    whole = pl.BlockSpec(memory_space=VMEM)
+    return pl.pallas_call(
+        functools.partial(down_kernel, chunk * width, before is not None, len(hidden)),
         out_shape=jax.ShapeDtypeStruct((total, depth), F32),
-        in_specs=[pl.BlockSpec(h.shape, lambda i: (0, 0)) for h in hidden]
-        + [pl.BlockSpec((width, tile), lambda i: (chunk, i))]
-        + [part] * (before is not None),
-        out_specs=part,
-        scratch_shapes=[pltpu.VMEM((total, width), BF16)],
-        compiler_params=pltpu.CompilerParams(vmem_limit_bytes=32 * 1024 * 1024),
+        in_specs=[whole] * (len(hidden) + 1 + (before is not None)),
+        out_specs=whole,
+        compiler_params=pltpu.CompilerParams(vmem_limit_bytes=8 * 1024 * 1024),
         cost_estimate=pl.CostEstimate(
             flops=2 * total * depth * width, bytes_accessed=2 * depth * width, transcendentals=0
         ),
@@ -344,7 +347,7 @@
         out_shape=[jax.ShapeDtypeStruct((columns, batches * rows, depth), BF16)] * ffn,
         in_specs=[pl.BlockSpec(memory_space=SMEM), pl.BlockSpec(memory_space=VMEM)],
         out_specs=[pl.BlockSpec(memory_space=VMEM)] * ffn,
-        compiler_params=pltpu.CompilerParams(vmem_limit_bytes=16 * 1024 * 1024),
+        compiler_params=pltpu.CompilerParams(vmem_limit_bytes=8 * 1024 * 1024),
         name="arrange",
     )(table, sums)
 
@@ -367,7 +370,7 @@
         out_shape=[jax.ShapeDtypeStruct((seqs, depth), BF16)] * columns,
         in_specs=[pl.BlockSpec(memory_space=VMEM)] * len(parts),
         out_specs=[pl.BlockSpec(memory_space=VMEM)] * columns,
-        compiler_params=pltpu.CompilerParams(vmem_limit_bytes=16 * 1024 * 1024),
+        compiler_params=pltpu.CompilerParams(vmem_limit_bytes=8 * 1024 * 1024),
         name="total",
     )(*parts)
 
@@ -395,7 +398,7 @@
         out_shape=jax.ShapeDtypeStruct((batches, 1, seqs // batches, depth), F32),
         in_specs=[pl.BlockSpec(memory_space=VMEM)] * (1 + len(changes)),
         out_specs=pl.BlockSpec(memory_space=VMEM),
-        compiler_params=pltpu.CompilerParams(vmem_limit_bytes=16 * 1024 * 1024),
+        compiler_params=pltpu.CompilerParams(vmem_limit_bytes=8 * 1024 * 1024),
         name="finish",
     )(stream, *changes)
 

time: 103 us -> 76.7 us (0.74)
  Pallas kernels: 32.9 us -> 18 us
  local copies, waits for them, and re-layouts: 12.3 us -> 0.73 us
    pallas_call x4, Pallas kernels: 24.3 us -> 7.92 us  [the longest x2 5.56 us: gate_up(): pl.pallas_call(functools.partial(gate_up_kernel, cols, batches, ffn, chun...]
    unnamed x26 -> x24, local copies, waits for them, and re-layouts: 12.3 us -> 0.73 us
    pallas_call x1, Pallas kernels: 5.29 us -> 6.83 us  [attend(): pl.pallas_call(functools.partial(attend_kernel, cols, kvh, heads_per_step...]
  transfers between devices with their start and end apart: 22 -> 22, of which waited for: 13 -> 14; matrix products, arithmetic and copies ran while one was open for 0% -> 0% of each run, Pallas kernels for 14% -> 8%
where the time goes in v2:
time: 76.7 us; the launch traced here: 76.3 us
  waiting for transfers between devices  37.6 us (49%)
  starting transfers between devices  19 us (25%)
  Pallas kernels  18 us (23%)
  between operations  0.92 us (1%)
    ppermute x16, waiting for transfers between devices, to_column(): return lax.ppermute(value, ('pair', 'rep'), route)  19.8 us
    ppermute x3, waiting for transfers between devices, per_device(): lax.ppermute(mine, 'ffn', [(i, (i - s) % ffn) for i in range(ffn)])  9.8 us
    ppermute x16, starting transfers between devices, to_column(): return lax.ppermute(value, ('pair', 'rep'), route)  9.28 us
    ppermute x3, waiting for transfers between devices, per_device(): lax.ppermute(shares[s], 'ffn', [(i, (i + s) % ffn) for i in range(ffn)])  8.04 us
    pallas_call x1, Pallas kernels, attend(): pl.pallas_call(functools.partial(attend_kernel, cols, kvh, heads_per_step...  6.83 us
    pallas_call x2, Pallas kernels, gate_up(): pl.pallas_call(functools.partial(gate_up_kernel, cols, batches, ffn, chun...  5.56 us
    ppermute x3, starting transfers between devices, per_device(): lax.ppermute(shares[s], 'ffn', [(i, (i + s) % ffn) for i in range(ffn)])  5.05 us
    ppermute x3, starting transfers between devices, per_device(): lax.ppermute(mine, 'ffn', [(i, (i - s) % ffn) for i in range(ffn)])  4.67 us
  transfers between devices with their start and end apart: 22, of which 14 were waited for; matrix products, arithmetic and copies ran while one was open for 0% of the time, Pallas kernels for 8%

profile of v2, /device:TPU:0, one launch (start us, length us, event | category | flops | bytes accessed | tf_op | source)
XLA Modules:
  0.0 76.3 jit_solution(2813028265369087628)
XLA Ops:
  1.3 6.8 %attend.1 = (f32[8,8192]{1,0:T(8,128)S(1)}, bf16[8,2048]{1,0:T(8,128)(2,1)S(1)}, bf16[8,2048]{1,0:T(8,128)(2,1)S(1)}, bf16[8,2048]{1,0:T(8,128)(2,1)S(1)}, bf16[8,2048]{1,0:T(8,128)(2,1)S(1)}) custom-call(s32[2,4]{1,0:T(2,128)S(1)} %bitcast.15, bf16[2,4,8192]{2,1,0:T(4,128)(2,1)} %bitcast.22, bf16[1024,1024]{1,0:T(8,128)(2,1)} %bitcast.19, ...), custom_call_target="tpu_custom_call" | custom-call | flops 99999997952 | bytes 100000000 | tf_op jit(solution)/shard_map/attend/pallas_call | solution.py:94
  8.2 2.4 %collective-permute-start.2 = (bf16[8,2048]{1,0:T(8,128)(2,1)S(1)}, bf16[8,2048]{1,0:T(8,128)(2,1)S(1)}, u32[]{:S(2)}, u32[]{:S(2)}) collective-permute-start(bf16[8,2048]{1,0:T(8,128)(2,1)S(1)} %get-tuple-element.27), channel_id=1, source_target_pairs={{0,3},{1,2},{2,1},{3,0},{4,7},{5,6},{6,5},{7,4},{8,11},{9,10},{10,... | collective-permute-start | bytes 98312 | tf_op jit(solution)/shard_map/ppermute | solution.py:413
  11.3 1.1 %collective-permute-done.2 = bf16[8,2048]{1,0:T(8,128)(2,1)S(1)} collective-permute-done((bf16[8,2048]{1,0:T(8,128)(2,1)S(1)}, bf16[8,2048]{1,0:T(8,128)(2,1)S(1)}, u32[]{:S(2)}, u32[]{:S(2)}) %collective-permute-start.2) | collective-permute-done | bytes 32800 | tf_op jit(solution)/shard_map/ppermute | solution.py:413
  12.4 2.8 %collective-permute-done = bf16[8,2048]{1,0:T(8,128)(2,1)S(1)} collective-permute-done((bf16[8,2048]{1,0:T(8,128)(2,1)S(1)}, bf16[8,2048]{1,0:T(8,128)(2,1)S(1)}, u32[]{:S(2)}, u32[]{:S(2)}) %collective-permute-start) | collective-permute-done | bytes 32800 | tf_op jit(solution)/shard_map/ppermute | solution.py:413
  15.2 3.7 %collective-permute-start.3 = (bf16[4,8,2048]{2,1,0:T(8,128)(2,1)S(1)}, bf16[4,8,2048]{2,1,0:T(8,128)(2,1)S(1)}, u32[]{:S(2)}, u32[]{:S(2)}) collective-permute-start(bf16[4,8,2048]{2,1,0:T(8,128)(2,1)S(1)} %pad_maximum_fusion.refs_0_), channel_id=1, source_target_pairs={{0,12},{4,0},{8,4},{12,8},{1,13},{5,1},{9,5},{13,9},{2,14},{6,2},{... | collective-permute-start | bytes 393224 | tf_op jit(solution)/shard_map/ppermute | solution.py:447
  18.9 1.0 %collective-permute-start.5 = (bf16[4,8,2048]{2,1,0:T(8,128)(2,1)S(1)}, bf16[4,8,2048]{2,1,0:T(8,128)(2,1)S(1)}, u32[]{:S(2)}, u32[]{:S(2)}) collective-permute-start(bf16[4,8,2048]{2,1,0:T(8,128)(2,1)S(1)} %pad_maximum_fusion.refs_0_), channel_id=1, source_target_pairs={{0,4},{4,8},{8,12},{12,0},{1,5},{5,9},{9,13},{13,1},{2,6},{6,10},{... | collective-permute-start | bytes 393224 | tf_op jit(solution)/shard_map/ppermute | solution.py:447
  19.9 2.9 %collective-permute-done.3.refs_1_ = bf16[4,8,2048]{2,1,0:T(8,128)(2,1)S(1)} collective-permute-done((bf16[4,8,2048]{2,1,0:T(8,128)(2,1)S(1)}, bf16[4,8,2048]{2,1,0:T(8,128)(2,1)S(1)}, u32[]{:S(2)}, u32[]{:S(2)}) %collective-permute-start.3) | collective-permute-done | bytes 131104 | tf_op jit(solution)/shard_map/ppermute | solution.py:447
  22.9 6.9 %collective-permute-done.4.refs_2_ = bf16[4,8,2048]{2,1,0:T(8,128)(2,1)S(1)} collective-permute-done((bf16[4,8,2048]{2,1,0:T(8,128)(2,1)S(1)}, bf16[4,8,2048]{2,1,0:T(8,128)(2,1)S(1)}, u32[]{:S(2)}, u32[]{:S(2)}) %collective-permute-start.4) | collective-permute-done | bytes 131104 | tf_op jit(solution)/shard_map/ppermute | solution.py:447
  29.7 2.8 %gate_up_0.1 = (f32[2,64,1792]{2,1,0:T(8,128)S(1)}, bf16[2,64,1792]{2,1,0:T(8,128)(2,1)S(1)}) custom-call(s32[2,4]{1,0:T(2,128)S(1)} %copy-done, bf16[4,8,2048]{2,1,0:T(8,128)(2,1)S(1)} %pad_maximum_fusion.refs_0_, bf16[4,8,2048]{2,1,0:T(8,128)(2,1)S(1)} %collective-permute-done.3.refs_1_, bf16[4,8,2048]{2,1,0:T(8,128)(2,1)S(1)} %collective-permute-done.4.refs_2_, ...), custom_call_target="tpu_custom_call" | custom-call | flops 99999997952 | bytes 100000000 | tf_op jit(solution)/shard_map/gate_up_0/pallas_call | solution.py:183
  32.7 2.8 %gate_up_1.1 = (f32[2,64,1792]{2,1,0:T(8,128)S(1)}, bf16[2,64,1792]{2,1,0:T(8,128)(2,1)S(1)}) custom-call(s32[2,4]{1,0:T(2,128)S(1)} %copy-done, bf16[4,8,2048]{2,1,0:T(8,128)(2,1)S(1)} %pad_maximum_fusion.refs_0_, bf16[4,8,2048]{2,1,0:T(8,128)(2,1)S(1)} %collective-permute-done.3.refs_1_, bf16[4,8,2048]{2,1,0:T(8,128)(2,1)S(1)} %collective-permute-done.4.refs_2_, ...), custom_call_target="tpu_custom_call" | custom-call | flops 99999997952 | bytes 100000000 | tf_op jit(solution)/shard_map/gate_up_1/pallas_call | solution.py:183
  37.8 1.0 %collective-permute-start.7 = (bf16[2,32,1792]{2,1,0:T(8,128)(2,1)S(1)}, bf16[2,32,1792]{2,1,0:T(8,128)(2,1)S(1)}, u32[]{:S(2)}, u32[]{:S(2)}) collective-permute-start(bf16[2,32,1792]{2,1,0:T(8,128)(2,1)S(1)} %get-tuple-element.31), channel_id=1, source_target_pairs={{0,2},{1,3},{2,0},{3,1},{4,6},{5,7},{6,4},{7,5},{8,10},{9,11},{10,... | collective-permute-start | bytes 688136 | tf_op jit(solution)/shard_map/ppermute | solution.py:413
  38.8 6.1 %collective-permute-done.12.refs_0_ = bf16[2,32,1792]{2,1,0:T(8,128)(2,1)S(1)} collective-permute-done((bf16[2,32,1792]{2,1,0:T(8,128)(2,1)S(1)}, bf16[2,32,1792]{2,1,0:T(8,128)(2,1)S(1)}, u32[]{:S(2)}, u32[]{:S(2)}) %collective-permute-start.12) | collective-permute-done | bytes 229408 | tf_op jit(solution)/shard_map/ppermute | solution.py:413
  45.7 4.1 %collective-permute-done.7.refs_0_ = bf16[2,32,1792]{2,1,0:T(8,128)(2,1)S(1)} collective-permute-done((bf16[2,32,1792]{2,1,0:T(8,128)(2,1)S(1)}, bf16[2,32,1792]{2,1,0:T(8,128)(2,1)S(1)}, u32[]{:S(2)}, u32[]{:S(2)}) %collective-permute-start.7) | collective-permute-done | bytes 229408 | tf_op jit(solution)/shard_map/ppermute | solution.py:413
  50.6 1.0 %collective-permute-done.13.refs_1_ = bf16[32,1792]{1,0:T(8,128)(2,1)S(1)} collective-permute-done((bf16[32,1792]{1,0:T(8,128)(2,1)S(1)}, bf16[32,1792]{1,0:T(8,128)(2,1)S(1)}, u32[]{:S(2)}, u32[]{:S(2)}) %collective-permute-start.13) | collective-permute-done | bytes 114720 | tf_op jit(solution)/shard_map/ppermute | solution.py:413
  52.1 2.7 %collective-permute-done.8.refs_1_ = bf16[32,1792]{1,0:T(8,128)(2,1)S(1)} collective-permute-done((bf16[32,1792]{1,0:T(8,128)(2,1)S(1)}, bf16[32,1792]{1,0:T(8,128)(2,1)S(1)}, u32[]{:S(2)}, u32[]{:S(2)}) %collective-permute-start.8) | collective-permute-done | bytes 114720 | tf_op jit(solution)/shard_map/ppermute | solution.py:413
  54.9 1.2 %down_0.1.refs_5_ = f32[128,2048]{1,0:T(8,128)S(1)} custom-call(bf16[32,1792]{1,0:T(8,128)(2,1)S(1)} %activate.3.refs_0_, bf16[32,1792]{1,0:T(8,128)(2,1)S(1)} %collective-permute-done.13.refs_1_, bf16[32,1792]{1,0:T(8,128)(2,1)S(1)} %collective-permute-done.14.refs_2_, bf16[32,1792]{1,0:T(8,128)(2,1)S(1)} %collective-permute-done.15.refs_3_, ...), custom_call_target="tpu_custom_call" | custom-call | flops 939524096 | bytes 7340032 | tf_op jit(solution)/shard_map/down_0/pallas_call | solution.py:301
  56.2 1.2 %down_1.1.sums_ref = f32[128,2048]{1,0:T(8,128)S(1)} custom-call(bf16[32,1792]{1,0:T(8,128)(2,1)S(1)} %activate.2.refs_0_.refs_1_, bf16[32,1792]{1,0:T(8,128)(2,1)S(1)} %collective-permute-done.8.refs_1_, bf16[32,1792]{1,0:T(8,128)(2,1)S(1)} %collective-permute-done.9.refs_2_, bf16[32,1792]{1,0:T(8,128)(2,1)S(1)} %collective-permute-done.10.refs_3_, ...), custom_call_target="tpu_custom_call" | custom-call | flops 939524096 | bytes 7340032 | tf_op jit(solution)/shard_map/down_1/pallas_call | solution.py:301
  58.3 2.0 %collective-permute-start.17 = (bf16[4,8,2048]{2,1,0:T(8,128)(2,1)S(1)}, bf16[4,8,2048]{2,1,0:T(8,128)(2,1)S(1)}, u32[]{:S(2)}, u32[]{:S(2)}) collective-permute-start(bf16[4,8,2048]{2,1,0:T(8,128)(2,1)S(1)} %get-tuple-element.38), channel_id=1, source_target_pairs={{0,8},{4,12},{8,0},{12,4},{1,9},{5,13},{9,1},{13,5},{2,10},{6,14},... | collective-permute-start | bytes 393224 | tf_op jit(solution)/shard_map/ppermute | solution.py:466
  60.3 2.8 %collective-permute-start.18 = (bf16[4,8,2048]{2,1,0:T(8,128)(2,1)S(1)}, bf16[4,8,2048]{2,1,0:T(8,128)(2,1)S(1)}, u32[]{:S(2)}, u32[]{:S(2)}) collective-permute-start(bf16[4,8,2048]{2,1,0:T(8,128)(2,1)S(1)} %get-tuple-element.39), channel_id=1, source_target_pairs={{0,12},{4,0},{8,4},{12,8},{1,13},{5,1},{9,5},{13,9},{2,14},{6,2},{... | collective-permute-start | bytes 393224 | tf_op jit(solution)/shard_map/ppermute | solution.py:466
  63.1 3.2 %collective-permute-done.16.refs_1_ = bf16[4,8,2048]{2,1,0:T(8,128)(2,1)S(1)} collective-permute-done((bf16[4,8,2048]{2,1,0:T(8,128)(2,1)S(1)}, bf16[4,8,2048]{2,1,0:T(8,128)(2,1)S(1)}, u32[]{:S(2)}, u32[]{:S(2)}) %collective-permute-start.16) | collective-permute-done | bytes 131104 | tf_op jit(solution)/shard_map/ppermute | solution.py:466
  66.4 4.8 %collective-permute-done.17.refs_2_ = bf16[4,8,2048]{2,1,0:T(8,128)(2,1)S(1)} collective-permute-done((bf16[4,8,2048]{2,1,0:T(8,128)(2,1)S(1)}, bf16[4,8,2048]{2,1,0:T(8,128)(2,1)S(1)}, u32[]{:S(2)}, u32[]{:S(2)}) %collective-permute-start.17) | collective-permute-done | bytes 131104 | tf_op jit(solution)/shard_map/ppermute | solution.py:466
  71.2 0.9 %collective-permute-start.19 = (bf16[8,2048]{1,0:T(8,128)(2,1)S(1)}, bf16[8,2048]{1,0:T(8,128)(2,1)S(1)}, u32[]{:S(2)}, u32[]{:S(2)}) collective-permute-start(bf16[8,2048]{1,0:T(8,128)(2,1)S(1)} %get-tuple-element.41), channel_id=1, source_target_pairs={{0,2},{1,3},{2,0},{3,1},{4,6},{5,7},{6,4},{7,5},{8,10},{9,11},{10,... | collective-permute-start | bytes 98312 | tf_op jit(solution)/shard_map/ppermute | solution.py:413
  72.2 1.3 %collective-permute-start.21 = (bf16[8,2048]{1,0:T(8,128)(2,1)S(1)}, bf16[8,2048]{1,0:T(8,128)(2,1)S(1)}, u32[]{:S(2)}, u32[]{:S(2)}) collective-permute-start(bf16[8,2048]{1,0:T(8,128)(2,1)S(1)} %get-tuple-element.43), channel_id=1, source_target_pairs={{0,3},{1,2},{2,1},{3,0},{4,7},{5,6},{6,5},{7,4},{8,11},{9,10},{10,... | collective-permute-start | bytes 98312 | tf_op jit(solution)/shard_map/ppermute | solution.py:413
  74.2 1.1 %collective-permute-done.19.refs_1_ = bf16[8,2048]{1,0:T(8,128)(2,1)S(1)} collective-permute-done((bf16[8,2048]{1,0:T(8,128)(2,1)S(1)}, bf16[8,2048]{1,0:T(8,128)(2,1)S(1)}, u32[]{:S(2)}, u32[]{:S(2)}) %collective-permute-start.19) | collective-permute-done | bytes 32800 | tf_op jit(solution)/shard_map/ppermute | solution.py:413
  (60 shorter events, 8.8 us)
Async XLA Ops:
  1.3 28.4 %copy-start.1 = (bf16[2048,3584]{1,0:T(8,128)(2,1)S(1)}, bf16[2048,3584]{1,0:T(8,128)(2,1)}, u32[]{:S(2)}) copy-start(bf16[2048,3584]{1,0:T(8,128)(2,1)} %refs_4_.5) | copy-start | bytes 44040196
  1.3 28.4 %copy-start.2 = (bf16[2048,3584]{1,0:T(8,128)(2,1)S(1)}, bf16[2048,3584]{1,0:T(8,128)(2,1)}, u32[]{:S(2)}) copy-start(bf16[2048,3584]{1,0:T(8,128)(2,1)} %refs_5_.3) | copy-start | bytes 44040196
  8.2 4.2 %collective-permute-start.2 = (bf16[8,2048]{1,0:T(8,128)(2,1)S(1)}, bf16[8,2048]{1,0:T(8,128)(2,1)S(1)}, u32[]{:S(2)}, u32[]{:S(2)}) collective-permute-start(bf16[8,2048]{1,0:T(8,128)(2,1)S(1)} %get-tuple-element.27), channel_id=1, source_target_pairs={{0,3},{1,2},{2,1},{3,0},{4,7},{5,6},{6,5},{7,4},{8,11},{9,10},{10,... | collective-permute-start | bytes 98312 | tf_op jit(solution)/shard_map/ppermute | solution.py:413
  10.6 1.8 %collective-permute-start.1 = (bf16[8,2048]{1,0:T(8,128)(2,1)S(1)}, bf16[8,2048]{1,0:T(8,128)(2,1)S(1)}, u32[]{:S(2)}, u32[]{:S(2)}) collective-permute-start(bf16[8,2048]{1,0:T(8,128)(2,1)S(1)} %get-tuple-element.26), channel_id=1, source_target_pairs={{0,1},{1,0},{2,3},{3,2},{4,5},{5,4},{6,7},{7,6},{8,9},{9,8},{10,11... | collective-permute-start | bytes 98312 | tf_op jit(solution)/shard_map/ppermute | solution.py:413
  11.3 3.9 %collective-permute-start = (bf16[8,2048]{1,0:T(8,128)(2,1)S(1)}, bf16[8,2048]{1,0:T(8,128)(2,1)S(1)}, u32[]{:S(2)}, u32[]{:S(2)}) collective-permute-start(bf16[8,2048]{1,0:T(8,128)(2,1)S(1)} %get-tuple-element.25), channel_id=1, source_target_pairs={{0,2},{1,3},{2,0},{3,1},{4,6},{5,7},{6,4},{7,5},{8,10},{9,11},{10,... | collective-permute-start | bytes 98312 | tf_op jit(solution)/shard_map/ppermute | solution.py:413
  15.2 7.6 %collective-permute-start.3 = (bf16[4,8,2048]{2,1,0:T(8,128)(2,1)S(1)}, bf16[4,8,2048]{2,1,0:T(8,128)(2,1)S(1)}, u32[]{:S(2)}, u32[]{:S(2)}) collective-permute-start(bf16[4,8,2048]{2,1,0:T(8,128)(2,1)S(1)} %pad_maximum_fusion.refs_0_), channel_id=1, source_target_pairs={{0,12},{4,0},{8,4},{12,8},{1,13},{5,1},{9,5},{13,9},{2,14},{6,2},{... | collective-permute-start | bytes 393224 | tf_op jit(solution)/shard_map/ppermute | solution.py:447
  18.9 10.8 %collective-permute-start.4 = (bf16[4,8,2048]{2,1,0:T(8,128)(2,1)S(1)}, bf16[4,8,2048]{2,1,0:T(8,128)(2,1)S(1)}, u32[]{:S(2)}, u32[]{:S(2)}) collective-permute-start(bf16[4,8,2048]{2,1,0:T(8,128)(2,1)S(1)} %pad_maximum_fusion.refs_0_), channel_id=1, source_target_pairs={{0,8},{4,12},{8,0},{12,4},{1,9},{5,13},{9,1},{13,5},{2,10},{6,14},... | collective-permute-start | bytes 393224 | tf_op jit(solution)/shard_map/ppermute | solution.py:447
  18.9 10.8 %collective-permute-start.5 = (bf16[4,8,2048]{2,1,0:T(8,128)(2,1)S(1)}, bf16[4,8,2048]{2,1,0:T(8,128)(2,1)S(1)}, u32[]{:S(2)}, u32[]{:S(2)}) collective-permute-start(bf16[4,8,2048]{2,1,0:T(8,128)(2,1)S(1)} %pad_maximum_fusion.refs_0_), channel_id=1, source_target_pairs={{0,4},{4,8},{8,12},{12,0},{1,5},{5,9},{9,13},{13,1},{2,6},{6,10},{... | collective-permute-start | bytes 393224 | tf_op jit(solution)/shard_map/ppermute | solution.py:447
  32.5 3.5 %collective-permute-start.11 = (bf16[2,64,1792]{2,1,0:T(8,128)(2,1)S(1)}, bf16[2,64,1792]{2,1,0:T(8,128)(2,1)S(1)}, u32[]{:S(2)}, u32[]{:S(2)}) collective-permute-start(bf16[2,64,1792]{2,1,0:T(8,128)(2,1)S(1)} %get-tuple-element.33), channel_id=1, source_target_pairs={{0,1},{1,0},{2,3},{3,2},{4,5},{5,4},{6,7},{7,6},{8,9},{9,8},{10,11... | collective-permute-start | bytes 1376264 | tf_op jit(solution)/shard_map/ppermute | solution.py:413
  35.5 2.0 %collective-permute-start.6 = (bf16[2,64,1792]{2,1,0:T(8,128)(2,1)S(1)}, bf16[2,64,1792]{2,1,0:T(8,128)(2,1)S(1)}, u32[]{:S(2)}, u32[]{:S(2)}) collective-permute-start(bf16[2,64,1792]{2,1,0:T(8,128)(2,1)S(1)} %get-tuple-element.29), channel_id=1, source_target_pairs={{0,1},{1,0},{2,3},{3,2},{4,5},{5,4},{6,7},{7,6},{8,9},{9,8},{10,11... | collective-permute-start | bytes 1376264 | tf_op jit(solution)/shard_map/ppermute | solution.py:413
  36.3 8.5 %collective-permute-start.12 = (bf16[2,32,1792]{2,1,0:T(8,128)(2,1)S(1)}, bf16[2,32,1792]{2,1,0:T(8,128)(2,1)S(1)}, u32[]{:S(2)}, u32[]{:S(2)}) collective-permute-start(bf16[2,32,1792]{2,1,0:T(8,128)(2,1)S(1)} %get-tuple-element.35), channel_id=1, source_target_pairs={{0,2},{1,3},{2,0},{3,1},{4,6},{5,7},{6,4},{7,5},{8,10},{9,11},{10,... | collective-permute-start | bytes 688136 | tf_op jit(solution)/shard_map/ppermute | solution.py:413
  37.8 12.0 %collective-permute-start.7 = (bf16[2,32,1792]{2,1,0:T(8,128)(2,1)S(1)}, bf16[2,32,1792]{2,1,0:T(8,128)(2,1)S(1)}, u32[]{:S(2)}, u32[]{:S(2)}) collective-permute-start(bf16[2,32,1792]{2,1,0:T(8,128)(2,1)S(1)} %get-tuple-element.31), channel_id=1, source_target_pairs={{0,2},{1,3},{2,0},{3,1},{4,6},{5,7},{6,4},{7,5},{8,10},{9,11},{10,... | collective-permute-start | bytes 688136 | tf_op jit(solution)/shard_map/ppermute | solution.py:413
  45.1 6.5 %collective-permute-start.13 = (bf16[32,1792]{1,0:T(8,128)(2,1)S(1)}, bf16[32,1792]{1,0:T(8,128)(2,1)S(1)}, u32[]{:S(2)}, u32[]{:S(2)}) collective-permute-start(bf16[32,1792]{1,0:T(8,128)(2,1)S(1)} %activate.3.refs_0_), channel_id=1, source_target_pairs={{0,2},{1,3},{2,0},{3,1},{4,6},{5,7},{6,4},{7,5},{8,10},{9,11},{10,... | collective-permute-start | bytes 344072 | tf_op jit(solution)/shard_map/ppermute | solution.py:413
  50.0 4.9 %collective-permute-start.8 = (bf16[32,1792]{1,0:T(8,128)(2,1)S(1)}, bf16[32,1792]{1,0:T(8,128)(2,1)S(1)}, u32[]{:S(2)}, u32[]{:S(2)}) collective-permute-start(bf16[32,1792]{1,0:T(8,128)(2,1)S(1)} %activate.2.refs_0_.refs_1_), channel_id=1, source_target_pairs={{0,2},{1,3},{2,0},{3,1},{4,6},{5,7},{6,4},{7,5},{8,10},{9,11},{10,... | collective-permute-start | bytes 344072 | tf_op jit(solution)/shard_map/ppermute | solution.py:413
  50.6 4.3 %collective-permute-start.14 = (bf16[32,1792]{1,0:T(8,128)(2,1)S(1)}, bf16[32,1792]{1,0:T(8,128)(2,1)S(1)}, u32[]{:S(2)}, u32[]{:S(2)}) collective-permute-start(bf16[32,1792]{1,0:T(8,128)(2,1)S(1)} %activate.3.refs_0_), channel_id=1, source_target_pairs={{0,1},{1,0},{2,3},{3,2},{4,5},{5,4},{6,7},{7,6},{8,9},{9,8},{10,11... | collective-permute-start | bytes 344072 | tf_op jit(solution)/shard_map/ppermute | solution.py:413
  51.6 3.3 %collective-permute-start.15 = (bf16[32,1792]{1,0:T(8,128)(2,1)S(1)}, bf16[32,1792]{1,0:T(8,128)(2,1)S(1)}, u32[]{:S(2)}, u32[]{:S(2)}) collective-permute-start(bf16[32,1792]{1,0:T(8,128)(2,1)S(1)} %collective-permute-done.13.refs_1_), channel_id=1, source_target_pairs={{0,1},{1,0},{2,3},{3,2},{4,5},{5,4},{6,7},{7,6},{8,9},{9,8},{10,11... | collective-permute-start | bytes 344072 | tf_op jit(solution)/shard_map/ppermute | solution.py:413
  51.6 4.5 %collective-permute-start.9 = (bf16[32,1792]{1,0:T(8,128)(2,1)S(1)}, bf16[32,1792]{1,0:T(8,128)(2,1)S(1)}, u32[]{:S(2)}, u32[]{:S(2)}) collective-permute-start(bf16[32,1792]{1,0:T(8,128)(2,1)S(1)} %activate.2.refs_0_.refs_1_), channel_id=1, source_target_pairs={{0,1},{1,0},{2,3},{3,2},{4,5},{5,4},{6,7},{7,6},{8,9},{9,8},{10,11... | collective-permute-start | bytes 344072 | tf_op jit(solution)/shard_map/ppermute | solution.py:413
  54.9 1.3 %collective-permute-start.10 = (bf16[32,1792]{1,0:T(8,128)(2,1)S(1)}, bf16[32,1792]{1,0:T(8,128)(2,1)S(1)}, u32[]{:S(2)}, u32[]{:S(2)}) collective-permute-start(bf16[32,1792]{1,0:T(8,128)(2,1)S(1)} %collective-permute-done.8.refs_1_), channel_id=1, source_target_pairs={{0,1},{1,0},{2,3},{3,2},{4,5},{5,4},{6,7},{7,6},{8,9},{9,8},{10,11... | collective-permute-start | bytes 344072 | tf_op jit(solution)/shard_map/ppermute | solution.py:413
  58.1 8.3 %collective-permute-start.16 = (bf16[4,8,2048]{2,1,0:T(8,128)(2,1)S(1)}, bf16[4,8,2048]{2,1,0:T(8,128)(2,1)S(1)}, u32[]{:S(2)}, u32[]{:S(2)}) collective-permute-start(bf16[4,8,2048]{2,1,0:T(8,128)(2,1)S(1)} %get-tuple-element.37), channel_id=1, source_target_pairs={{0,4},{4,8},{8,12},{12,0},{1,5},{5,9},{9,13},{13,1},{2,6},{6,10},{... | collective-permute-start | bytes 393224 | tf_op jit(solution)/shard_map/ppermute | solution.py:466
  58.3 12.9 %collective-permute-start.17 = (bf16[4,8,2048]{2,1,0:T(8,128)(2,1)S(1)}, bf16[4,8,2048]{2,1,0:T(8,128)(2,1)S(1)}, u32[]{:S(2)}, u32[]{:S(2)}) collective-permute-start(bf16[4,8,2048]{2,1,0:T(8,128)(2,1)S(1)} %get-tuple-element.38), channel_id=1, source_target_pairs={{0,8},{4,12},{8,0},{12,4},{1,9},{5,13},{9,1},{13,5},{2,10},{6,14},... | collective-permute-start | bytes 393224 | tf_op jit(solution)/shard_map/ppermute | solution.py:466
  60.3 10.9 %collective-permute-start.18 = (bf16[4,8,2048]{2,1,0:T(8,128)(2,1)S(1)}, bf16[4,8,2048]{2,1,0:T(8,128)(2,1)S(1)}, u32[]{:S(2)}, u32[]{:S(2)}) collective-permute-start(bf16[4,8,2048]{2,1,0:T(8,128)(2,1)S(1)} %get-tuple-element.39), channel_id=1, source_target_pairs={{0,12},{4,0},{8,4},{12,8},{1,13},{5,1},{9,5},{13,9},{2,14},{6,2},{... | collective-permute-start | bytes 393224 | tf_op jit(solution)/shard_map/ppermute | solution.py:466
  71.2 4.0 %collective-permute-start.19 = (bf16[8,2048]{1,0:T(8,128)(2,1)S(1)}, bf16[8,2048]{1,0:T(8,128)(2,1)S(1)}, u32[]{:S(2)}, u32[]{:S(2)}) collective-permute-start(bf16[8,2048]{1,0:T(8,128)(2,1)S(1)} %get-tuple-element.41), channel_id=1, source_target_pairs={{0,2},{1,3},{2,0},{3,1},{4,6},{5,7},{6,4},{7,5},{8,10},{9,11},{10,... | collective-permute-start | bytes 98312 | tf_op jit(solution)/shard_map/ppermute | solution.py:413
  72.2 3.1 %collective-permute-start.20 = (bf16[8,2048]{1,0:T(8,128)(2,1)S(1)}, bf16[8,2048]{1,0:T(8,128)(2,1)S(1)}, u32[]{:S(2)}, u32[]{:S(2)}) collective-permute-start(bf16[8,2048]{1,0:T(8,128)(2,1)S(1)} %get-tuple-element.42), channel_id=1, source_target_pairs={{0,1},{1,0},{2,3},{3,2},{4,5},{5,4},{6,7},{7,6},{8,9},{9,8},{10,11... | collective-permute-start | bytes 98312 | tf_op jit(solution)/shard_map/ppermute | solution.py:413
  72.2 3.4 %collective-permute-start.21 = (bf16[8,2048]{1,0:T(8,128)(2,1)S(1)}, bf16[8,2048]{1,0:T(8,128)(2,1)S(1)}, u32[]{:S(2)}, u32[]{:S(2)}) collective-permute-start(bf16[8,2048]{1,0:T(8,128)(2,1)S(1)} %get-tuple-element.43), channel_id=1, source_target_pairs={{0,3},{1,2},{2,1},{3,0},{4,7},{5,6},{6,5},{7,4},{8,11},{9,10},{10,... | collective-permute-start | bytes 98312 | tf_op jit(solution)/shard_map/ppermute | solution.py:413
  (10 other events, 188.3 us)

commit v3 on v0

v3 whole, which is shorter than its diff:
```python
import functools
import math

import jax
import jax.numpy as jnp
from jax import lax
from jax.experimental import pallas as pl
from jax.experimental.pallas import tpu as pltpu
from jax.sharding import PartitionSpec as P

HD = 128
F32 = jnp.float32
BF16 = jnp.bfloat16
SMEM = pltpu.MemorySpace.SMEM
VMEM = pltpu.MemorySpace.VMEM
WHOLE = pl.BlockSpec(memory_space=VMEM)
UNREAD = pl.BlockSpec(memory_space=pl.ANY)
LONG = 5 * 10**10
TABLE = pl.BlockSpec(memory_space=SMEM)


def in_hbm(value):
    return pltpu.with_memory_space_constraint(value, pltpu.MemorySpace.HBM)


def params(size=4):
    return pltpu.CompilerParams(vmem_limit_bytes=size * 1024 * 1024)


def cost(flops=10**6):
    return pl.CostEstimate(flops=flops, bytes_accessed=flops // 1000, transcendentals=0)


def place_of(index, cols, sign=1):
    pairs, reps = cols
    dr, dp = divmod(index, pairs)
    pair = lax.rem(lax.axis_index("pair") + sign * dp + pairs, pairs)
    rep = lax.rem(lax.axis_index("rep") + sign * dr + reps, reps)
    return pair * reps + rep


def attend_kernel(
    cols, kvh, per_step, len_ref, query_ref, key_ref, value_ref, residual_ref, gain_ref, *refs
):
    pairs, reps = cols
    stream_ref = refs[0]
    piece_refs = refs[1 : 1 + pairs * reps]
    bias_ref, = refs[1 + pairs * reps :]
    step = pl.program_id(0)
    batches, rows, wide = query_ref.shape
    seqs = batches * rows
    cache = key_ref.shape[0] // seqs
    group = wide // (per_step * HD)
    each = group * seqs
    scale = 1.0 / math.sqrt(HD)

    @pl.when(step == 0)
    def _():
        seq = lax.rem(lax.broadcasted_iota(jnp.int32, bias_ref.shape, 1), seqs)
        place = lax.broadcasted_iota(jnp.int32, bias_ref.shape, 0)
        limit = jnp.zeros(bias_ref.shape, jnp.int32)
        for one in range(seqs):
            limit = jnp.where(seq == one, len_ref[one // rows, one % rows], limit)
        bias_ref[...] = jnp.where(place < limit, 0.0, -1e30)

    queries = jnp.concatenate([query_ref[b].astype(F32) for b in range(batches)], axis=0)
    residual = jnp.concatenate([residual_ref[b] for b in range(batches)], axis=0)
    lane_seq = lax.rem(lax.broadcasted_iota(jnp.int32, (cache, 2 * each), 1), seqs)
    row_seq = lax.rem(lax.broadcasted_iota(jnp.int32, (2 * each, cache), 0), seqs)
    mixed = []
    for low in range(0, per_step, 2):
        both = slice(low * HD, (low + 2) * HD)
        blocks = []
        for k in range(2):
            heads = range((low + k) * group, (low + k + 1) * group)
            stacked = jnp.concatenate([queries[:, h * HD : (h + 1) * HD] for h in heads], axis=0)
            empty = jnp.zeros_like(stacked)
            blocks.append(jnp.concatenate([empty, stacked] if k else [stacked, empty], axis=1))
        spread = jnp.concatenate(blocks, axis=0).astype(BF16)
        scores = None
        for one in range(0, seqs, 2):
            products = lax.dot_general(
                key_ref[one * cache : (one + 2) * cache, both],
                spread,
                (((1,), (1,)), ((), ())),
                preferred_element_type=F32,
            )
            mine = jnp.where(lane_seq == one, products[:cache], products[cache:])
            scores = mine if one == 0 else jnp.where(lane_seq >= one, mine, scores)
        scores = scores * scale + bias_ref[...]
        peak = jnp.max(scores, axis=0, keepdims=True)
        raised = jnp.exp(scores - peak)
        probs = jnp.transpose(raised / jnp.sum(raised, axis=0, keepdims=True))
        apart = [jnp.where(row_seq == one, probs, 0.0).astype(BF16) for one in range(seqs)]
        out = jnp.dot(
            jnp.concatenate(apart, axis=1), value_ref[:, both], preferred_element_type=F32
        )
        out = out.astype(BF16).astype(F32)
        mixed += [
            out[k * each + h * seqs : k * each + (h + 1) * seqs, k * HD : (k + 1) * HD]
            for k in range(2)
            for h in range(group)
        ]
    start = pl.multiple_of(step * wide, wide)
    stream_ref[:, pl.ds(start, wide)] = residual + jnp.concatenate(mixed, axis=1)

    @pl.when(step == kvh // per_step - 1)
    def _():
        stream = stream_ref[...]
        width = stream.shape[1] // (pairs * reps)
        factor = lax.rsqrt(jnp.mean(stream * stream, axis=-1, keepdims=True) + 1e-05)
        for index, piece_ref in enumerate(piece_refs):
            dr, dp = divmod(index, pairs)
            column = lax.rem(lax.axis_index("pair") + dp, pairs) * reps
            column = column + lax.rem(lax.axis_index("rep") + dr, reps)
            own = pl.ds(pl.multiple_of(column * width, width), width)
            piece_ref[...] = (stream_ref[:, own] * factor * gain_ref[:, own]).astype(BF16)


def attend(cols, cache_len, query, key_cache, value_cache, residual, norm_gain):
    batches, _, rows, depth = query.shape
    seqs = batches * rows
    cache, kv = key_cache.shape[3:]
    kvh = kv // HD
    heads_per_step = 4
    wide = depth // kvh * heads_per_step
    columns = cols[0] * cols[1]
    by_head = pl.BlockSpec((batches, rows, wide), lambda i: (0, 0, i))
    cached = pl.BlockSpec((seqs * cache, heads_per_step * HD), lambda i: (0, i))
    return pl.pallas_call(
        functools.partial(attend_kernel, cols, kvh, heads_per_step),
        grid=(kvh // heads_per_step,),
        out_shape=[jax.ShapeDtypeStruct((seqs, depth), F32)]
        + [jax.ShapeDtypeStruct((seqs, depth // columns), BF16)] * columns,
        in_specs=[
            pl.BlockSpec(memory_space=SMEM),
            by_head,
            cached,
            cached,
            by_head,
            pl.BlockSpec((1, depth), lambda i: (0, 0)),
        ],
        out_specs=[pl.BlockSpec((seqs, depth), lambda i: (0, 0))]
        + [pl.BlockSpec((seqs, depth // columns), lambda i: (0, 0))] * columns,
        scratch_shapes=[pltpu.VMEM((cache, 2 * depth // kvh // HD * seqs), F32)],
        compiler_params=params(8),
        cost_estimate=cost(10**11),
        name="attend",
    )(
        cache_len.reshape(batches, rows),
        in_hbm(query.reshape(batches, rows, depth)),
        in_hbm(key_cache.reshape(seqs * cache, kv)),
        in_hbm(value_cache.reshape(seqs * cache, kv)),
        in_hbm(residual.reshape(batches, rows, depth)),
        in_hbm(norm_gain.reshape(1, depth)),
    )


def pack_kernel(cols, batches, table_ref, *refs):
    columns = cols[0] * cols[1]
    pieces = [ref[...].astype(F32) for ref in refs[:columns]]
    seqs = pieces[0].shape[0]
    row = lax.broadcasted_iota(jnp.int32, pieces[0].shape, 0)
    groups = [place_of(slot, cols, -1) for slot in range(columns)]
    picked = []
    for index in range(columns):
        column = place_of(index, cols)
        value = jnp.zeros_like(pieces[0])
        for micro in range(batches):
            taken = jnp.zeros_like(pieces[0])
            for slot in range(columns):
                taken = jnp.where(table_ref[micro, groups[slot]] == column, pieces[slot], taken)
            value = jnp.where(row >= micro * (seqs // batches), taken, value)
        picked.append(value)
    refs[columns][...] = jnp.concatenate(picked, axis=0).astype(BF16)


def pack(cols, batches, table, pieces):
    seqs, depth = pieces[0].shape
    return pl.pallas_call(
        functools.partial(pack_kernel, cols, batches),
        out_shape=jax.ShapeDtypeStruct((seqs * len(pieces), depth), BF16),
        in_specs=[TABLE] + [WHOLE] * len(pieces),
        out_specs=WHOLE,
        compiler_params=params(),
        cost_estimate=cost(),
        name="pack",
    )(table, *pieces)


def project_into(held, weight_ref, keep_ref, send_refs):
    half = keep_ref.shape[0]
    each = send_refs[0].shape[0]
    width = keep_ref.shape[1]
    tile = math.gcd(width, 256)
    for low in range(0, width, tile):
        part = slice(low, low + tile)
        sums = jnp.dot(held, weight_ref[:, part], preferred_element_type=F32)
        keep_ref[:, part] = sums[:half]
        for cut, send_ref in enumerate(send_refs):
            low_row = half + cut * each
            send_ref[:, part] = sums[low_row : low_row + each].astype(BF16)


def project_kernel(columns, count, cuts, weight_ref, *refs):
    keep_ref, *send_refs = refs[-1 - cuts :]
    packs = [ref[...].astype(F32) for ref in refs[:count]]
    rows = packs[0].shape[0] // columns
    held = [p[i * rows : (i + 1) * rows] for i in range(columns) for p in packs]
    held = jnp.concatenate(held, axis=0).astype(BF16)
    project_into(held, weight_ref, keep_ref, send_refs)


def sums_of(rows, width, reps, cuts):
    half = rows // reps
    return [
        jax.ShapeDtypeStruct((half, width), F32),
        *[jax.ShapeDtypeStruct(((rows - half) // cuts, width), BF16)] * cuts,
    ]


def project(cols, name, packs, weight, after, cuts=1, flops=LONG, kept=()):
    pairs, reps = cols
    rows = packs[0].shape[0] * len(packs)
    return pl.pallas_call(
        functools.partial(project_kernel, pairs * reps, len(packs), cuts),
        out_shape=sums_of(rows, weight.shape[1], reps, cuts),
        in_specs=[WHOLE] * (1 + len(packs)) + [UNREAD] * len(after) + [WHOLE] * len(kept),
        out_specs=[WHOLE] * (1 + cuts),
        compiler_params=params(),
        cost_estimate=cost(flops),
        name=name,
    )(weight, *packs, *after, *kept)


def mark_kernel(*refs):
    refs[-1][...] = jnp.zeros(refs[-1].shape, F32)


def mark(name, after, kept):
    return pl.pallas_call(
        mark_kernel,
        out_shape=jax.ShapeDtypeStruct((8, 128), F32),
        in_specs=[UNREAD] * len(after) + [WHOLE] * len(kept),
        out_specs=WHOLE,
        compiler_params=params(),
        cost_estimate=cost(LONG),
        name=name,
    )(*after, *kept)


def hold_kernel(*refs):
    refs[-1][...] = refs[0][...]


def hold(name, value, after):
    return pl.pallas_call(
        hold_kernel,
        out_shape=jax.ShapeDtypeStruct(value.shape, value.dtype),
        in_specs=[WHOLE] + [UNREAD] * len(after),
        out_specs=WHOLE,
        compiler_params=params(),
        cost_estimate=cost(LONG),
        name=name,
    )(value, *after)


def join_kernel(pairs, counts, *refs):
    outs = refs[-pairs:]
    rows = outs[0].shape[1]
    start = 0
    for place, count in enumerate(counts):
        keep_ref, *came_refs = refs[start : start + 1 + count]
        start += 1 + count
        came = jnp.concatenate([ref[...].astype(F32) for ref in came_refs], axis=0)
        outs[0][place] = keep_ref[:rows] + came[:rows]
        for dp in range(1, pairs):
            part = slice(dp * rows, (dp + 1) * rows)
            outs[dp][place] = (keep_ref[part] + came[part]).astype(BF16)


def join(pairs, name, sums, after):
    total, width = sums[0][0].shape
    shape = (2, total // pairs, width)
    counts = [len(item) - 1 for item in sums]
    flat = [part for item in sums for part in item]
    return pl.pallas_call(
        functools.partial(join_kernel, pairs, counts),
        out_shape=[jax.ShapeDtypeStruct(shape, F32)]
        + [jax.ShapeDtypeStruct(shape, BF16)] * (pairs - 1),
        in_specs=[WHOLE] * len(flat) + [UNREAD] * len(after),
        out_specs=[WHOLE] * pairs,
        compiler_params=params(),
        cost_estimate=cost(),
        name=name,
    )(*flat, *after)


def act_kernel(count, own_ref, *refs):
    sums = own_ref[...]
    for ref in refs[:count]:
        sums = sums + ref[...].astype(F32)
    gate = sums[0]
    refs[-1][...] = (gate / (1.0 + jnp.exp(-gate)) * sums[1]).astype(BF16)


def activate(name, own, arrived, after, flops=10**6):
    return pl.pallas_call(
        functools.partial(act_kernel, len(arrived)),
        out_shape=jax.ShapeDtypeStruct(own.shape[1:], BF16),
        in_specs=[WHOLE] * (1 + len(arrived)) + [UNREAD] * len(after),
        out_specs=WHOLE,
        compiler_params=params(),
        cost_estimate=cost(flops),
        name=name,
    )(own, *arrived, *after)


def served_kernel(batches, rows, *refs):
    out_ref = refs[-1]
    start = lax.axis_index("ffn") * rows
    parts = [ref[...].astype(F32) for ref in refs[:-1]]
    seqs = batches * rows
    for micro in range(batches):
        low = micro * rows
        mine = [p[s + low : s + low + rows] for p in parts for s in range(0, p.shape[0], seqs)]
        mine = jnp.concatenate(mine, axis=0)
        out_ref[micro, 0] = pltpu.roll(mine, start, 0).astype(BF16)


def serve(batches, rows, hidden):
    count, width = hidden[0].shape
    return pl.pallas_call(
        functools.partial(served_kernel, batches, rows),
        out_shape=jax.ShapeDtypeStruct((batches, 1, count * len(hidden) // batches, width), BF16),
        in_specs=[WHOLE] * len(hidden),
        out_specs=WHOLE,
        compiler_params=params(),
        cost_estimate=cost(),
        name="serve",
    )(*hidden)


def down_kernel(cols, batches, rows, sizes, skip, table_ref, weight_ref, *refs):
    pairs, reps = cols
    columns = pairs * reps
    count = columns * len(sizes)
    held = jnp.concatenate([ref[...] for ref in refs[:count]], axis=0)
    share_refs = refs[count + skip : -1]
    sums_ref = refs[-1]
    depth = weight_ref.shape[1]
    tile = math.gcd(depth, 256)
    for low in range(0, depth, tile):
        part = slice(low, low + tile)
        sums_ref[:, part] = jnp.dot(held, weight_ref[:, part], preferred_element_type=F32)
    seqs = batches * rows
    row = lax.broadcasted_iota(jnp.int32, (seqs, depth), 0)
    places = []
    for index in range(columns):
        held_at = []
        for micro in range(batches):
            column = table_ref[micro, place_of(index, cols)]
            to_pair = lax.rem(column // reps - lax.axis_index("pair") + pairs, pairs)
            to_rep = lax.rem(lax.rem(column, reps) - lax.axis_index("rep") + reps, reps)
            held_at.append(to_rep * pairs + to_pair)
        places.append(held_at)
    first = 0
    shift = 0
    for size in sizes:
        for inner in range(size // seqs):
            blocks = []
            for held_at in places:
                value = jnp.zeros((seqs, depth), F32)
                for micro, place in enumerate(held_at):
                    base = pl.multiple_of(first + place * size + inner * seqs, seqs)
                    value = jnp.where(row >= micro * rows, sums_ref[pl.ds(base, seqs), :], value)
                blocks.append(value)
            same = [blocks[dr * pairs] for dr in range(reps)]
            other = [blocks[dr * pairs + dp] for dp in range(1, pairs) for dr in range(reps)]
            share_refs[2 * shift][...] = jnp.concatenate(same, axis=0).astype(BF16)
            share_refs[2 * shift + 1][...] = jnp.concatenate(other, axis=0).astype(BF16)
            shift += 1
        first += columns * size


def down(cols, name, batches, rows, table, blocks, weight, after):
    pairs, reps = cols
    depth = weight.shape[1]
    seqs = batches * rows
    sizes = [block[0].shape[0] for block in blocks]
    shifts = sum(sizes) // seqs
    flat = [part for block in blocks for part in block]
    same = jax.ShapeDtypeStruct((reps * seqs, depth), BF16)
    other = jax.ShapeDtypeStruct(((pairs - 1) * reps * seqs, depth), BF16)
    out = pl.pallas_call(
        functools.partial(down_kernel, cols, batches, rows, sizes, len(after)),
        out_shape=[same, other] * shifts,
        in_specs=[TABLE] + [WHOLE] * (1 + len(flat)) + [UNREAD] * len(after),
        out_specs=[WHOLE] * (2 * shifts),
        scratch_shapes=[pltpu.VMEM((sum(sizes) * pairs * reps, depth), F32)],
        compiler_params=params(8),
        cost_estimate=cost(LONG),
        name=name,
    )(table, weight, *flat, *after)
    return out[0::2], out[1::2]


def total_kernel(count, outs, cuts, *refs):
    sums = refs[0][...].astype(F32)
    for ref in refs[1:count]:
        sums = sums + ref[...].astype(F32)
    rows, width = refs[-1].shape
    for index, out_ref in enumerate(refs[-outs:]):
        row, column = divmod(index, cuts)
        part = sums[row * rows : (row + 1) * rows, column * width : (column + 1) * width]
        out_ref[...] = part.astype(BF16)


def total(name, seqs, parts, after, cuts):
    rows, depth = parts[0].shape
    outs = rows // seqs * cuts
    return pl.pallas_call(
        functools.partial(total_kernel, len(parts), outs, cuts),
        out_shape=[jax.ShapeDtypeStruct((seqs, depth // cuts), BF16)] * outs,
        in_specs=[WHOLE] * len(parts) + [UNREAD] * len(after),
        out_specs=[WHOLE] * outs,
        compiler_params=params(),
        cost_estimate=cost(LONG),
        name=name,
    )(*parts, *after)


def finish_kernel(cols, pieces, stream_ref, *refs):
    out_ref = refs[-1]
    batches, _, rows, depth = out_ref.shape
    width = depth // (cols[0] * cols[1])
    start = 0
    for index, count in enumerate(pieces):
        column = place_of(index, cols, -1)
        for piece in range(count):
            ref = refs[start + piece]
            low = column * width + piece * (width // count)
            own = pl.ds(pl.multiple_of(low, width // count), width // count)
            sums = stream_ref[:, own] + ref[...].astype(F32)
            for micro in range(batches):
                out_ref[micro, 0, :, own] = sums[micro * rows : (micro + 1) * rows]
        start += count


def finish(cols, batches, stream, changes):
    seqs, depth = stream.shape
    flat = [part for parts in changes for part in parts]
    return pl.pallas_call(
        functools.partial(finish_kernel, cols, [len(parts) for parts in changes]),
        out_shape=jax.ShapeDtypeStruct((batches, 1, seqs // batches, depth), F32),
        in_specs=[WHOLE] * (1 + len(flat)),
        out_specs=WHOLE,
        compiler_params=params(),
        cost_estimate=cost(),
        name="finish",
    )(stream, *flat)


def to_column(cols, value, dr, dp):
    pairs, reps = cols
    route = [
        (p * reps + r, (p + dp) % pairs * reps + (r + dr) % reps)
        for p in range(pairs)
        for r in range(reps)
    ]
    return lax.ppermute(value, ("pair", "rep"), route)


def turn(value, ffn, shift):
    return lax.ppermute(value, "ffn", [(i, (i + shift) % ffn) for i in range(ffn)])


def per_device(
    cols,
    ffn,
    residual,
    query,
    key_cache,
    value_cache,
    cache_len,
    partner_table,
    norm_gain,
    gate_weight,
    up_weight,
    down_weight,
):
    pairs, reps = cols
    batches, _, rows, _ = query.shape
    stream, *normed = attend(
        cols, cache_len, query, key_cache, value_cache, residual, norm_gain
    )
    half = ffn // 2

    def spread(parts):
        return [to_column(cols, part, 0, dp + 1) for dp, part in enumerate(parts)]

    def swap(sums):
        return [sums[0], *[to_column(cols, part, 1, 0) for part in sums[1:]]]

    def collect(hidden):
        block = [hidden] + [to_column(cols, hidden, 0, pairs - dp) for dp in range(1, pairs)]
        return block + [to_column(cols, item, 1, 0) for item in block]

    mine = pack(cols, batches, partner_table, [
        to_column(cols, piece, *divmod(index, pairs)) if index else piece
        for index, piece in enumerate(normed)
    ])
    packs = [mine] + [turn(mine, ffn, -s) for s in range(1, ffn)]
    near, far = packs[:half], packs[half:]
    gate_near = project(cols, "gate_near", near, gate_weight, [], kept=[up_weight])
    up_near = project(cols, "up_near", near, up_weight, [])
    here = mark("far_here", far, [gate_weight, up_weight])
    near_own, *near_sent = join(pairs, "join_near", (swap(gate_near), swap(up_near)), [here])
    near_came = spread(near_sent)
    gate_far = project(cols, "gate_far", far, gate_weight, [near_own], pairs, kept=[up_weight])
    up_far = project(cols, "up_far", far, up_weight, [gate_far[0]], pairs, 10**6)
    near_hidden = activate("activate_near", near_own, near_came, [])
    far_own, *far_sent = join(
        pairs, "join_far", (swap(gate_far), swap(up_far)), [near_hidden]
    )
    far_came = spread(far_sent)
    far_hidden = activate("activate_far", far_own, far_came, [])
    hiddens = [near_hidden, far_hidden]
    blocks = [collect(hidden) for hidden in hiddens]
    shares = down(cols, "down", batches, rows, partner_table, blocks, down_weight, [])
    totals = []
    for kind in (1, 0):
        gathered = [shares[kind][0]] + [turn(shares[kind][s], ffn, s) for s in range(1, ffn)]
        after = [part for parts in totals for part in parts[:1]]
        name = ("total_same", "total_other")[kind]
        totals.append(total(name, batches * rows, gathered, after, 2 - kind))
    other, same = totals
    changes = []
    for dr in range(reps):
        parts = same[2 * dr : 2 * dr + 2]
        changes.append([to_column(cols, part, dr, 0) if dr else part for part in parts])
        for dp in range(1, pairs):
            changes.append([to_column(cols, other[(dp - 1) * reps + dr], dr, dp)])
    served = serve(batches, rows, hiddens)
    updated = finish(cols, batches, stream, changes)
    return (updated, served)


def solution(mesh):
    sizes = dict(mesh.shape)
    cols = (sizes["pair"], sizes["rep"])
    rows = P(None, ("parts", "pair", "rep"), "ffn", None)
    caches = P(None, ("parts", "pair", "rep"), "ffn", None, None)
    placed = (
        rows,
        rows,
        caches,
        caches,
        P(None, ("parts", "pair", "rep"), "ffn"),
        P("parts", None),
        P(),
        P(("pair", "rep"), "ffn"),
        P(("pair", "rep"), "ffn"),
        P("ffn", ("pair", "rep")),
    )
    return jax.shard_map(
        functools.partial(per_device, cols, sizes["ffn"]),
        mesh=mesh,
        in_specs=placed,
        out_specs=(rows, P(None, ("parts", "pair", "rep"), None, "ffn")),
        check_vma=False,
    )
```

time: 400 us -> 71.6 us (0.18)
  other arithmetic: 98.5 us -> 0.01 us
  blocking collectives: 73.3 us -> 0 us
  local copies, waits for them, and re-layouts: 66.8 us -> 0.71 us
  waiting for transfers between devices: 84.3 us -> 23.7 us
  matrix products: 46.3 us -> 0 us
  Pallas kernels: 0 us -> 20.7 us
  between operations: 14.9 us -> 0.88 us
  starting transfers between devices: 14.3 us -> 25.3 us
    unnamed x2 -> x1, other arithmetic: 90.4 us -> 0.01 us
    psum x1 -> x0, waiting for transfers between devices: 77.5 us -> none  [layer_step(): summed = lax.psum(partial_value, ('pair', 'rep'))]
    dot_general x10 -> x0, matrix products: 46.3 us -> none  [the longest x2 25.4 us: layer_step(): jnp.einsum('bgrd,df->bgrf', lax.all_gather(routed, 'ffn', axis=2, tiled=T...]
    unnamed x1 -> x0, blocking collectives: 43.8 us -> none
    all_gather x2 -> x0, blocking collectives: 29.4 us -> none  [layer_step(): lax.all_gather(routed, 'ffn', axis=2, tiled=True)]
    unnamed x19 -> x18, local copies, waits for them, and re-layouts: 27.5 us -> 0.71 us
    ppermute x0 -> x30, starting transfers between devices: none -> 25.3 us  [the longest x9 13.7 us: turn(): lax.ppermute(value, 'ffn', [(i, (i + shift) % ffn) for i in range(ffn)])]
    ppermute x0 -> x30, waiting for transfers between devices: none -> 23.7 us  [the longest x21 14.5 us: to_column(): return lax.ppermute(value, ('pair', 'rep'), route)]
  transfers between devices with their start and end apart: 5 -> 30, of which waited for: 3 -> 15; matrix products, arithmetic and copies ran while one was open for 18% -> 0% of each run, Pallas kernels for 0% -> 16%
where the time goes in v3:
time: 71.6 us; the launch traced here: 71.4 us
  starting transfers between devices  25.3 us (35%)
  waiting for transfers between devices  23.7 us (33%)
  Pallas kernels  20.7 us (29%)
  between operations  0.88 us (1%)
    ppermute x21, waiting for transfers between devices, to_column(): return lax.ppermute(value, ('pair', 'rep'), route)  14.5 us
    ppermute x9, starting transfers between devices, turn(): lax.ppermute(value, 'ffn', [(i, (i + shift) % ffn) for i in range(ffn)])  13.7 us
    ppermute x21, starting transfers between devices, to_column(): return lax.ppermute(value, ('pair', 'rep'), route)  11.6 us
    pallas_call x4, Pallas kernels, project(): pl.pallas_call(functools.partial(project_kernel, pairs * reps, len(packs)...  10.5 us
    ppermute x9, waiting for transfers between devices, turn(): lax.ppermute(value, 'ffn', [(i, (i + shift) % ffn) for i in range(ffn)])  9.29 us
    pallas_call x1, Pallas kernels, attend(): pl.pallas_call(functools.partial(attend_kernel, cols, kvh, heads_per_step...  4.58 us
    pallas_call x1, Pallas kernels, down(): pl.pallas_call(functools.partial(down_kernel, cols, batches, rows, sizes,...  3.01 us
  transfers between devices with their start and end apart: 30, of which 15 were waited for; matrix products, arithmetic and copies ran while one was open for 0% of the time, Pallas kernels for 16%

profile of v3, /device:TPU:0, one launch (start us, length us, event | category | flops | bytes accessed | tf_op | source)
XLA Modules:
  0.0 71.4 jit_solution(11070920573234078794)
XLA Ops:
  1.3 4.6 %attend.1 = (f32[8,8192]{1,0:T(8,128)S(1)}, bf16[8,2048]{1,0:T(8,128)(2,1)S(1)}, bf16[8,2048]{1,0:T(8,128)(2,1)S(1)}, bf16[8,2048]{1,0:T(8,128)(2,1)S(1)}, bf16[8,2048]{1,0:T(8,128)(2,1)S(1)}) custom-call(s32[2,4]{1,0:T(2,128)S(1)} %bitcast.8, bf16[2,4,8192]{2,1,0:T(4,128)(2,1)} %bitcast.12, bf16[1024,1024]{1,0:T(8,128)(2,1)} %bitcast.9, ...), custom_call_target="tpu_custom_call" | custom-call | flops 99999997952 | bytes 100000000 | tf_op jit(solution)/shard_map/attend/pallas_call | solution.py:130
  5.9 3.0 %collective-permute-start = (bf16[8,2048]{1,0:T(8,128)(2,1)S(1)}, bf16[8,2048]{1,0:T(8,128)(2,1)S(1)}, u32[]{:S(2)}, u32[]{:S(2)}) collective-permute-start(bf16[8,2048]{1,0:T(8,128)(2,1)S(1)} %get-tuple-element.37), channel_id=1, source_target_pairs={{0,2},{1,3},{2,0},{3,1},{4,6},{5,7},{6,4},{7,5},{8,10},{9,11},{10,... | collective-permute-start | bytes 98312 | tf_op jit(solution)/shard_map/ppermute | solution.py:471
  9.1 1.7 %collective-permute-done.refs_1_ = bf16[8,2048]{1,0:T(8,128)(2,1)S(1)} collective-permute-done((bf16[8,2048]{1,0:T(8,128)(2,1)S(1)}, bf16[8,2048]{1,0:T(8,128)(2,1)S(1)}, u32[]{:S(2)}, u32[]{:S(2)}) %collective-permute-start) | collective-permute-done | bytes 32800 | tf_op jit(solution)/shard_map/ppermute | solution.py:471
  10.8 1.4 %collective-permute-done.2.refs_3_ = bf16[8,2048]{1,0:T(8,128)(2,1)S(1)} collective-permute-done((bf16[8,2048]{1,0:T(8,128)(2,1)S(1)}, bf16[8,2048]{1,0:T(8,128)(2,1)S(1)}, u32[]{:S(2)}, u32[]{:S(2)}) %collective-permute-start.2) | collective-permute-done | bytes 32800 | tf_op jit(solution)/shard_map/ppermute | solution.py:471
  13.0 3.6 %collective-permute-start.3 = (bf16[32,2048]{1,0:T(8,128)(2,1)S(1)}, bf16[32,2048]{1,0:T(8,128)(2,1)S(1)}, u32[]{:S(2)}, u32[]{:S(2)}) collective-permute-start(bf16[32,2048]{1,0:T(8,128)(2,1)S(1)} %pack.1.refs_0_), channel_id=1, source_target_pairs={{0,12},{4,0},{8,4},{12,8},{1,13},{5,1},{9,5},{13,9},{2,14},{6,2},{... | collective-permute-start | bytes 393224 | tf_op jit(solution)/shard_map/ppermute | solution.py:475
  16.6 1.0 %collective-permute-start.7 = (bf16[32,2048]{1,0:T(8,128)(2,1)S(1)}, bf16[32,2048]{1,0:T(8,128)(2,1)S(1)}, u32[]{:S(2)}, u32[]{:S(2)}) collective-permute-start(bf16[32,2048]{1,0:T(8,128)(2,1)S(1)} %pack.1.refs_0_), channel_id=1, source_target_pairs={{0,4},{4,8},{8,12},{12,0},{1,5},{5,9},{9,13},{13,1},{2,6},{6,10},{... | collective-permute-start | bytes 393224 | tf_op jit(solution)/shard_map/ppermute | solution.py:475
  17.6 2.9 %collective-permute-done.3.refs_1_ = bf16[32,2048]{1,0:T(8,128)(2,1)S(1)} collective-permute-done((bf16[32,2048]{1,0:T(8,128)(2,1)S(1)}, bf16[32,2048]{1,0:T(8,128)(2,1)S(1)}, u32[]{:S(2)}, u32[]{:S(2)}) %collective-permute-start.3) | collective-permute-done | bytes 131104 | tf_op jit(solution)/shard_map/ppermute | solution.py:475
  20.5 2.6 %up_near.1 = (f32[32,3584]{1,0:T(8,128)S(1)}, bf16[32,3584]{1,0:T(8,128)(2,1)S(1)}) custom-call(bf16[2048,3584]{1,0:T(8,128)(2,1)S(1)} %copy-done, bf16[32,2048]{1,0:T(8,128)(2,1)S(1)} %pack.1.refs_0_, bf16[32,2048]{1,0:T(8,128)(2,1)S(1)} %collective-permute-done.3.refs_1_), custom_call_target="tpu_custom_call" | custom-call | flops 49999998976 | bytes 50000000 | tf_op jit(solution)/shard_map/up_near/pallas_call | solution.py:225
  23.3 2.6 %gate_near.1 = (f32[32,3584]{1,0:T(8,128)S(1)}, bf16[32,3584]{1,0:T(8,128)(2,1)S(1)}) custom-call(bf16[2048,3584]{1,0:T(8,128)(2,1)S(1)} %bitcast.7, bf16[32,2048]{1,0:T(8,128)(2,1)S(1)} %pack.1.refs_0_, bf16[32,2048]{1,0:T(8,128)(2,1)S(1)} %collective-permute-done.3.refs_1_, bf16[2048,3584]{1,0:T(8,128)(2,1)S(1)} %copy-done), custom_call_target="tpu_custom_call" | custom-call | flops 49999998976 | bytes 50000000 | tf_op jit(solution)/shard_map/gate_near/pallas_call | solution.py:225
  26.5 2.3 %collective-permute-done.6.refs_0_ = bf16[32,2048]{1,0:T(8,128)(2,1)S(1)} collective-permute-done((bf16[32,2048]{1,0:T(8,128)(2,1)S(1)}, bf16[32,2048]{1,0:T(8,128)(2,1)S(1)}, u32[]{:S(2)}, u32[]{:S(2)}) %collective-permute-start.6) | collective-permute-done | bytes 131104 | tf_op jit(solution)/shard_map/ppermute | solution.py:475
  29.4 2.6 %gate_far.1 = (f32[32,3584]{1,0:T(8,128)S(1)}, bf16[16,3584]{1,0:T(8,128)(2,1)S(1)}, bf16[16,3584]{1,0:T(8,128)(2,1)S(1)}) custom-call(bf16[2048,3584]{1,0:T(8,128)(2,1)S(1)} %bitcast.7, bf16[32,2048]{1,0:T(8,128)(2,1)S(1)} %collective-permute-done.6.refs_0_, bf16[32,2048]{1,0:T(8,128)(2,1)S(1)} %collective-permute-done.7.refs_1_, ...), custom_call_target="tpu_custom_call" | custom-call | flops 49999998976 | bytes 50000000 | tf_op jit(solution)/shard_map/gate_far/pallas_call | solution.py:225
  32.1 2.6 %up_far.1 = (f32[32,3584]{1,0:T(8,128)S(1)}, bf16[16,3584]{1,0:T(8,128)(2,1)S(1)}, bf16[16,3584]{1,0:T(8,128)(2,1)S(1)}) custom-call(bf16[2048,3584]{1,0:T(8,128)(2,1)S(1)} %copy-done, bf16[32,2048]{1,0:T(8,128)(2,1)S(1)} %collective-permute-done.6.refs_0_, bf16[32,2048]{1,0:T(8,128)(2,1)S(1)} %collective-permute-done.7.refs_1_, ...), custom_call_target="tpu_custom_call" | custom-call | flops 1000000 | bytes 1000 | tf_op jit(solution)/shard_map/up_far/pallas_call | solution.py:225
  36.8 1.6 %collective-permute-start.16 = (bf16[2,16,3584]{2,1,0:T(8,128)(2,1)S(1)}, bf16[2,16,3584]{2,1,0:T(8,128)(2,1)S(1)}, u32[]{:S(2)}, u32[]{:S(2)}) collective-permute-start(bf16[2,16,3584]{2,1,0:T(8,128)(2,1)S(1)} %get-tuple-element.53), channel_id=1, source_target_pairs={{0,2},{1,3},{2,0},{3,1},{4,6},{5,7},{6,4},{7,5},{8,10},{9,11},{10,... | collective-permute-start | bytes 688136 | tf_op jit(solution)/shard_map/ppermute | solution.py:471
  38.9 6.4 %collective-permute-done.16.refs_0_ = bf16[2,16,3584]{2,1,0:T(8,128)(2,1)S(1)} collective-permute-done((bf16[2,16,3584]{2,1,0:T(8,128)(2,1)S(1)}, bf16[2,16,3584]{2,1,0:T(8,128)(2,1)S(1)}, u32[]{:S(2)}, u32[]{:S(2)}) %collective-permute-start.16) | collective-permute-done | bytes 229408 | tf_op jit(solution)/shard_map/ppermute | solution.py:471
  45.4 1.6 %collective-permute-start.17 = (bf16[16,3584]{1,0:T(8,128)(2,1)S(1)}, bf16[16,3584]{1,0:T(8,128)(2,1)S(1)}, u32[]{:S(2)}, u32[]{:S(2)}) collective-permute-start(bf16[16,3584]{1,0:T(8,128)(2,1)S(1)} %activate_far.1.refs_4_.refs_1_), channel_id=1, source_target_pairs={{0,2},{1,3},{2,0},{3,1},{4,6},{5,7},{6,4},{7,5},{8,10},{9,11},{10,... | collective-permute-start | bytes 344072 | tf_op jit(solution)/shard_map/ppermute | solution.py:471
  47.8 2.5 %collective-permute-done.17.refs_5_ = bf16[16,3584]{1,0:T(8,128)(2,1)S(1)} collective-permute-done((bf16[16,3584]{1,0:T(8,128)(2,1)S(1)}, bf16[16,3584]{1,0:T(8,128)(2,1)S(1)}, u32[]{:S(2)}, u32[]{:S(2)}) %collective-permute-start.17) | collective-permute-done | bytes 114720 | tf_op jit(solution)/shard_map/ppermute | solution.py:471
  50.3 1.3 %collective-permute-done.19.refs_7_ = bf16[16,3584]{1,0:T(8,128)(2,1)S(1)} collective-permute-done((bf16[16,3584]{1,0:T(8,128)(2,1)S(1)}, bf16[16,3584]{1,0:T(8,128)(2,1)S(1)}, u32[]{:S(2)}, u32[]{:S(2)}) %collective-permute-start.19) | collective-permute-done | bytes 114720 | tf_op jit(solution)/shard_map/ppermute | solution.py:471
  51.6 3.0 %down.1 = (bf16[16,2048]{1,0:T(8,128)(2,1)S(1)}, bf16[16,2048]{1,0:T(8,128)(2,1)S(1)}, bf16[16,2048]{1,0:T(8,128)(2,1)S(1)}, bf16[16,2048]{1,0:T(8,128)(2,1)S(1)...) custom-call(s32[2,4]{1,0:T(2,128)S(1)} %copy-done.2, ...), custom_call_target="tpu_custom_call" | custom-call | flops 49999998976 | bytes 50000000 | tf_op jit(solution)/shard_map/down/pallas_call | solution.py:395
  55.2 3.6 %collective-permute-start.24 = (bf16[16,2048]{1,0:T(8,128)(2,1)S(1)}, bf16[16,2048]{1,0:T(8,128)(2,1)S(1)}, u32[]{:S(2)}, u32[]{:S(2)}) collective-permute-start(bf16[16,2048]{1,0:T(8,128)(2,1)S(1)} %get-tuple-element.60), channel_id=1, source_target_pairs={{0,8},{4,12},{8,0},{12,4},{1,9},{5,13},{9,1},{13,5},{2,10},{6,14},... | collective-permute-start | bytes 196616 | tf_op jit(solution)/shard_map/ppermute | solution.py:475
  58.9 1.2 %collective-permute-start.25 = (bf16[16,2048]{1,0:T(8,128)(2,1)S(1)}, bf16[16,2048]{1,0:T(8,128)(2,1)S(1)}, u32[]{:S(2)}, u32[]{:S(2)}) collective-permute-start(bf16[16,2048]{1,0:T(8,128)(2,1)S(1)} %get-tuple-element.61), channel_id=1, source_target_pairs={{0,12},{4,0},{8,4},{12,8},{1,13},{5,1},{9,5},{13,9},{2,14},{6,2},{... | collective-permute-start | bytes 196616 | tf_op jit(solution)/shard_map/ppermute | solution.py:475
  61.1 2.8 %collective-permute-start.22 = (bf16[16,2048]{1,0:T(8,128)(2,1)S(1)}, bf16[16,2048]{1,0:T(8,128)(2,1)S(1)}, u32[]{:S(2)}, u32[]{:S(2)}) collective-permute-start(bf16[16,2048]{1,0:T(8,128)(2,1)S(1)} %get-tuple-element.57), channel_id=1, source_target_pairs={{0,12},{4,0},{8,4},{12,8},{1,13},{5,1},{9,5},{13,9},{2,14},{6,2},{... | collective-permute-start | bytes 196616 | tf_op jit(solution)/shard_map/ppermute | solution.py:475
  64.2 1.4 %collective-permute-start.26 = (bf16[8,2048]{1,0:T(8,128)(2,1)S(1)}, bf16[8,2048]{1,0:T(8,128)(2,1)S(1)}, u32[]{:S(2)}, u32[]{:S(2)}) collective-permute-start(bf16[8,2048]{1,0:T(8,128)(2,1)S(1)} %get-tuple-element.62.refs_4_), channel_id=1, source_target_pairs={{0,2},{1,3},{2,0},{3,1},{4,6},{5,7},{6,4},{7,5},{8,10},{9,11},{10,... | collective-permute-start | bytes 98312 | tf_op jit(solution)/shard_map/ppermute | solution.py:471
  65.5 1.2 %collective-permute-done.20.refs_1_ = bf16[16,2048]{1,0:T(8,128)(2,1)S(1)} collective-permute-done((bf16[16,2048]{1,0:T(8,128)(2,1)S(1)}, bf16[16,2048]{1,0:T(8,128)(2,1)S(1)}, u32[]{:S(2)}, u32[]{:S(2)}) %collective-permute-start.20) | collective-permute-done | bytes 65568 | tf_op jit(solution)/shard_map/ppermute | solution.py:475
  66.7 2.5 %collective-permute-done.21.refs_2_ = bf16[16,2048]{1,0:T(8,128)(2,1)S(1)} collective-permute-done((bf16[16,2048]{1,0:T(8,128)(2,1)S(1)}, bf16[16,2048]{1,0:T(8,128)(2,1)S(1)}, u32[]{:S(2)}, u32[]{:S(2)}) %collective-permute-start.21) | collective-permute-done | bytes 65568 | tf_op jit(solution)/shard_map/ppermute | solution.py:475
  (71 shorter events, 10.3 us)
Async XLA Ops:
  5.9 4.9 %collective-permute-start = (bf16[8,2048]{1,0:T(8,128)(2,1)S(1)}, bf16[8,2048]{1,0:T(8,128)(2,1)S(1)}, u32[]{:S(2)}, u32[]{:S(2)}) collective-permute-start(bf16[8,2048]{1,0:T(8,128)(2,1)S(1)} %get-tuple-element.37), channel_id=1, source_target_pairs={{0,2},{1,3},{2,0},{3,1},{4,6},{5,7},{6,4},{7,5},{8,10},{9,11},{10,... | collective-permute-start | bytes 98312 | tf_op jit(solution)/shard_map/ppermute | solution.py:471
  8.9 1.9 %collective-permute-start.1 = (bf16[8,2048]{1,0:T(8,128)(2,1)S(1)}, bf16[8,2048]{1,0:T(8,128)(2,1)S(1)}, u32[]{:S(2)}, u32[]{:S(2)}) collective-permute-start(bf16[8,2048]{1,0:T(8,128)(2,1)S(1)} %get-tuple-element.38), channel_id=1, source_target_pairs={{0,1},{1,0},{2,3},{3,2},{4,5},{5,4},{6,7},{7,6},{8,9},{9,8},{10,11... | collective-permute-start | bytes 98312 | tf_op jit(solution)/shard_map/ppermute | solution.py:471
  8.9 3.3 %collective-permute-start.2 = (bf16[8,2048]{1,0:T(8,128)(2,1)S(1)}, bf16[8,2048]{1,0:T(8,128)(2,1)S(1)}, u32[]{:S(2)}, u32[]{:S(2)}) collective-permute-start(bf16[8,2048]{1,0:T(8,128)(2,1)S(1)} %get-tuple-element.39), channel_id=1, source_target_pairs={{0,3},{1,2},{2,1},{3,0},{4,7},{5,6},{6,5},{7,4},{8,11},{9,10},{10,... | collective-permute-start | bytes 98312 | tf_op jit(solution)/shard_map/ppermute | solution.py:471
  13.0 7.5 %collective-permute-start.3 = (bf16[32,2048]{1,0:T(8,128)(2,1)S(1)}, bf16[32,2048]{1,0:T(8,128)(2,1)S(1)}, u32[]{:S(2)}, u32[]{:S(2)}) collective-permute-start(bf16[32,2048]{1,0:T(8,128)(2,1)S(1)} %pack.1.refs_0_), channel_id=1, source_target_pairs={{0,12},{4,0},{8,4},{12,8},{1,13},{5,1},{9,5},{13,9},{2,14},{6,2},{... | collective-permute-start | bytes 393224 | tf_op jit(solution)/shard_map/ppermute | solution.py:475
  16.6 12.1 %collective-permute-start.6 = (bf16[32,2048]{1,0:T(8,128)(2,1)S(1)}, bf16[32,2048]{1,0:T(8,128)(2,1)S(1)}, u32[]{:S(2)}, u32[]{:S(2)}) collective-permute-start(bf16[32,2048]{1,0:T(8,128)(2,1)S(1)} %pack.1.refs_0_), channel_id=1, source_target_pairs={{0,8},{4,12},{8,0},{12,4},{1,9},{5,13},{9,1},{13,5},{2,10},{6,14},... | collective-permute-start | bytes 393224 | tf_op jit(solution)/shard_map/ppermute | solution.py:475
  16.6 12.1 %collective-permute-start.7 = (bf16[32,2048]{1,0:T(8,128)(2,1)S(1)}, bf16[32,2048]{1,0:T(8,128)(2,1)S(1)}, u32[]{:S(2)}, u32[]{:S(2)}) collective-permute-start(bf16[32,2048]{1,0:T(8,128)(2,1)S(1)} %pack.1.refs_0_), channel_id=1, source_target_pairs={{0,4},{4,8},{8,12},{12,0},{1,5},{5,9},{9,13},{13,1},{2,6},{6,10},{... | collective-permute-start | bytes 393224 | tf_op jit(solution)/shard_map/ppermute | solution.py:475
  23.2 5.6 %collective-permute-start.5 = (bf16[32,3584]{1,0:T(8,128)(2,1)S(1)}, bf16[32,3584]{1,0:T(8,128)(2,1)S(1)}, u32[]{:S(2)}, u32[]{:S(2)}) collective-permute-start(bf16[32,3584]{1,0:T(8,128)(2,1)S(1)} %get-tuple-element.43), channel_id=1, source_target_pairs={{0,1},{1,0},{2,3},{3,2},{4,5},{5,4},{6,7},{7,6},{8,9},{9,8},{10,11... | collective-permute-start | bytes 688136 | tf_op jit(solution)/shard_map/ppermute | solution.py:471
  25.9 2.9 %collective-permute-start.4 = (bf16[32,3584]{1,0:T(8,128)(2,1)S(1)}, bf16[32,3584]{1,0:T(8,128)(2,1)S(1)}, u32[]{:S(2)}, u32[]{:S(2)}) collective-permute-start(bf16[32,3584]{1,0:T(8,128)(2,1)S(1)} %get-tuple-element.41), channel_id=1, source_target_pairs={{0,1},{1,0},{2,3},{3,2},{4,5},{5,4},{6,7},{7,6},{8,9},{9,8},{10,11... | collective-permute-start | bytes 688136 | tf_op jit(solution)/shard_map/ppermute | solution.py:471
  28.9 7.2 %collective-permute-start.8 = (bf16[2,16,3584]{2,1,0:T(8,128)(2,1)S(1)}, bf16[2,16,3584]{2,1,0:T(8,128)(2,1)S(1)}, u32[]{:S(2)}, u32[]{:S(2)}) collective-permute-start(bf16[2,16,3584]{2,1,0:T(8,128)(2,1)S(1)} %get-tuple-element.45), channel_id=1, source_target_pairs={{0,2},{1,3},{2,0},{3,1},{4,6},{5,7},{6,4},{7,5},{8,10},{9,11},{10,... | collective-permute-start | bytes 688136 | tf_op jit(solution)/shard_map/ppermute | solution.py:471
  34.7 1.5 %collective-permute-start.14 = (bf16[16,3584]{1,0:T(8,128)(2,1)S(1)}, bf16[16,3584]{1,0:T(8,128)(2,1)S(1)}, u32[]{:S(2)}, u32[]{:S(2)}) collective-permute-start(bf16[16,3584]{1,0:T(8,128)(2,1)S(1)} %get-tuple-element.50), channel_id=1, source_target_pairs={{0,1},{1,0},{2,3},{3,2},{4,5},{5,4},{6,7},{7,6},{8,9},{9,8},{10,11... | collective-permute-start | bytes 344072 | tf_op jit(solution)/shard_map/ppermute | solution.py:471
  36.8 8.5 %collective-permute-start.16 = (bf16[2,16,3584]{2,1,0:T(8,128)(2,1)S(1)}, bf16[2,16,3584]{2,1,0:T(8,128)(2,1)S(1)}, u32[]{:S(2)}, u32[]{:S(2)}) collective-permute-start(bf16[2,16,3584]{2,1,0:T(8,128)(2,1)S(1)} %get-tuple-element.53), channel_id=1, source_target_pairs={{0,2},{1,3},{2,0},{3,1},{4,6},{5,7},{6,4},{7,5},{8,10},{9,11},{10,... | collective-permute-start | bytes 688136 | tf_op jit(solution)/shard_map/ppermute | solution.py:471
  38.5 8.8 %collective-permute-start.9 = (bf16[16,3584]{1,0:T(8,128)(2,1)S(1)}, bf16[16,3584]{1,0:T(8,128)(2,1)S(1)}, u32[]{:S(2)}, u32[]{:S(2)}) collective-permute-start(bf16[16,3584]{1,0:T(8,128)(2,1)S(1)} %activate_near.1.refs_6_.refs_0_), channel_id=1, source_target_pairs={{0,2},{1,3},{2,0},{3,1},{4,6},{5,7},{6,4},{7,5},{8,10},{9,11},{10,... | collective-permute-start | bytes 344072 | tf_op jit(solution)/shard_map/ppermute | solution.py:471
  45.4 4.9 %collective-permute-start.17 = (bf16[16,3584]{1,0:T(8,128)(2,1)S(1)}, bf16[16,3584]{1,0:T(8,128)(2,1)S(1)}, u32[]{:S(2)}, u32[]{:S(2)}) collective-permute-start(bf16[16,3584]{1,0:T(8,128)(2,1)S(1)} %activate_far.1.refs_4_.refs_1_), channel_id=1, source_target_pairs={{0,2},{1,3},{2,0},{3,1},{4,6},{5,7},{6,4},{7,5},{8,10},{9,11},{10,... | collective-permute-start | bytes 344072 | tf_op jit(solution)/shard_map/ppermute | solution.py:471
  47.1 3.2 %collective-permute-start.10 = (bf16[16,3584]{1,0:T(8,128)(2,1)S(1)}, bf16[16,3584]{1,0:T(8,128)(2,1)S(1)}, u32[]{:S(2)}, u32[]{:S(2)}) collective-permute-start(bf16[16,3584]{1,0:T(8,128)(2,1)S(1)} %activate_near.1.refs_6_.refs_0_), channel_id=1, source_target_pairs={{0,1},{1,0},{2,3},{3,2},{4,5},{5,4},{6,7},{7,6},{8,9},{9,8},{10,11... | collective-permute-start | bytes 344072 | tf_op jit(solution)/shard_map/ppermute | solution.py:471
  47.3 3.0 %collective-permute-start.11 = (bf16[16,3584]{1,0:T(8,128)(2,1)S(1)}, bf16[16,3584]{1,0:T(8,128)(2,1)S(1)}, u32[]{:S(2)}, u32[]{:S(2)}) collective-permute-start(bf16[16,3584]{1,0:T(8,128)(2,1)S(1)} %collective-permute-done.9.refs_1_), channel_id=1, source_target_pairs={{0,1},{1,0},{2,3},{3,2},{4,5},{5,4},{6,7},{7,6},{8,9},{9,8},{10,11... | collective-permute-start | bytes 344072 | tf_op jit(solution)/shard_map/ppermute | solution.py:471
  47.6 2.7 %collective-permute-start.18 = (bf16[16,3584]{1,0:T(8,128)(2,1)S(1)}, bf16[16,3584]{1,0:T(8,128)(2,1)S(1)}, u32[]{:S(2)}, u32[]{:S(2)}) collective-permute-start(bf16[16,3584]{1,0:T(8,128)(2,1)S(1)} %activate_far.1.refs_4_.refs_1_), channel_id=1, source_target_pairs={{0,1},{1,0},{2,3},{3,2},{4,5},{5,4},{6,7},{7,6},{8,9},{9,8},{10,11... | collective-permute-start | bytes 344072 | tf_op jit(solution)/shard_map/ppermute | solution.py:471
  54.6 6.5 %collective-permute-start.23 = (bf16[16,2048]{1,0:T(8,128)(2,1)S(1)}, bf16[16,2048]{1,0:T(8,128)(2,1)S(1)}, u32[]{:S(2)}, u32[]{:S(2)}) collective-permute-start(bf16[16,2048]{1,0:T(8,128)(2,1)S(1)} %get-tuple-element.59), channel_id=1, source_target_pairs={{0,4},{4,8},{8,12},{12,0},{1,5},{5,9},{9,13},{13,1},{2,6},{6,10},{... | collective-permute-start | bytes 196616 | tf_op jit(solution)/shard_map/ppermute | solution.py:475
  55.2 8.7 %collective-permute-start.24 = (bf16[16,2048]{1,0:T(8,128)(2,1)S(1)}, bf16[16,2048]{1,0:T(8,128)(2,1)S(1)}, u32[]{:S(2)}, u32[]{:S(2)}) collective-permute-start(bf16[16,2048]{1,0:T(8,128)(2,1)S(1)} %get-tuple-element.60), channel_id=1, source_target_pairs={{0,8},{4,12},{8,0},{12,4},{1,9},{5,13},{9,1},{13,5},{2,10},{6,14},... | collective-permute-start | bytes 196616 | tf_op jit(solution)/shard_map/ppermute | solution.py:475
  58.9 5.2 %collective-permute-start.25 = (bf16[16,2048]{1,0:T(8,128)(2,1)S(1)}, bf16[16,2048]{1,0:T(8,128)(2,1)S(1)}, u32[]{:S(2)}, u32[]{:S(2)}) collective-permute-start(bf16[16,2048]{1,0:T(8,128)(2,1)S(1)} %get-tuple-element.61), channel_id=1, source_target_pairs={{0,12},{4,0},{8,4},{12,8},{1,13},{5,1},{9,5},{13,9},{2,14},{6,2},{... | collective-permute-start | bytes 196616 | tf_op jit(solution)/shard_map/ppermute | solution.py:475
  60.1 6.7 %collective-permute-start.20 = (bf16[16,2048]{1,0:T(8,128)(2,1)S(1)}, bf16[16,2048]{1,0:T(8,128)(2,1)S(1)}, u32[]{:S(2)}, u32[]{:S(2)}) collective-permute-start(bf16[16,2048]{1,0:T(8,128)(2,1)S(1)} %get-tuple-element.55), channel_id=1, source_target_pairs={{0,4},{4,8},{8,12},{12,0},{1,5},{5,9},{9,13},{13,1},{2,6},{6,10},{... | collective-permute-start | bytes 196616 | tf_op jit(solution)/shard_map/ppermute | solution.py:475
  60.9 8.3 %collective-permute-start.21 = (bf16[16,2048]{1,0:T(8,128)(2,1)S(1)}, bf16[16,2048]{1,0:T(8,128)(2,1)S(1)}, u32[]{:S(2)}, u32[]{:S(2)}) collective-permute-start(bf16[16,2048]{1,0:T(8,128)(2,1)S(1)} %get-tuple-element.56), channel_id=1, source_target_pairs={{0,8},{4,12},{8,0},{12,4},{1,9},{5,13},{9,1},{13,5},{2,10},{6,14},... | collective-permute-start | bytes 196616 | tf_op jit(solution)/shard_map/ppermute | solution.py:475
  61.1 8.1 %collective-permute-start.22 = (bf16[16,2048]{1,0:T(8,128)(2,1)S(1)}, bf16[16,2048]{1,0:T(8,128)(2,1)S(1)}, u32[]{:S(2)}, u32[]{:S(2)}) collective-permute-start(bf16[16,2048]{1,0:T(8,128)(2,1)S(1)} %get-tuple-element.57), channel_id=1, source_target_pairs={{0,12},{4,0},{8,4},{12,8},{1,13},{5,1},{9,5},{13,9},{2,14},{6,2},{... | collective-permute-start | bytes 196616 | tf_op jit(solution)/shard_map/ppermute | solution.py:475
  64.2 6.5 %collective-permute-start.26 = (bf16[8,2048]{1,0:T(8,128)(2,1)S(1)}, bf16[8,2048]{1,0:T(8,128)(2,1)S(1)}, u32[]{:S(2)}, u32[]{:S(2)}) collective-permute-start(bf16[8,2048]{1,0:T(8,128)(2,1)S(1)} %get-tuple-element.62.refs_4_), channel_id=1, source_target_pairs={{0,2},{1,3},{2,0},{3,1},{4,6},{5,7},{6,4},{7,5},{8,10},{9,11},{10,... | collective-permute-start | bytes 98312 | tf_op jit(solution)/shard_map/ppermute | solution.py:471
  65.5 5.2 %collective-permute-start.29 = (bf16[8,2048]{1,0:T(8,128)(2,1)S(1)}, bf16[8,2048]{1,0:T(8,128)(2,1)S(1)}, u32[]{:S(2)}, u32[]{:S(2)}) collective-permute-start(bf16[8,2048]{1,0:T(8,128)(2,1)S(1)} %get-tuple-element.67), channel_id=1, source_target_pairs={{0,3},{1,2},{2,1},{3,0},{4,7},{5,6},{6,5},{7,4},{8,11},{9,10},{10,... | collective-permute-start | bytes 98312 | tf_op jit(solution)/shard_map/ppermute | solution.py:471
  (15 other events, 120.1 us)

commit v4 on v3

--- a/solution.py
+++ b/solution.py
@@ -58,9 +58,13 @@
     def _():
         seq = lax.rem(lax.broadcasted_iota(jnp.int32, bias_ref.shape, 1), seqs)
         place = lax.broadcasted_iota(jnp.int32, bias_ref.shape, 0)
-        limit = jnp.zeros(bias_ref.shape, jnp.int32)
+        place = place.astype(F32)
+        limit = jnp.zeros(bias_ref.shape, F32)
         for one in range(seqs):
-            limit = jnp.where(seq == one, len_ref[one // rows, one % rows], limit)
+            lengths = len_ref[one // rows].astype(F32)
+            here = lax.broadcasted_iota(jnp.int32, lengths.shape, 1) == one % rows
+            length = jnp.sum(jnp.where(here, lengths, 0.0), axis=1, keepdims=True)
+            limit = jnp.where(seq == one, length, limit)
         bias_ref[...] = jnp.where(place < limit, 0.0, -1e30)
 
     queries = jnp.concatenate([query_ref[b].astype(F32) for b in range(batches)], axis=0)
@@ -133,7 +137,7 @@
         out_shape=[jax.ShapeDtypeStruct((seqs, depth), F32)]
         + [jax.ShapeDtypeStruct((seqs, depth // columns), BF16)] * columns,
         in_specs=[
-            pl.BlockSpec(memory_space=SMEM),
+            pl.BlockSpec(cache_len.shape, lambda i: (0, 0, 0)),
             by_head,
             cached,
             cached,
@@ -147,7 +151,7 @@
         cost_estimate=cost(10**11),
         name="attend",
     )(
-        cache_len.reshape(batches, rows),
+        in_hbm(cache_len),
         in_hbm(query.reshape(batches, rows, depth)),
         in_hbm(key_cache.reshape(seqs * cache, kv)),
         in_hbm(value_cache.reshape(seqs * cache, kv)),
@@ -165,12 +169,12 @@
     picked = []
     for index in range(columns):
         column = place_of(index, cols)
-        value = jnp.zeros_like(pieces[0])
+        value = None
         for micro in range(batches):
-            taken = jnp.zeros_like(pieces[0])
-            for slot in range(columns):
+            taken = pieces[0]
+            for slot in range(1, columns):
                 taken = jnp.where(table_ref[micro, groups[slot]] == column, pieces[slot], taken)
-            value = jnp.where(row >= micro * (seqs // batches), taken, value)
+            value = jnp.where(row >= micro * (seqs // batches), taken, value) if micro else taken
         picked.append(value)
     refs[columns][...] = jnp.concatenate(picked, axis=0).astype(BF16)
 
@@ -188,49 +192,50 @@
     )(table, *pieces)
 
 
-def project_into(held, weight_ref, keep_ref, send_refs):
-    half = keep_ref.shape[0]
-    each = send_refs[0].shape[0]
-    width = keep_ref.shape[1]
+def gate_up_kernel(columns, count, cuts, start, gate_ref, up_ref, *refs):
+    keep_ref, *send_refs = refs[-1 - cuts :]
+    if count > 1:
+        packs = [ref[...].astype(F32) for ref in refs[:count]]
+        rows = packs[0].shape[0] // columns
+        held = [p[i * rows : (i + 1) * rows] for i in range(columns) for p in packs]
+        refs[-2 - cuts][...] = jnp.concatenate(held, axis=0).astype(BF16)
+        held = refs[-2 - cuts][...]
+    else:
+        held = refs[0][...]
+    half, width = keep_ref.shape[1:]
+    each = send_refs[0].shape[1]
     tile = math.gcd(width, 256)
-    for low in range(0, width, tile):
-        part = slice(low, low + tile)
-        sums = jnp.dot(held, weight_ref[:, part], preferred_element_type=F32)
-        keep_ref[:, part] = sums[:half]
-        for cut, send_ref in enumerate(send_refs):
-            low_row = half + cut * each
-            send_ref[:, part] = sums[low_row : low_row + each].astype(BF16)
-
-
-def project_kernel(columns, count, cuts, weight_ref, *refs):
-    keep_ref, *send_refs = refs[-1 - cuts :]
-    packs = [ref[...].astype(F32) for ref in refs[:count]]
-    rows = packs[0].shape[0] // columns
-    held = [p[i * rows : (i + 1) * rows] for i in range(columns) for p in packs]
-    held = jnp.concatenate(held, axis=0).astype(BF16)
-    project_into(held, weight_ref, keep_ref, send_refs)
-
-
-def sums_of(rows, width, reps, cuts):
-    half = rows // reps
-    return [
-        jax.ShapeDtypeStruct((half, width), F32),
-        *[jax.ShapeDtypeStruct(((rows - half) // cuts, width), BF16)] * cuts,
-    ]
-
-
-def project(cols, name, packs, weight, after, cuts=1, flops=LONG, kept=()):
+    for place, weight_ref in enumerate((gate_ref, up_ref)):
+        for low in range(0, width, tile):
+            part = slice(low, low + tile)
+            weight = weight_ref[:, start + low : start + low + tile]
+            sums = jnp.dot(held, weight, preferred_element_type=F32)
+            keep_ref[place, :, part] = sums[:half]
+            for cut, send_ref in enumerate(send_refs):
+                low_row = half + cut * each
+                send_ref[place, :, part] = sums[low_row : low_row + each].astype(BF16)
+
+
+def gate_up(cols, name, packs, weights, span, after, cuts, flops):
     pairs, reps = cols
     rows = packs[0].shape[0] * len(packs)
-    return pl.pallas_call(
-        functools.partial(project_kernel, pairs * reps, len(packs), cuts),
-        out_shape=sums_of(rows, weight.shape[1], reps, cuts),
-        in_specs=[WHOLE] * (1 + len(packs)) + [UNREAD] * len(after) + [WHOLE] * len(kept),
-        out_specs=[WHOLE] * (1 + cuts),
+    half = rows // reps
+    start, stop = span
+    width = stop - start
+    hand_on = [jax.ShapeDtypeStruct((rows, packs[0].shape[1]), BF16)] * (len(packs) > 1)
+    return pl.pallas_call(
+        functools.partial(gate_up_kernel, pairs * reps, len(packs), cuts, start),
+        out_shape=hand_on
+        + [
+            jax.ShapeDtypeStruct((2, half, width), F32),
+            *[jax.ShapeDtypeStruct((2, (rows - half) // cuts, width), BF16)] * cuts,
+        ],
+        in_specs=[WHOLE] * (2 + len(packs)) + [UNREAD] * len(after),
+        out_specs=[WHOLE] * (len(hand_on) + 1 + cuts),
         compiler_params=params(),
         cost_estimate=cost(flops),
         name=name,
-    )(weight, *packs, *after, *kept)
+    )(*weights, *packs, *after)
 
 
 def mark_kernel(*refs):
@@ -269,19 +274,22 @@
     outs = refs[-pairs:]
     rows = outs[0].shape[1]
     start = 0
-    for place, count in enumerate(counts):
+    low = 0
+    for count in counts:
         keep_ref, *came_refs = refs[start : start + 1 + count]
         start += 1 + count
-        came = jnp.concatenate([ref[...].astype(F32) for ref in came_refs], axis=0)
-        outs[0][place] = keep_ref[:rows] + came[:rows]
+        came = jnp.concatenate([ref[...].astype(F32) for ref in came_refs], axis=1)
+        part = slice(low, low + keep_ref.shape[2])
+        low += keep_ref.shape[2]
+        outs[0][:, :, part] = keep_ref[:, :rows] + came[:, :rows]
         for dp in range(1, pairs):
-            part = slice(dp * rows, (dp + 1) * rows)
-            outs[dp][place] = (keep_ref[part] + came[part]).astype(BF16)
+            block = slice(dp * rows, (dp + 1) * rows)
+            outs[dp][:, :, part] = (keep_ref[:, block] + came[:, block]).astype(BF16)
 
 
 def join(pairs, name, sums, after):
-    total, width = sums[0][0].shape
-    shape = (2, total // pairs, width)
+    width = sum(item[0].shape[2] for item in sums)
+    shape = (2, sums[0][0].shape[1] // pairs, width)
     counts = [len(item) - 1 for item in sums]
     flat = [part for item in sums for part in item]
     return pl.pallas_call(
@@ -316,36 +324,51 @@
     )(own, *arrived, *after)
 
 
-def served_kernel(batches, rows, *refs):
+def served_kernel(batches, rows, counts, *refs):
     out_ref = refs[-1]
-    start = lax.axis_index("ffn") * rows
-    parts = [ref[...].astype(F32) for ref in refs[:-1]]
+    turned = lax.axis_index("ffn") * rows
     seqs = batches * rows
+    groups = []
+    start = 0
+    for count in counts:
+        parts = [ref[...].astype(F32) for ref in refs[start : start + count]]
+        groups.append(jnp.concatenate(parts, axis=1))
+        start += count
     for micro in range(batches):
         low = micro * rows
-        mine = [p[s + low : s + low + rows] for p in parts for s in range(0, p.shape[0], seqs)]
+        mine = [p[s + low : s + low + rows] for p in groups for s in range(0, p.shape[0], seqs)]
         mine = jnp.concatenate(mine, axis=0)
-        out_ref[micro, 0] = pltpu.roll(mine, start, 0).astype(BF16)
+        out_ref[micro, 0] = pltpu.roll(mine, turned, 0).astype(BF16)
 
 
 def serve(batches, rows, hidden):
-    count, width = hidden[0].shape
-    return pl.pallas_call(
-        functools.partial(served_kernel, batches, rows),
-        out_shape=jax.ShapeDtypeStruct((batches, 1, count * len(hidden) // batches, width), BF16),
-        in_specs=[WHOLE] * len(hidden),
+    flat = [part for group in hidden for part in group]
+    width = sum(part.shape[1] for part in hidden[0])
+    total_rows = sum(group[0].shape[0] for group in hidden)
+    return pl.pallas_call(
+        functools.partial(served_kernel, batches, rows, [len(group) for group in hidden]),
+        out_shape=jax.ShapeDtypeStruct((batches, 1, total_rows // batches, width), BF16),
+        in_specs=[WHOLE] * len(flat),
         out_specs=WHOLE,
         compiler_params=params(),
         cost_estimate=cost(),
         name="serve",
-    )(*hidden)
-
-
-def down_kernel(cols, batches, rows, sizes, skip, table_ref, weight_ref, *refs):
+    )(*flat)
+
+
+def down_kernel(cols, batches, rows, sizes, parts, skip, table_ref, weight_ref, *refs):
     pairs, reps = cols
     columns = pairs * reps
-    count = columns * len(sizes)
-    held = jnp.concatenate([ref[...] for ref in refs[:count]], axis=0)
+    count = columns * sum(parts)
+    held = []
+    start = 0
+    for part_count in parts:
+        wide = []
+        for _ in range(part_count):
+            wide.append(jnp.concatenate([ref[...] for ref in refs[start : start + columns]], axis=0))
+            start += columns
+        held.append(jnp.concatenate(wide, axis=1))
+    held = jnp.concatenate(held, axis=0)
     share_refs = refs[count + skip : -1]
     sums_ref = refs[-1]
     depth = weight_ref.shape[1]
@@ -370,10 +393,11 @@
         for inner in range(size // seqs):
             blocks = []
             for held_at in places:
-                value = jnp.zeros((seqs, depth), F32)
+                value = None
                 for micro, place in enumerate(held_at):
                     base = pl.multiple_of(first + place * size + inner * seqs, seqs)
-                    value = jnp.where(row >= micro * rows, sums_ref[pl.ds(base, seqs), :], value)
+                    found = sums_ref[pl.ds(base, seqs), :]
+                    value = jnp.where(row >= micro * rows, found, value) if micro else found
                 blocks.append(value)
             same = [blocks[dr * pairs] for dr in range(reps)]
             other = [blocks[dr * pairs + dp] for dp in range(1, pairs) for dr in range(reps)]
@@ -387,13 +411,14 @@
     pairs, reps = cols
     depth = weight.shape[1]
     seqs = batches * rows
-    sizes = [block[0].shape[0] for block in blocks]
+    sizes = [group[0][0].shape[0] for group in blocks]
+    parts = [len(group) for group in blocks]
     shifts = sum(sizes) // seqs
-    flat = [part for block in blocks for part in block]
+    flat = [item for group in blocks for block in group for item in block]
     same = jax.ShapeDtypeStruct((reps * seqs, depth), BF16)
     other = jax.ShapeDtypeStruct(((pairs - 1) * reps * seqs, depth), BF16)
     out = pl.pallas_call(
-        functools.partial(down_kernel, cols, batches, rows, sizes, len(after)),
+        functools.partial(down_kernel, cols, batches, rows, sizes, parts, len(after)),
         out_shape=[same, other] * shifts,
         in_specs=[TABLE] + [WHOLE] * (1 + len(flat)) + [UNREAD] * len(after),
         out_specs=[WHOLE] * (2 * shifts),
@@ -512,21 +537,26 @@
     ])
     packs = [mine] + [turn(mine, ffn, -s) for s in range(1, ffn)]
     near, far = packs[:half], packs[half:]
-    gate_near = project(cols, "gate_near", near, gate_weight, [], kept=[up_weight])
-    up_near = project(cols, "up_near", near, up_weight, [])
-    here = mark("far_here", far, [gate_weight, up_weight])
-    near_own, *near_sent = join(pairs, "join_near", (swap(gate_near), swap(up_near)), [here])
+    weights = (gate_weight, up_weight)
+    units = gate_weight.shape[1] // 128
+    edge = units // 2 * 128
+    spans = ((0, edge), (edge, units * 128))
+    held, *first = gate_up(cols, "gate_up_near_0", near, weights, spans[0], [], 1, LONG)
+    second = gate_up(cols, "gate_up_near_1", [held], weights, spans[1], [], 1, LONG)
+    here = mark("far_here", far, [])
+    near_own, *near_sent = join(pairs, "join_near", [swap(first), swap(second)], [here])
     near_came = spread(near_sent)
-    gate_far = project(cols, "gate_far", far, gate_weight, [near_own], pairs, kept=[up_weight])
-    up_far = project(cols, "up_far", far, up_weight, [gate_far[0]], pairs, 10**6)
-    near_hidden = activate("activate_near", near_own, near_came, [])
-    far_own, *far_sent = join(
-        pairs, "join_far", (swap(gate_far), swap(up_far)), [near_hidden]
-    )
-    far_came = spread(far_sent)
-    far_hidden = activate("activate_far", far_own, far_came, [])
-    hiddens = [near_hidden, far_hidden]
-    blocks = [collect(hidden) for hidden in hiddens]
+    held, *first = gate_up(cols, "gate_up_far_0", far, weights, spans[0], [near_own], pairs, LONG)
+    second = gate_up(cols, "gate_up_far_1", [held], weights, spans[1], [], pairs, 10**6)
+    first_own, *first_sent = join(pairs, "join_far_0", [swap(first)], [])
+    first_came = spread(first_sent)
+    near_hidden = activate("activate_near", near_own, near_came, [first_own], LONG)
+    second_own, *second_sent = join(pairs, "join_far_1", [swap(second)], [])
+    second_came = spread(second_sent)
+    first_hidden = activate("activate_far_0", first_own, first_came, [])
+    second_hidden = activate("activate_far_1", second_own, second_came, [])
+    hiddens = [[near_hidden], [first_hidden, second_hidden]]
+    blocks = [[collect(part) for part in group] for group in hiddens]
     shares = down(cols, "down", batches, rows, partner_table, blocks, down_weight, [])
     totals = []
     for kind in (1, 0):

time: 71.6 us -> 69.3 us (0.968)
  waiting for transfers between devices: 23.7 us -> 19.7 us
  starting transfers between devices: 25.3 us -> 27.7 us
    ppermute x21 -> x25, waiting for transfers between devices: 14.5 us -> 9.55 us  [to_column(): return lax.ppermute(value, ('pair', 'rep'), route)]
    ppermute x21 -> x25, starting transfers between devices: 11.6 us -> 15 us  [to_column(): return lax.ppermute(value, ('pair', 'rep'), route)]
    ppermute x9, starting transfers between devices: 13.7 us -> 12.7 us  [turn(): lax.ppermute(value, 'ffn', [(i, (i + shift) % ffn) for i in range(ffn)])]
    ppermute x9, waiting for transfers between devices: 9.29 us -> 10.1 us  [turn(): lax.ppermute(value, 'ffn', [(i, (i + shift) % ffn) for i in range(ffn)])]
  transfers between devices with their start and end apart: 30 -> 34, of which waited for: 15 -> 15; matrix products, arithmetic and copies ran while one was open for 0% -> 0% of each run, Pallas kernels for 16% -> 17%
where the time goes in v4:
time: 69.3 us; the launch traced here: 69.2 us
  starting transfers between devices  27.7 us (40%)
  Pallas kernels  20.9 us (30%)
  waiting for transfers between devices  19.7 us (28%)
  between operations  0.86 us (1%)
    ppermute x25, starting transfers between devices, to_column(): return lax.ppermute(value, ('pair', 'rep'), route)  15 us
    ppermute x9, starting transfers between devices, turn(): lax.ppermute(value, 'ffn', [(i, (i + shift) % ffn) for i in range(ffn)])  12.7 us
    pallas_call x4, Pallas kernels, gate_up(): pl.pallas_call(functools.partial(gate_up_kernel, pairs * reps, len(packs)...  10.5 us
    ppermute x9, waiting for transfers between devices, turn(): lax.ppermute(value, 'ffn', [(i, (i + shift) % ffn) for i in range(ffn)])  10.1 us
    ppermute x25, waiting for transfers between devices, to_column(): return lax.ppermute(value, ('pair', 'rep'), route)  9.55 us
    pallas_call x1, Pallas kernels, attend(): pl.pallas_call(functools.partial(attend_kernel, cols, kvh, heads_per_step...  4.7 us
    pallas_call x1, Pallas kernels, down(): pl.pallas_call(functools.partial(down_kernel, cols, batches, rows, sizes,...  2.98 us
  transfers between devices with their start and end apart: 34, of which 15 were waited for; matrix products, arithmetic and copies ran while one was open for 0% of the time, Pallas kernels for 17%

profile of v4, /device:TPU:0, one launch (start us, length us, event | category | flops | bytes accessed | tf_op | source)
XLA Modules:
  0.0 69.2 jit_solution(16375839181667867192)
XLA Ops:
  0.7 4.7 %attend.1 = (f32[8,8192]{1,0:T(8,128)S(1)}, bf16[8,2048]{1,0:T(8,128)(2,1)S(1)}, bf16[8,2048]{1,0:T(8,128)(2,1)S(1)}, bf16[8,2048]{1,0:T(8,128)(2,1)S(1)}, bf16[8,2048]{1,0:T(8,128)(2,1)S(1)}) custom-call(s32[2,1,4]{2,1,0:T(1,128)} %len_ref.1, bf16[2,4,8192]{2,1,0:T(4,128)(2,1)} %bitcast.10, bf16[1024,1024]{1,0:T(8,128)(2,1)} %bitcast.7, ...), custom_call_target="tpu_custom_call" | custom-call | flops 99999997952 | bytes 100000000 | tf_op jit(solution)/shard_map/attend/pallas_call | solution.py:134
  5.4 3.0 %collective-permute-start = (bf16[8,2048]{1,0:T(8,128)(2,1)S(1)}, bf16[8,2048]{1,0:T(8,128)(2,1)S(1)}, u32[]{:S(2)}, u32[]{:S(2)}) collective-permute-start(bf16[8,2048]{1,0:T(8,128)(2,1)S(1)} %get-tuple-element.41), channel_id=1, source_target_pairs={{0,2},{1,3},{2,0},{3,1},{4,6},{5,7},{6,4},{7,5},{8,10},{9,11},{10,... | collective-permute-start | bytes 98312 | tf_op jit(solution)/shard_map/ppermute | solution.py:496
  8.6 1.7 %collective-permute-done.refs_1_ = bf16[8,2048]{1,0:T(8,128)(2,1)S(1)} collective-permute-done((bf16[8,2048]{1,0:T(8,128)(2,1)S(1)}, bf16[8,2048]{1,0:T(8,128)(2,1)S(1)}, u32[]{:S(2)}, u32[]{:S(2)}) %collective-permute-start) | collective-permute-done | bytes 32800 | tf_op jit(solution)/shard_map/ppermute | solution.py:496
  10.3 1.4 %collective-permute-done.2.refs_3_ = bf16[8,2048]{1,0:T(8,128)(2,1)S(1)} collective-permute-done((bf16[8,2048]{1,0:T(8,128)(2,1)S(1)}, bf16[8,2048]{1,0:T(8,128)(2,1)S(1)}, u32[]{:S(2)}, u32[]{:S(2)}) %collective-permute-start.2) | collective-permute-done | bytes 32800 | tf_op jit(solution)/shard_map/ppermute | solution.py:496
  12.4 3.7 %collective-permute-start.3 = (bf16[32,2048]{1,0:T(8,128)(2,1)S(1)}, bf16[32,2048]{1,0:T(8,128)(2,1)S(1)}, u32[]{:S(2)}, u32[]{:S(2)}) collective-permute-start(bf16[32,2048]{1,0:T(8,128)(2,1)S(1)} %pack.1.refs_0_), channel_id=1, source_target_pairs={{0,12},{4,0},{8,4},{12,8},{1,13},{5,1},{9,5},{13,9},{2,14},{6,2},{... | collective-permute-start | bytes 393224 | tf_op jit(solution)/shard_map/ppermute | solution.py:500
  16.0 1.0 %collective-permute-start.6 = (bf16[32,2048]{1,0:T(8,128)(2,1)S(1)}, bf16[32,2048]{1,0:T(8,128)(2,1)S(1)}, u32[]{:S(2)}, u32[]{:S(2)}) collective-permute-start(bf16[32,2048]{1,0:T(8,128)(2,1)S(1)} %pack.1.refs_0_), channel_id=1, source_target_pairs={{0,8},{4,12},{8,0},{12,4},{1,9},{5,13},{9,1},{13,5},{2,10},{6,14},... | collective-permute-start | bytes 393224 | tf_op jit(solution)/shard_map/ppermute | solution.py:500
  17.0 2.9 %collective-permute-done.3.refs_1_ = bf16[32,2048]{1,0:T(8,128)(2,1)S(1)} collective-permute-done((bf16[32,2048]{1,0:T(8,128)(2,1)S(1)}, bf16[32,2048]{1,0:T(8,128)(2,1)S(1)}, u32[]{:S(2)}, u32[]{:S(2)}) %collective-permute-start.3) | collective-permute-done | bytes 131104 | tf_op jit(solution)/shard_map/ppermute | solution.py:500
  19.9 2.6 %gate_up_near_0.1 = (bf16[64,2048]{1,0:T(8,128)(2,1)S(1)}, f32[2,32,1792]{2,1,0:T(8,128)S(1)}, bf16[2,32,1792]{2,1,0:T(8,128)(2,1)S(1)}) custom-call(bf16[2048,3584]{1,0:T(8,128)(2,1)S(1)} %copy-done, bf16[2048,3584]{1,0:T(8,128)(2,1)S(1)} %copy-done.1, bf16[32,2048]{1,0:T(8,128)(2,1)S(1)} %pack.1.refs_0_, bf16[32,2048]{1,0:T(8,128)(2,1)S(1)} %collective-permute-done.3.refs_1_), custom_call_target="tpu_custom_call" | custom-call | flops 49999998976 | bytes 50000000 | tf_op jit(solution)/shard_map/gate_up_near_0/pallas_call | solution.py:226
  22.6 2.6 %gate_up_near_1.1 = (f32[2,32,1792]{2,1,0:T(8,128)S(1)}, bf16[2,32,1792]{2,1,0:T(8,128)(2,1)S(1)}) custom-call(bf16[2048,3584]{1,0:T(8,128)(2,1)S(1)} %copy-done, bf16[2048,3584]{1,0:T(8,128)(2,1)S(1)} %copy-done.1, bf16[64,2048]{1,0:T(8,128)(2,1)S(1)} %get-tuple-element.46.refs_0_), custom_call_target="tpu_custom_call" | custom-call | flops 49999998976 | bytes 50000000 | tf_op jit(solution)/shard_map/gate_up_near_1/pallas_call | solution.py:226
  25.8 2.4 %collective-permute-done.6.refs_0_ = bf16[32,2048]{1,0:T(8,128)(2,1)S(1)} collective-permute-done((bf16[32,2048]{1,0:T(8,128)(2,1)S(1)}, bf16[32,2048]{1,0:T(8,128)(2,1)S(1)}, u32[]{:S(2)}, u32[]{:S(2)}) %collective-permute-start.6) | collective-permute-done | bytes 131104 | tf_op jit(solution)/shard_map/ppermute | solution.py:500
  28.9 2.6 %gate_up_far_0.1 = (bf16[64,2048]{1,0:T(8,128)(2,1)S(1)}, f32[2,32,1792]{2,1,0:T(8,128)S(1)}, bf16[2,16,1792]{2,1,0:T(8,128)(2,1)S(1)}, bf16[2,16,1792]{2,1,0:T(8,128)(2,1)S(1)}) custom-call(bf16[2048,3584]{1,0:T(8,128)(2,1)S(1)} %copy-done, bf16[2048,3584]{1,0:T(8,128)(2,1)S(1)} %copy-done.1, bf16[32,2048]{1,0:T(8,128)(2,1)S(1)} %collective-permute-done.6.refs_0_, ...), custom_call_target="tpu_custom_call" | custom-call | flops 49999998976 | bytes 50000000 | tf_op jit(solution)/shard_map/gate_up_far_0/pallas_call | solution.py:226
  32.1 2.6 %gate_up_far_1.1 = (f32[2,32,1792]{2,1,0:T(8,128)S(1)}, bf16[2,16,1792]{2,1,0:T(8,128)(2,1)S(1)}, bf16[2,16,1792]{2,1,0:T(8,128)(2,1)S(1)}) custom-call(bf16[2048,3584]{1,0:T(8,128)(2,1)S(1)} %copy-done, bf16[2048,3584]{1,0:T(8,128)(2,1)S(1)} %copy-done.1, bf16[64,2048]{1,0:T(8,128)(2,1)S(1)} %get-tuple-element.56.refs_0_), custom_call_target="tpu_custom_call" | custom-call | flops 1000000 | bytes 1000 | tf_op jit(solution)/shard_map/gate_up_far_1/pallas_call | solution.py:226
  35.4 1.5 %collective-permute-start.14 = (bf16[2,16,1792]{2,1,0:T(8,128)(2,1)S(1)}, bf16[2,16,1792]{2,1,0:T(8,128)(2,1)S(1)}, u32[]{:S(2)}, u32[]{:S(2)}) collective-permute-start(bf16[2,16,1792]{2,1,0:T(8,128)(2,1)S(1)} %get-tuple-element.55), channel_id=1, source_target_pairs={{0,2},{1,3},{2,0},{3,1},{4,6},{5,7},{6,4},{7,5},{8,10},{9,11},{10,... | collective-permute-start | bytes 344072 | tf_op jit(solution)/shard_map/ppermute | solution.py:496
  38.0 1.2 %collective-permute-start.11 = (bf16[16,3584]{1,0:T(8,128)(2,1)S(1)}, bf16[16,3584]{1,0:T(8,128)(2,1)S(1)}, u32[]{:S(2)}, u32[]{:S(2)}) collective-permute-start(bf16[16,3584]{1,0:T(8,128)(2,1)S(1)} %activate_near.1.refs_0_), channel_id=1, source_target_pairs={{0,2},{1,3},{2,0},{3,1},{4,6},{5,7},{6,4},{7,5},{8,10},{9,11},{10,... | collective-permute-start | bytes 344072 | tf_op jit(solution)/shard_map/ppermute | solution.py:496
  39.3 2.2 %collective-permute-done.14.refs_0_ = bf16[2,16,1792]{2,1,0:T(8,128)(2,1)S(1)} collective-permute-done((bf16[2,16,1792]{2,1,0:T(8,128)(2,1)S(1)}, bf16[2,16,1792]{2,1,0:T(8,128)(2,1)S(1)}, u32[]{:S(2)}, u32[]{:S(2)}) %collective-permute-start.14) | collective-permute-done | bytes 114720 | tf_op jit(solution)/shard_map/ppermute | solution.py:496
  41.6 1.5 %collective-permute-start.15 = (bf16[16,1792]{1,0:T(8,128)(2,1)S(1)}, bf16[16,1792]{1,0:T(8,128)(2,1)S(1)}, u32[]{:S(2)}, u32[]{:S(2)}) collective-permute-start(bf16[16,1792]{1,0:T(8,128)(2,1)S(1)} %activate_far_0.1.refs_4_.refs_1_), channel_id=1, source_target_pairs={{0,2},{1,3},{2,0},{3,1},{4,6},{5,7},{6,4},{7,5},{8,10},{9,11},{10,... | collective-permute-start | bytes 172040 | tf_op jit(solution)/shard_map/ppermute | solution.py:496
  44.0 1.5 %collective-permute-start.21 = (bf16[16,1792]{1,0:T(8,128)(2,1)S(1)}, bf16[16,1792]{1,0:T(8,128)(2,1)S(1)}, u32[]{:S(2)}, u32[]{:S(2)}) collective-permute-start(bf16[16,1792]{1,0:T(8,128)(2,1)S(1)} %activate_far_1.1.refs_8_.refs_2_), channel_id=1, source_target_pairs={{0,2},{1,3},{2,0},{3,1},{4,6},{5,7},{6,4},{7,5},{8,10},{9,11},{10,... | collective-permute-start | bytes 172040 | tf_op jit(solution)/shard_map/ppermute | solution.py:496
  49.5 3.0 %down.1 = (bf16[16,2048]{1,0:T(8,128)(2,1)S(1)}, bf16[16,2048]{1,0:T(8,128)(2,1)S(1)}, bf16[16,2048]{1,0:T(8,128)(2,1)S(1)}, bf16[16,2048]{1,0:T(8,128)(2,1)S(1)...) custom-call(s32[2,4]{1,0:T(2,128)S(1)} %copy-done.2, ...), custom_call_target="tpu_custom_call" | custom-call | flops 49999998976 | bytes 50000000 | tf_op jit(solution)/shard_map/down/pallas_call | solution.py:420
  52.5 4.0 %collective-permute-start.28 = (bf16[16,2048]{1,0:T(8,128)(2,1)S(1)}, bf16[16,2048]{1,0:T(8,128)(2,1)S(1)}, u32[]{:S(2)}, u32[]{:S(2)}) collective-permute-start(bf16[16,2048]{1,0:T(8,128)(2,1)S(1)} %get-tuple-element.68), channel_id=1, source_target_pairs={{0,8},{4,12},{8,0},{12,4},{1,9},{5,13},{9,1},{13,5},{2,10},{6,14},... | collective-permute-start | bytes 196616 | tf_op jit(solution)/shard_map/ppermute | solution.py:500
  56.5 2.0 %collective-permute-start.24 = (bf16[16,2048]{1,0:T(8,128)(2,1)S(1)}, bf16[16,2048]{1,0:T(8,128)(2,1)S(1)}, u32[]{:S(2)}, u32[]{:S(2)}) collective-permute-start(bf16[16,2048]{1,0:T(8,128)(2,1)S(1)} %get-tuple-element.63), channel_id=1, source_target_pairs={{0,4},{4,8},{8,12},{12,0},{1,5},{5,9},{9,13},{13,1},{2,6},{6,10},{... | collective-permute-start | bytes 196616 | tf_op jit(solution)/shard_map/ppermute | solution.py:500
  59.4 2.0 %collective-permute-start.26 = (bf16[16,2048]{1,0:T(8,128)(2,1)S(1)}, bf16[16,2048]{1,0:T(8,128)(2,1)S(1)}, u32[]{:S(2)}, u32[]{:S(2)}) collective-permute-start(bf16[16,2048]{1,0:T(8,128)(2,1)S(1)} %get-tuple-element.65), channel_id=1, source_target_pairs={{0,12},{4,0},{8,4},{12,8},{1,13},{5,1},{9,5},{13,9},{2,14},{6,2},{... | collective-permute-start | bytes 196616 | tf_op jit(solution)/shard_map/ppermute | solution.py:500
  61.4 2.0 %collective-permute-done.28.refs_2_ = bf16[16,2048]{1,0:T(8,128)(2,1)S(1)} collective-permute-done((bf16[16,2048]{1,0:T(8,128)(2,1)S(1)}, bf16[16,2048]{1,0:T(8,128)(2,1)S(1)}, u32[]{:S(2)}, u32[]{:S(2)}) %collective-permute-start.28) | collective-permute-done | bytes 65568 | tf_op jit(solution)/shard_map/ppermute | solution.py:500
  63.7 1.4 %collective-permute-start.30 = (bf16[8,2048]{1,0:T(8,128)(2,1)S(1)}, bf16[8,2048]{1,0:T(8,128)(2,1)S(1)}, u32[]{:S(2)}, u32[]{:S(2)}) collective-permute-start(bf16[8,2048]{1,0:T(8,128)(2,1)S(1)} %get-tuple-element.70.refs_4_), channel_id=1, source_target_pairs={{0,2},{1,3},{2,0},{3,1},{4,6},{5,7},{6,4},{7,5},{8,10},{9,11},{10,... | collective-permute-start | bytes 98312 | tf_op jit(solution)/shard_map/ppermute | solution.py:496
  65.1 1.9 %collective-permute-done.25.refs_2_ = bf16[16,2048]{1,0:T(8,128)(2,1)S(1)} collective-permute-done((bf16[16,2048]{1,0:T(8,128)(2,1)S(1)}, bf16[16,2048]{1,0:T(8,128)(2,1)S(1)}, u32[]{:S(2)}, u32[]{:S(2)}) %collective-permute-start.25) | collective-permute-done | bytes 65568 | tf_op jit(solution)/shard_map/ppermute | solution.py:500
  (77 shorter events, 12.8 us)
Async XLA Ops:
  5.4 4.9 %collective-permute-start = (bf16[8,2048]{1,0:T(8,128)(2,1)S(1)}, bf16[8,2048]{1,0:T(8,128)(2,1)S(1)}, u32[]{:S(2)}, u32[]{:S(2)}) collective-permute-start(bf16[8,2048]{1,0:T(8,128)(2,1)S(1)} %get-tuple-element.41), channel_id=1, source_target_pairs={{0,2},{1,3},{2,0},{3,1},{4,6},{5,7},{6,4},{7,5},{8,10},{9,11},{10,... | collective-permute-start | bytes 98312 | tf_op jit(solution)/shard_map/ppermute | solution.py:496
  8.4 3.3 %collective-permute-start.2 = (bf16[8,2048]{1,0:T(8,128)(2,1)S(1)}, bf16[8,2048]{1,0:T(8,128)(2,1)S(1)}, u32[]{:S(2)}, u32[]{:S(2)}) collective-permute-start(bf16[8,2048]{1,0:T(8,128)(2,1)S(1)} %get-tuple-element.43), channel_id=1, source_target_pairs={{0,3},{1,2},{2,1},{3,0},{4,7},{5,6},{6,5},{7,4},{8,11},{9,10},{10,... | collective-permute-start | bytes 98312 | tf_op jit(solution)/shard_map/ppermute | solution.py:496
  12.4 7.5 %collective-permute-start.3 = (bf16[32,2048]{1,0:T(8,128)(2,1)S(1)}, bf16[32,2048]{1,0:T(8,128)(2,1)S(1)}, u32[]{:S(2)}, u32[]{:S(2)}) collective-permute-start(bf16[32,2048]{1,0:T(8,128)(2,1)S(1)} %pack.1.refs_0_), channel_id=1, source_target_pairs={{0,12},{4,0},{8,4},{12,8},{1,13},{5,1},{9,5},{13,9},{2,14},{6,2},{... | collective-permute-start | bytes 393224 | tf_op jit(solution)/shard_map/ppermute | solution.py:500
  16.0 9.8 %collective-permute-start.7 = (bf16[32,2048]{1,0:T(8,128)(2,1)S(1)}, bf16[32,2048]{1,0:T(8,128)(2,1)S(1)}, u32[]{:S(2)}, u32[]{:S(2)}) collective-permute-start(bf16[32,2048]{1,0:T(8,128)(2,1)S(1)} %pack.1.refs_0_), channel_id=1, source_target_pairs={{0,4},{4,8},{8,12},{12,0},{1,5},{5,9},{9,13},{13,1},{2,6},{6,10},{... | collective-permute-start | bytes 393224 | tf_op jit(solution)/shard_map/ppermute | solution.py:500
  16.0 12.1 %collective-permute-start.6 = (bf16[32,2048]{1,0:T(8,128)(2,1)S(1)}, bf16[32,2048]{1,0:T(8,128)(2,1)S(1)}, u32[]{:S(2)}, u32[]{:S(2)}) collective-permute-start(bf16[32,2048]{1,0:T(8,128)(2,1)S(1)} %pack.1.refs_0_), channel_id=1, source_target_pairs={{0,8},{4,12},{8,0},{12,4},{1,9},{5,13},{9,1},{13,5},{2,10},{6,14},... | collective-permute-start | bytes 393224 | tf_op jit(solution)/shard_map/ppermute | solution.py:500
  22.5 5.6 %collective-permute-start.4 = (bf16[2,32,1792]{2,1,0:T(8,128)(2,1)S(1)}, bf16[2,32,1792]{2,1,0:T(8,128)(2,1)S(1)}, u32[]{:S(2)}, u32[]{:S(2)}) collective-permute-start(bf16[2,32,1792]{2,1,0:T(8,128)(2,1)S(1)} %get-tuple-element.45), channel_id=1, source_target_pairs={{0,1},{1,0},{2,3},{3,2},{4,5},{5,4},{6,7},{7,6},{8,9},{9,8},{10,11... | collective-permute-start | bytes 688136 | tf_op jit(solution)/shard_map/ppermute | solution.py:496
  28.3 9.6 %collective-permute-start.8 = (bf16[2,16,3584]{2,1,0:T(8,128)(2,1)S(1)}, bf16[2,16,3584]{2,1,0:T(8,128)(2,1)S(1)}, u32[]{:S(2)}, u32[]{:S(2)}) collective-permute-start(bf16[2,16,3584]{2,1,0:T(8,128)(2,1)S(1)} %get-tuple-element.50), channel_id=1, source_target_pairs={{0,2},{1,3},{2,0},{3,1},{4,6},{5,7},{6,4},{7,5},{8,10},{9,11},{10,... | collective-permute-start | bytes 688136 | tf_op jit(solution)/shard_map/ppermute | solution.py:496
  31.5 3.8 %collective-permute-start.9 = (bf16[2,16,1792]{2,1,0:T(8,128)(2,1)S(1)}, bf16[2,16,1792]{2,1,0:T(8,128)(2,1)S(1)}, u32[]{:S(2)}, u32[]{:S(2)}) collective-permute-start(bf16[2,16,1792]{2,1,0:T(8,128)(2,1)S(1)} %get-tuple-element.52), channel_id=1, source_target_pairs={{0,1},{1,0},{2,3},{3,2},{4,5},{5,4},{6,7},{7,6},{8,9},{9,8},{10,11... | collective-permute-start | bytes 344072 | tf_op jit(solution)/shard_map/ppermute | solution.py:496
  31.6 3.7 %collective-permute-start.10 = (bf16[2,16,1792]{2,1,0:T(8,128)(2,1)S(1)}, bf16[2,16,1792]{2,1,0:T(8,128)(2,1)S(1)}, u32[]{:S(2)}, u32[]{:S(2)}) collective-permute-start(bf16[2,16,1792]{2,1,0:T(8,128)(2,1)S(1)} %get-tuple-element.53), channel_id=1, source_target_pairs={{0,1},{1,0},{2,3},{3,2},{4,5},{5,4},{6,7},{7,6},{8,9},{9,8},{10,11... | collective-permute-start | bytes 344072 | tf_op jit(solution)/shard_map/ppermute | solution.py:496
  35.4 6.1 %collective-permute-start.14 = (bf16[2,16,1792]{2,1,0:T(8,128)(2,1)S(1)}, bf16[2,16,1792]{2,1,0:T(8,128)(2,1)S(1)}, u32[]{:S(2)}, u32[]{:S(2)}) collective-permute-start(bf16[2,16,1792]{2,1,0:T(8,128)(2,1)S(1)} %get-tuple-element.55), channel_id=1, source_target_pairs={{0,2},{1,3},{2,0},{3,1},{4,6},{5,7},{6,4},{7,5},{8,10},{9,11},{10,... | collective-permute-start | bytes 344072 | tf_op jit(solution)/shard_map/ppermute | solution.py:496
  37.0 6.9 %collective-permute-start.20 = (bf16[2,16,1792]{2,1,0:T(8,128)(2,1)S(1)}, bf16[2,16,1792]{2,1,0:T(8,128)(2,1)S(1)}, u32[]{:S(2)}, u32[]{:S(2)}) collective-permute-start(bf16[2,16,1792]{2,1,0:T(8,128)(2,1)S(1)} %get-tuple-element.61), channel_id=1, source_target_pairs={{0,2},{1,3},{2,0},{3,1},{4,6},{5,7},{6,4},{7,5},{8,10},{9,11},{10,... | collective-permute-start | bytes 344072 | tf_op jit(solution)/shard_map/ppermute | solution.py:496
  38.0 8.1 %collective-permute-start.11 = (bf16[16,3584]{1,0:T(8,128)(2,1)S(1)}, bf16[16,3584]{1,0:T(8,128)(2,1)S(1)}, u32[]{:S(2)}, u32[]{:S(2)}) collective-permute-start(bf16[16,3584]{1,0:T(8,128)(2,1)S(1)} %activate_near.1.refs_0_), channel_id=1, source_target_pairs={{0,2},{1,3},{2,0},{3,1},{4,6},{5,7},{6,4},{7,5},{8,10},{9,11},{10,... | collective-permute-start | bytes 344072 | tf_op jit(solution)/shard_map/ppermute | solution.py:496
  39.3 8.9 %collective-permute-start.12 = (bf16[16,3584]{1,0:T(8,128)(2,1)S(1)}, bf16[16,3584]{1,0:T(8,128)(2,1)S(1)}, u32[]{:S(2)}, u32[]{:S(2)}) collective-permute-start(bf16[16,3584]{1,0:T(8,128)(2,1)S(1)} %activate_near.1.refs_0_), channel_id=1, source_target_pairs={{0,1},{1,0},{2,3},{3,2},{4,5},{5,4},{6,7},{7,6},{8,9},{9,8},{10,11... | collective-permute-start | bytes 344072 | tf_op jit(solution)/shard_map/ppermute | solution.py:496
  41.5 4.6 %collective-permute-start.16 = (bf16[16,1792]{1,0:T(8,128)(2,1)S(1)}, bf16[16,1792]{1,0:T(8,128)(2,1)S(1)}, u32[]{:S(2)}, u32[]{:S(2)}) collective-permute-start(bf16[16,1792]{1,0:T(8,128)(2,1)S(1)} %activate_far_0.1.refs_4_.refs_1_), channel_id=1, source_target_pairs={{0,1},{1,0},{2,3},{3,2},{4,5},{5,4},{6,7},{7,6},{8,9},{9,8},{10,11... | collective-permute-start | bytes 172040 | tf_op jit(solution)/shard_map/ppermute | solution.py:496
  41.6 5.7 %collective-permute-start.15 = (bf16[16,1792]{1,0:T(8,128)(2,1)S(1)}, bf16[16,1792]{1,0:T(8,128)(2,1)S(1)}, u32[]{:S(2)}, u32[]{:S(2)}) collective-permute-start(bf16[16,1792]{1,0:T(8,128)(2,1)S(1)} %activate_far_0.1.refs_4_.refs_1_), channel_id=1, source_target_pairs={{0,2},{1,3},{2,0},{3,1},{4,6},{5,7},{6,4},{7,5},{8,10},{9,11},{10,... | collective-permute-start | bytes 172040 | tf_op jit(solution)/shard_map/ppermute | solution.py:496
  44.0 4.2 %collective-permute-start.21 = (bf16[16,1792]{1,0:T(8,128)(2,1)S(1)}, bf16[16,1792]{1,0:T(8,128)(2,1)S(1)}, u32[]{:S(2)}, u32[]{:S(2)}) collective-permute-start(bf16[16,1792]{1,0:T(8,128)(2,1)S(1)} %activate_far_1.1.refs_8_.refs_2_), channel_id=1, source_target_pairs={{0,2},{1,3},{2,0},{3,1},{4,6},{5,7},{6,4},{7,5},{8,10},{9,11},{10,... | collective-permute-start | bytes 172040 | tf_op jit(solution)/shard_map/ppermute | solution.py:496
  52.5 6.9 %collective-permute-start.27 = (bf16[16,2048]{1,0:T(8,128)(2,1)S(1)}, bf16[16,2048]{1,0:T(8,128)(2,1)S(1)}, u32[]{:S(2)}, u32[]{:S(2)}) collective-permute-start(bf16[16,2048]{1,0:T(8,128)(2,1)S(1)} %get-tuple-element.67), channel_id=1, source_target_pairs={{0,4},{4,8},{8,12},{12,0},{1,5},{5,9},{9,13},{13,1},{2,6},{6,10},{... | collective-permute-start | bytes 196616 | tf_op jit(solution)/shard_map/ppermute | solution.py:500
  52.5 10.8 %collective-permute-start.28 = (bf16[16,2048]{1,0:T(8,128)(2,1)S(1)}, bf16[16,2048]{1,0:T(8,128)(2,1)S(1)}, u32[]{:S(2)}, u32[]{:S(2)}) collective-permute-start(bf16[16,2048]{1,0:T(8,128)(2,1)S(1)} %get-tuple-element.68), channel_id=1, source_target_pairs={{0,8},{4,12},{8,0},{12,4},{1,9},{5,13},{9,1},{13,5},{2,10},{6,14},... | collective-permute-start | bytes 196616 | tf_op jit(solution)/shard_map/ppermute | solution.py:500
  56.5 7.1 %collective-permute-start.29 = (bf16[16,2048]{1,0:T(8,128)(2,1)S(1)}, bf16[16,2048]{1,0:T(8,128)(2,1)S(1)}, u32[]{:S(2)}, u32[]{:S(2)}) collective-permute-start(bf16[16,2048]{1,0:T(8,128)(2,1)S(1)} %get-tuple-element.69), channel_id=1, source_target_pairs={{0,12},{4,0},{8,4},{12,8},{1,13},{5,1},{9,5},{13,9},{2,14},{6,2},{... | collective-permute-start | bytes 196616 | tf_op jit(solution)/shard_map/ppermute | solution.py:500
  56.5 8.6 %collective-permute-start.24 = (bf16[16,2048]{1,0:T(8,128)(2,1)S(1)}, bf16[16,2048]{1,0:T(8,128)(2,1)S(1)}, u32[]{:S(2)}, u32[]{:S(2)}) collective-permute-start(bf16[16,2048]{1,0:T(8,128)(2,1)S(1)} %get-tuple-element.63), channel_id=1, source_target_pairs={{0,4},{4,8},{8,12},{12,0},{1,5},{5,9},{9,13},{13,1},{2,6},{6,10},{... | collective-permute-start | bytes 196616 | tf_op jit(solution)/shard_map/ppermute | solution.py:500
  58.5 8.4 %collective-permute-start.25 = (bf16[16,2048]{1,0:T(8,128)(2,1)S(1)}, bf16[16,2048]{1,0:T(8,128)(2,1)S(1)}, u32[]{:S(2)}, u32[]{:S(2)}) collective-permute-start(bf16[16,2048]{1,0:T(8,128)(2,1)S(1)} %get-tuple-element.64), channel_id=1, source_target_pairs={{0,8},{4,12},{8,0},{12,4},{1,9},{5,13},{9,1},{13,5},{2,10},{6,14},... | collective-permute-start | bytes 196616 | tf_op jit(solution)/shard_map/ppermute | solution.py:500
  59.4 7.6 %collective-permute-start.26 = (bf16[16,2048]{1,0:T(8,128)(2,1)S(1)}, bf16[16,2048]{1,0:T(8,128)(2,1)S(1)}, u32[]{:S(2)}, u32[]{:S(2)}) collective-permute-start(bf16[16,2048]{1,0:T(8,128)(2,1)S(1)} %get-tuple-element.65), channel_id=1, source_target_pairs={{0,12},{4,0},{8,4},{12,8},{1,13},{5,1},{9,5},{13,9},{2,14},{6,2},{... | collective-permute-start | bytes 196616 | tf_op jit(solution)/shard_map/ppermute | solution.py:500
  63.7 4.8 %collective-permute-start.33 = (bf16[8,2048]{1,0:T(8,128)(2,1)S(1)}, bf16[8,2048]{1,0:T(8,128)(2,1)S(1)}, u32[]{:S(2)}, u32[]{:S(2)}) collective-permute-start(bf16[8,2048]{1,0:T(8,128)(2,1)S(1)} %get-tuple-element.75), channel_id=1, source_target_pairs={{0,3},{1,2},{2,1},{3,0},{4,7},{5,6},{6,5},{7,4},{8,11},{9,10},{10,... | collective-permute-start | bytes 98312 | tf_op jit(solution)/shard_map/ppermute | solution.py:496
  63.7 4.7 %collective-permute-start.30 = (bf16[8,2048]{1,0:T(8,128)(2,1)S(1)}, bf16[8,2048]{1,0:T(8,128)(2,1)S(1)}, u32[]{:S(2)}, u32[]{:S(2)}) collective-permute-start(bf16[8,2048]{1,0:T(8,128)(2,1)S(1)} %get-tuple-element.70.refs_4_), channel_id=1, source_target_pairs={{0,2},{1,3},{2,0},{3,1},{4,6},{5,7},{6,4},{7,5},{8,10},{9,11},{10,... | collective-permute-start | bytes 98312 | tf_op jit(solution)/shard_map/ppermute | solution.py:496
  (17 other events, 121.2 us)

commit v5 on v4

--- a/solution.py
+++ b/solution.py
@@ -325,7 +325,8 @@
 
 
 def served_kernel(batches, rows, counts, *refs):
-    out_ref = refs[-1]
+    out_ref, mark_ref = refs[-2:]
+    mark_ref[...] = jnp.zeros(mark_ref.shape, F32)
     turned = lax.axis_index("ffn") * rows
     seqs = batches * rows
     groups = []
@@ -347,11 +348,14 @@
     total_rows = sum(group[0].shape[0] for group in hidden)
     return pl.pallas_call(
         functools.partial(served_kernel, batches, rows, [len(group) for group in hidden]),
-        out_shape=jax.ShapeDtypeStruct((batches, 1, total_rows // batches, width), BF16),
+        out_shape=[
+            jax.ShapeDtypeStruct((batches, 1, total_rows // batches, width), BF16),
+            jax.ShapeDtypeStruct((8, 128), F32),
+        ],
         in_specs=[WHOLE] * len(flat),
-        out_specs=WHOLE,
-        compiler_params=params(),
-        cost_estimate=cost(),
+        out_specs=[WHOLE] * 2,
+        compiler_params=params(),
+        cost_estimate=cost(LONG),
         name="serve",
     )(*flat)
 
@@ -387,6 +391,9 @@
             to_rep = lax.rem(lax.rem(column, reps) - lax.axis_index("rep") + reps, reps)
             held_at.append(to_rep * pairs + to_pair)
         places.append(held_at)
+    count = sum(sizes) // seqs
+    mine_refs, peer_refs = share_refs[:count], share_refs[count : count + reps - 1]
+    other_refs = share_refs[count + reps - 1 :]
     first = 0
     shift = 0
     for size in sizes:
@@ -399,10 +406,11 @@
                     found = sums_ref[pl.ds(base, seqs), :]
                     value = jnp.where(row >= micro * rows, found, value) if micro else found
                 blocks.append(value)
-            same = [blocks[dr * pairs] for dr in range(reps)]
+            mine_refs[shift][...] = blocks[0].astype(BF16)
+            for dr in range(1, reps):
+                peer_refs[dr - 1][shift] = blocks[dr * pairs].astype(BF16)
             other = [blocks[dr * pairs + dp] for dp in range(1, pairs) for dr in range(reps)]
-            share_refs[2 * shift][...] = jnp.concatenate(same, axis=0).astype(BF16)
-            share_refs[2 * shift + 1][...] = jnp.concatenate(other, axis=0).astype(BF16)
+            other_refs[shift][...] = jnp.concatenate(other, axis=0).astype(BF16)
             shift += 1
         first += columns * size
 
@@ -415,38 +423,58 @@
     parts = [len(group) for group in blocks]
     shifts = sum(sizes) // seqs
     flat = [item for group in blocks for block in group for item in block]
-    same = jax.ShapeDtypeStruct((reps * seqs, depth), BF16)
+    mine = jax.ShapeDtypeStruct((seqs, depth), BF16)
+    peer = jax.ShapeDtypeStruct((shifts, seqs, depth), BF16)
     other = jax.ShapeDtypeStruct(((pairs - 1) * reps * seqs, depth), BF16)
     out = pl.pallas_call(
         functools.partial(down_kernel, cols, batches, rows, sizes, parts, len(after)),
-        out_shape=[same, other] * shifts,
+        out_shape=[mine] * shifts + [peer] * (reps - 1) + [other] * shifts,
         in_specs=[TABLE] + [WHOLE] * (1 + len(flat)) + [UNREAD] * len(after),
-        out_specs=[WHOLE] * (2 * shifts),
+        out_specs=[WHOLE] * (2 * shifts + reps - 1),
         scratch_shapes=[pltpu.VMEM((sum(sizes) * pairs * reps, depth), F32)],
         compiler_params=params(8),
         cost_estimate=cost(LONG),
         name=name,
     )(table, weight, *flat, *after)
-    return out[0::2], out[1::2]
-
-
-def total_kernel(count, outs, cuts, *refs):
+    return out[:shifts], out[shifts : shifts + reps - 1], out[shifts + reps - 1 :]
+
+
+def merge_kernel(shifts, reps, *refs):
+    out_refs = refs[-shifts:]
+    for shift, out_ref in enumerate(out_refs):
+        out_ref[0] = refs[shift][...]
+        for dr in range(1, reps):
+            out_ref[dr] = refs[shifts + dr - 1][shift]
+
+
+def merge(mine, peers, after):
+    shifts, reps = len(mine), len(peers) + 1
+    return pl.pallas_call(
+        functools.partial(merge_kernel, shifts, reps),
+        out_shape=[jax.ShapeDtypeStruct((reps, *mine[0].shape), BF16)] * shifts,
+        in_specs=[WHOLE] * (shifts + reps - 1) + [UNREAD] * len(after),
+        out_specs=[WHOLE] * shifts,
+        compiler_params=params(),
+        cost_estimate=cost(),
+        name="merge",
+    )(*mine, *peers, *after)
+
+
+def total_kernel(count, outs, *refs):
     sums = refs[0][...].astype(F32)
     for ref in refs[1:count]:
         sums = sums + ref[...].astype(F32)
-    rows, width = refs[-1].shape
+    if sums.ndim == 2:
+        sums = sums.reshape(outs, sums.shape[0] // outs, sums.shape[1])
     for index, out_ref in enumerate(refs[-outs:]):
-        row, column = divmod(index, cuts)
-        part = sums[row * rows : (row + 1) * rows, column * width : (column + 1) * width]
-        out_ref[...] = part.astype(BF16)
-
-
-def total(name, seqs, parts, after, cuts):
-    rows, depth = parts[0].shape
-    outs = rows // seqs * cuts
-    return pl.pallas_call(
-        functools.partial(total_kernel, len(parts), outs, cuts),
-        out_shape=[jax.ShapeDtypeStruct((seqs, depth // cuts), BF16)] * outs,
+        out_ref[...] = sums[index].astype(BF16)
+
+
+def total(name, seqs, parts, after):
+    outs = parts[0].size // parts[0].shape[-1] // seqs
+    return pl.pallas_call(
+        functools.partial(total_kernel, len(parts), outs),
+        out_shape=[jax.ShapeDtypeStruct((seqs, parts[0].shape[-1]), BF16)] * outs,
         in_specs=[WHOLE] * len(parts) + [UNREAD] * len(after),
         out_specs=[WHOLE] * outs,
         compiler_params=params(),
@@ -557,21 +585,20 @@
     second_hidden = activate("activate_far_1", second_own, second_came, [])
     hiddens = [[near_hidden], [first_hidden, second_hidden]]
     blocks = [[collect(part) for part in group] for group in hiddens]
-    shares = down(cols, "down", batches, rows, partner_table, blocks, down_weight, [])
-    totals = []
-    for kind in (1, 0):
-        gathered = [shares[kind][0]] + [turn(shares[kind][s], ffn, s) for s in range(1, ffn)]
-        after = [part for parts in totals for part in parts[:1]]
-        name = ("total_same", "total_other")[kind]
-        totals.append(total(name, batches * rows, gathered, after, 2 - kind))
-    other, same = totals
+    served, placed = serve(batches, rows, hiddens)
+    mine, peers, other = down(cols, "down", batches, rows, partner_table, blocks, down_weight, [])
+    other = [other[0]] + [turn(other[s], ffn, s) for s in range(1, ffn)]
+    same = merge(
+        mine, [to_column(cols, peer, dr + 1, 0) for dr, peer in enumerate(peers)], [placed]
+    )
+    same = [same[0]] + [turn(same[s], ffn, s) for s in range(1, ffn)]
+    other = total("total_other", batches * rows, other, [same[0]])
+    same = total("total_same", batches * rows, same, other[:1])
     changes = []
     for dr in range(reps):
-        parts = same[2 * dr : 2 * dr + 2]
-        changes.append([to_column(cols, part, dr, 0) if dr else part for part in parts])
+        changes.append([same[dr]])
         for dp in range(1, pairs):
             changes.append([to_column(cols, other[(dp - 1) * reps + dr], dr, dp)])
-    served = serve(batches, rows, hiddens)
     updated = finish(cols, batches, stream, changes)
     return (updated, served)
 

time: 69.3 us -> 68.1 us (0.983)
  waiting for transfers between devices: 19.7 us -> 18.1 us
    ppermute x9, waiting for transfers between devices: 10.1 us -> 7.79 us  [turn(): lax.ppermute(value, 'ffn', [(i, (i + shift) % ffn) for i in range(ffn)])]
    ppermute x9, starting transfers between devices: 12.7 us -> 13.5 us  [turn(): lax.ppermute(value, 'ffn', [(i, (i + shift) % ffn) for i in range(ffn)])]
    ppermute x25 -> x24, waiting for transfers between devices: 9.55 us -> 10.3 us  [to_column(): return lax.ppermute(value, ('pair', 'rep'), route)]
    ppermute x25 -> x24, starting transfers between devices: 15 us -> 14.6 us  [to_column(): return lax.ppermute(value, ('pair', 'rep'), route)]
  transfers between devices with their start and end apart: 34 -> 33, of which waited for: 15 -> 15; matrix products, arithmetic and copies ran while one was open for 0% -> 0% of each run, Pallas kernels for 17% -> 17%
where the time goes in v5:
time: 68.1 us; the launch traced here: 68 us
  starting transfers between devices  28.2 us (41%)
  Pallas kernels  20.9 us (31%)
  waiting for transfers between devices  18.1 us (27%)
  between operations  0.87 us (1%)
    ppermute x24, starting transfers between devices, to_column(): return lax.ppermute(value, ('pair', 'rep'), route)  14.6 us
    ppermute x9, starting transfers between devices, turn(): lax.ppermute(value, 'ffn', [(i, (i + shift) % ffn) for i in range(ffn)])  13.5 us
    pallas_call x4, Pallas kernels, gate_up(): pl.pallas_call(functools.partial(gate_up_kernel, pairs * reps, len(packs)...  10.5 us
    ppermute x24, waiting for transfers between devices, to_column(): return lax.ppermute(value, ('pair', 'rep'), route)  10.3 us
    ppermute x9, waiting for transfers between devices, turn(): lax.ppermute(value, 'ffn', [(i, (i + shift) % ffn) for i in range(ffn)])  7.79 us
    pallas_call x1, Pallas kernels, attend(): pl.pallas_call(functools.partial(attend_kernel, cols, kvh, heads_per_step...  4.69 us
    pallas_call x1, Pallas kernels, down(): pl.pallas_call(functools.partial(down_kernel, cols, batches, rows, sizes,...  2.95 us
  transfers between devices with their start and end apart: 33, of which 15 were waited for; matrix products, arithmetic and copies ran while one was open for 0% of the time, Pallas kernels for 17%

profile of v5, /device:TPU:0, one launch (start us, length us, event | category | flops | bytes accessed | tf_op | source)
XLA Modules:
  0.0 68.0 jit_solution(3452639831479640824)
XLA Ops:
  0.7 4.7 %attend.1 = (f32[8,8192]{1,0:T(8,128)S(1)}, bf16[8,2048]{1,0:T(8,128)(2,1)S(1)}, bf16[8,2048]{1,0:T(8,128)(2,1)S(1)}, bf16[8,2048]{1,0:T(8,128)(2,1)S(1)}, bf16[8,2048]{1,0:T(8,128)(2,1)S(1)}) custom-call(s32[2,1,4]{2,1,0:T(1,128)} %len_ref.1, bf16[2,4,8192]{2,1,0:T(4,128)(2,1)} %bitcast.10, bf16[1024,1024]{1,0:T(8,128)(2,1)} %bitcast.7, ...), custom_call_target="tpu_custom_call" | custom-call | flops 99999997952 | bytes 100000000 | tf_op jit(solution)/shard_map/attend/pallas_call | solution.py:134
  5.4 3.0 %collective-permute-start = (bf16[8,2048]{1,0:T(8,128)(2,1)S(1)}, bf16[8,2048]{1,0:T(8,128)(2,1)S(1)}, u32[]{:S(2)}, u32[]{:S(2)}) collective-permute-start(bf16[8,2048]{1,0:T(8,128)(2,1)S(1)} %get-tuple-element.46), channel_id=1, source_target_pairs={{0,2},{1,3},{2,0},{3,1},{4,6},{5,7},{6,4},{7,5},{8,10},{9,11},{10,... | collective-permute-start | bytes 98312 | tf_op jit(solution)/shard_map/ppermute | solution.py:524
  8.6 1.7 %collective-permute-done.refs_1_ = bf16[8,2048]{1,0:T(8,128)(2,1)S(1)} collective-permute-done((bf16[8,2048]{1,0:T(8,128)(2,1)S(1)}, bf16[8,2048]{1,0:T(8,128)(2,1)S(1)}, u32[]{:S(2)}, u32[]{:S(2)}) %collective-permute-start) | collective-permute-done | bytes 32800 | tf_op jit(solution)/shard_map/ppermute | solution.py:524
  10.3 1.4 %collective-permute-done.2.refs_3_ = bf16[8,2048]{1,0:T(8,128)(2,1)S(1)} collective-permute-done((bf16[8,2048]{1,0:T(8,128)(2,1)S(1)}, bf16[8,2048]{1,0:T(8,128)(2,1)S(1)}, u32[]{:S(2)}, u32[]{:S(2)}) %collective-permute-start.2) | collective-permute-done | bytes 32800 | tf_op jit(solution)/shard_map/ppermute | solution.py:524
  12.4 3.6 %collective-permute-start.3 = (bf16[32,2048]{1,0:T(8,128)(2,1)S(1)}, bf16[32,2048]{1,0:T(8,128)(2,1)S(1)}, u32[]{:S(2)}, u32[]{:S(2)}) collective-permute-start(bf16[32,2048]{1,0:T(8,128)(2,1)S(1)} %pack.1.refs_0_), channel_id=1, source_target_pairs={{0,12},{4,0},{8,4},{12,8},{1,13},{5,1},{9,5},{13,9},{2,14},{6,2},{... | collective-permute-start | bytes 393224 | tf_op jit(solution)/shard_map/ppermute | solution.py:528
  16.0 1.0 %collective-permute-start.6 = (bf16[32,2048]{1,0:T(8,128)(2,1)S(1)}, bf16[32,2048]{1,0:T(8,128)(2,1)S(1)}, u32[]{:S(2)}, u32[]{:S(2)}) collective-permute-start(bf16[32,2048]{1,0:T(8,128)(2,1)S(1)} %pack.1.refs_0_), channel_id=1, source_target_pairs={{0,8},{4,12},{8,0},{12,4},{1,9},{5,13},{9,1},{13,5},{2,10},{6,14},... | collective-permute-start | bytes 393224 | tf_op jit(solution)/shard_map/ppermute | solution.py:528
  17.0 2.8 %collective-permute-done.3.refs_1_ = bf16[32,2048]{1,0:T(8,128)(2,1)S(1)} collective-permute-done((bf16[32,2048]{1,0:T(8,128)(2,1)S(1)}, bf16[32,2048]{1,0:T(8,128)(2,1)S(1)}, u32[]{:S(2)}, u32[]{:S(2)}) %collective-permute-start.3) | collective-permute-done | bytes 131104 | tf_op jit(solution)/shard_map/ppermute | solution.py:528
  19.9 2.6 %gate_up_near_0.1 = (bf16[64,2048]{1,0:T(8,128)(2,1)S(1)}, f32[2,32,1792]{2,1,0:T(8,128)S(1)}, bf16[2,32,1792]{2,1,0:T(8,128)(2,1)S(1)}) custom-call(bf16[2048,3584]{1,0:T(8,128)(2,1)S(1)} %copy-done, bf16[2048,3584]{1,0:T(8,128)(2,1)S(1)} %copy-done.1, bf16[32,2048]{1,0:T(8,128)(2,1)S(1)} %pack.1.refs_0_, bf16[32,2048]{1,0:T(8,128)(2,1)S(1)} %collective-permute-done.3.refs_1_), custom_call_target="tpu_custom_call" | custom-call | flops 49999998976 | bytes 50000000 | tf_op jit(solution)/shard_map/gate_up_near_0/pallas_call | solution.py:226
  22.6 2.6 %gate_up_near_1.1 = (f32[2,32,1792]{2,1,0:T(8,128)S(1)}, bf16[2,32,1792]{2,1,0:T(8,128)(2,1)S(1)}) custom-call(bf16[2048,3584]{1,0:T(8,128)(2,1)S(1)} %copy-done, bf16[2048,3584]{1,0:T(8,128)(2,1)S(1)} %copy-done.1, bf16[64,2048]{1,0:T(8,128)(2,1)S(1)} %get-tuple-element.51.refs_0_), custom_call_target="tpu_custom_call" | custom-call | flops 49999998976 | bytes 50000000 | tf_op jit(solution)/shard_map/gate_up_near_1/pallas_call | solution.py:226
  25.8 2.4 %collective-permute-done.6.refs_0_ = bf16[32,2048]{1,0:T(8,128)(2,1)S(1)} collective-permute-done((bf16[32,2048]{1,0:T(8,128)(2,1)S(1)}, bf16[32,2048]{1,0:T(8,128)(2,1)S(1)}, u32[]{:S(2)}, u32[]{:S(2)}) %collective-permute-start.6) | collective-permute-done | bytes 131104 | tf_op jit(solution)/shard_map/ppermute | solution.py:528
  28.9 2.6 %gate_up_far_0.1 = (bf16[64,2048]{1,0:T(8,128)(2,1)S(1)}, f32[2,32,1792]{2,1,0:T(8,128)S(1)}, bf16[2,16,1792]{2,1,0:T(8,128)(2,1)S(1)}, bf16[2,16,1792]{2,1,0:T(8,128)(2,1)S(1)}) custom-call(bf16[2048,3584]{1,0:T(8,128)(2,1)S(1)} %copy-done, bf16[2048,3584]{1,0:T(8,128)(2,1)S(1)} %copy-done.1, bf16[32,2048]{1,0:T(8,128)(2,1)S(1)} %collective-permute-done.6.refs_0_, ...), custom_call_target="tpu_custom_call" | custom-call | flops 49999998976 | bytes 50000000 | tf_op jit(solution)/shard_map/gate_up_far_0/pallas_call | solution.py:226
  32.1 2.6 %gate_up_far_1.1 = (f32[2,32,1792]{2,1,0:T(8,128)S(1)}, bf16[2,16,1792]{2,1,0:T(8,128)(2,1)S(1)}, bf16[2,16,1792]{2,1,0:T(8,128)(2,1)S(1)}) custom-call(bf16[2048,3584]{1,0:T(8,128)(2,1)S(1)} %copy-done, bf16[2048,3584]{1,0:T(8,128)(2,1)S(1)} %copy-done.1, bf16[64,2048]{1,0:T(8,128)(2,1)S(1)} %get-tuple-element.61.refs_0_), custom_call_target="tpu_custom_call" | custom-call | flops 1000000 | bytes 1000 | tf_op jit(solution)/shard_map/gate_up_far_1/pallas_call | solution.py:226
  35.4 1.5 %collective-permute-start.14 = (bf16[2,16,1792]{2,1,0:T(8,128)(2,1)S(1)}, bf16[2,16,1792]{2,1,0:T(8,128)(2,1)S(1)}, u32[]{:S(2)}, u32[]{:S(2)}) collective-permute-start(bf16[2,16,1792]{2,1,0:T(8,128)(2,1)S(1)} %get-tuple-element.60), channel_id=1, source_target_pairs={{0,2},{1,3},{2,0},{3,1},{4,6},{5,7},{6,4},{7,5},{8,10},{9,11},{10,... | collective-permute-start | bytes 344072 | tf_op jit(solution)/shard_map/ppermute | solution.py:524
  37.0 0.9 %collective-permute-start.20 = (bf16[2,16,1792]{2,1,0:T(8,128)(2,1)S(1)}, bf16[2,16,1792]{2,1,0:T(8,128)(2,1)S(1)}, u32[]{:S(2)}, u32[]{:S(2)}) collective-permute-start(bf16[2,16,1792]{2,1,0:T(8,128)(2,1)S(1)} %get-tuple-element.66), channel_id=1, source_target_pairs={{0,2},{1,3},{2,0},{3,1},{4,6},{5,7},{6,4},{7,5},{8,10},{9,11},{10,... | collective-permute-start | bytes 344072 | tf_op jit(solution)/shard_map/ppermute | solution.py:524
  38.0 1.2 %collective-permute-start.11 = (bf16[16,3584]{1,0:T(8,128)(2,1)S(1)}, bf16[16,3584]{1,0:T(8,128)(2,1)S(1)}, u32[]{:S(2)}, u32[]{:S(2)}) collective-permute-start(bf16[16,3584]{1,0:T(8,128)(2,1)S(1)} %activate_near.1.refs_0_), channel_id=1, source_target_pairs={{0,2},{1,3},{2,0},{3,1},{4,6},{5,7},{6,4},{7,5},{8,10},{9,11},{10,... | collective-permute-start | bytes 344072 | tf_op jit(solution)/shard_map/ppermute | solution.py:524
  39.3 2.2 %collective-permute-done.14.refs_0_ = bf16[2,16,1792]{2,1,0:T(8,128)(2,1)S(1)} collective-permute-done((bf16[2,16,1792]{2,1,0:T(8,128)(2,1)S(1)}, bf16[2,16,1792]{2,1,0:T(8,128)(2,1)S(1)}, u32[]{:S(2)}, u32[]{:S(2)}) %collective-permute-start.14) | collective-permute-done | bytes 114720 | tf_op jit(solution)/shard_map/ppermute | solution.py:524
  41.6 1.5 %collective-permute-start.15 = (bf16[16,1792]{1,0:T(8,128)(2,1)S(1)}, bf16[16,1792]{1,0:T(8,128)(2,1)S(1)}, u32[]{:S(2)}, u32[]{:S(2)}) collective-permute-start(bf16[16,1792]{1,0:T(8,128)(2,1)S(1)} %activate_far_0.1.refs_4_.refs_1_), channel_id=1, source_target_pairs={{0,2},{1,3},{2,0},{3,1},{4,6},{5,7},{6,4},{7,5},{8,10},{9,11},{10,... | collective-permute-start | bytes 172040 | tf_op jit(solution)/shard_map/ppermute | solution.py:524
  44.0 1.5 %collective-permute-start.21 = (bf16[16,1792]{1,0:T(8,128)(2,1)S(1)}, bf16[16,1792]{1,0:T(8,128)(2,1)S(1)}, u32[]{:S(2)}, u32[]{:S(2)}) collective-permute-start(bf16[16,1792]{1,0:T(8,128)(2,1)S(1)} %activate_far_1.1.refs_8_.refs_2_), channel_id=1, source_target_pairs={{0,2},{1,3},{2,0},{3,1},{4,6},{5,7},{6,4},{7,5},{8,10},{9,11},{10,... | collective-permute-start | bytes 172040 | tf_op jit(solution)/shard_map/ppermute | solution.py:524
  49.5 2.9 %down.1 = (bf16[8,2048]{1,0:T(8,128)(2,1)S(1)}, bf16[8,2048]{1,0:T(8,128)(2,1)S(1)}, bf16[8,2048]{1,0:T(8,128)(2,1)S(1)}, bf16[8,2048]{1,0:T(8,128)(2,1)S(1)}, b...) custom-call(s32[2,4]{1,0:T(2,128)S(1)} %copy-done.3, ...), custom_call_target="tpu_custom_call" | custom-call | flops 49999998976 | bytes 50000000 | tf_op jit(solution)/shard_map/down/pallas_call | solution.py:429
  52.5 4.0 %collective-permute-start.29 = (bf16[16,2048]{1,0:T(8,128)(2,1)S(1)}, bf16[16,2048]{1,0:T(8,128)(2,1)S(1)}, u32[]{:S(2)}, u32[]{:S(2)}) collective-permute-start(bf16[16,2048]{1,0:T(8,128)(2,1)S(1)} %get-tuple-element.79), channel_id=1, source_target_pairs={{0,8},{4,12},{8,0},{12,4},{1,9},{5,13},{9,1},{13,5},{2,10},{6,14},... | collective-permute-start | bytes 196616 | tf_op jit(solution)/shard_map/ppermute | solution.py:528
  57.9 2.1 %collective-permute-start.25 = (bf16[2,8,2048]{2,1,0:T(8,128)(2,1)S(1)}, bf16[2,8,2048]{2,1,0:T(8,128)(2,1)S(1)}, u32[]{:S(2)}, u32[]{:S(2)}) collective-permute-start(bf16[2,8,2048]{2,1,0:T(8,128)(2,1)S(1)} %get-tuple-element.74), channel_id=1, source_target_pairs={{0,4},{4,8},{8,12},{12,0},{1,5},{5,9},{9,13},{13,1},{2,6},{6,10},{... | collective-permute-start | bytes 196616 | tf_op jit(solution)/shard_map/ppermute | solution.py:528
  60.0 2.7 %collective-permute-start.27 = (bf16[2,8,2048]{2,1,0:T(8,128)(2,1)S(1)}, bf16[2,8,2048]{2,1,0:T(8,128)(2,1)S(1)}, u32[]{:S(2)}, u32[]{:S(2)}) collective-permute-start(bf16[2,8,2048]{2,1,0:T(8,128)(2,1)S(1)} %get-tuple-element.76), channel_id=1, source_target_pairs={{0,12},{4,0},{8,4},{12,8},{1,13},{5,1},{9,5},{13,9},{2,14},{6,2},{... | collective-permute-start | bytes 196616 | tf_op jit(solution)/shard_map/ppermute | solution.py:528
  63.2 1.2 %collective-permute-start.31 = (bf16[8,2048]{1,0:T(8,128)(2,1)S(1)}, bf16[8,2048]{1,0:T(8,128)(2,1)S(1)}, u32[]{:S(2)}, u32[]{:S(2)}) collective-permute-start(bf16[8,2048]{1,0:T(8,128)(2,1)S(1)} %get-tuple-element.81.refs_4_), channel_id=1, source_target_pairs={{0,2},{1,3},{2,0},{3,1},{4,6},{5,7},{6,4},{7,5},{8,10},{9,11},{10,... | collective-permute-start | bytes 98312 | tf_op jit(solution)/shard_map/ppermute | solution.py:524
  64.7 2.3 %collective-permute-done.26.refs_2_ = bf16[2,8,2048]{2,1,0:T(8,128)(2,1)S(1)} collective-permute-done((bf16[2,8,2048]{2,1,0:T(8,128)(2,1)S(1)}, bf16[2,8,2048]{2,1,0:T(8,128)(2,1)S(1)}, u32[]{:S(2)}, u32[]{:S(2)}) %collective-permute-start.26) | collective-permute-done | bytes 65568 | tf_op jit(solution)/shard_map/ppermute | solution.py:528
  (78 shorter events, 11.7 us)
Async XLA Ops:
  5.4 4.9 %collective-permute-start = (bf16[8,2048]{1,0:T(8,128)(2,1)S(1)}, bf16[8,2048]{1,0:T(8,128)(2,1)S(1)}, u32[]{:S(2)}, u32[]{:S(2)}) collective-permute-start(bf16[8,2048]{1,0:T(8,128)(2,1)S(1)} %get-tuple-element.46), channel_id=1, source_target_pairs={{0,2},{1,3},{2,0},{3,1},{4,6},{5,7},{6,4},{7,5},{8,10},{9,11},{10,... | collective-permute-start | bytes 98312 | tf_op jit(solution)/shard_map/ppermute | solution.py:524
  12.4 7.5 %collective-permute-start.3 = (bf16[32,2048]{1,0:T(8,128)(2,1)S(1)}, bf16[32,2048]{1,0:T(8,128)(2,1)S(1)}, u32[]{:S(2)}, u32[]{:S(2)}) collective-permute-start(bf16[32,2048]{1,0:T(8,128)(2,1)S(1)} %pack.1.refs_0_), channel_id=1, source_target_pairs={{0,12},{4,0},{8,4},{12,8},{1,13},{5,1},{9,5},{13,9},{2,14},{6,2},{... | collective-permute-start | bytes 393224 | tf_op jit(solution)/shard_map/ppermute | solution.py:528
  16.0 9.8 %collective-permute-start.7 = (bf16[32,2048]{1,0:T(8,128)(2,1)S(1)}, bf16[32,2048]{1,0:T(8,128)(2,1)S(1)}, u32[]{:S(2)}, u32[]{:S(2)}) collective-permute-start(bf16[32,2048]{1,0:T(8,128)(2,1)S(1)} %pack.1.refs_0_), channel_id=1, source_target_pairs={{0,4},{4,8},{8,12},{12,0},{1,5},{5,9},{9,13},{13,1},{2,6},{6,10},{... | collective-permute-start | bytes 393224 | tf_op jit(solution)/shard_map/ppermute | solution.py:528
  16.0 12.1 %collective-permute-start.6 = (bf16[32,2048]{1,0:T(8,128)(2,1)S(1)}, bf16[32,2048]{1,0:T(8,128)(2,1)S(1)}, u32[]{:S(2)}, u32[]{:S(2)}) collective-permute-start(bf16[32,2048]{1,0:T(8,128)(2,1)S(1)} %pack.1.refs_0_), channel_id=1, source_target_pairs={{0,8},{4,12},{8,0},{12,4},{1,9},{5,13},{9,1},{13,5},{2,10},{6,14},... | collective-permute-start | bytes 393224 | tf_op jit(solution)/shard_map/ppermute | solution.py:528
  22.5 5.7 %collective-permute-start.4 = (bf16[2,32,1792]{2,1,0:T(8,128)(2,1)S(1)}, bf16[2,32,1792]{2,1,0:T(8,128)(2,1)S(1)}, u32[]{:S(2)}, u32[]{:S(2)}) collective-permute-start(bf16[2,32,1792]{2,1,0:T(8,128)(2,1)S(1)} %get-tuple-element.50), channel_id=1, source_target_pairs={{0,1},{1,0},{2,3},{3,2},{4,5},{5,4},{6,7},{7,6},{8,9},{9,8},{10,11... | collective-permute-start | bytes 688136 | tf_op jit(solution)/shard_map/ppermute | solution.py:524
  28.3 9.6 %collective-permute-start.8 = (bf16[2,16,3584]{2,1,0:T(8,128)(2,1)S(1)}, bf16[2,16,3584]{2,1,0:T(8,128)(2,1)S(1)}, u32[]{:S(2)}, u32[]{:S(2)}) collective-permute-start(bf16[2,16,3584]{2,1,0:T(8,128)(2,1)S(1)} %get-tuple-element.55), channel_id=1, source_target_pairs={{0,2},{1,3},{2,0},{3,1},{4,6},{5,7},{6,4},{7,5},{8,10},{9,11},{10,... | collective-permute-start | bytes 688136 | tf_op jit(solution)/shard_map/ppermute | solution.py:524
  31.5 3.8 %collective-permute-start.9 = (bf16[2,16,1792]{2,1,0:T(8,128)(2,1)S(1)}, bf16[2,16,1792]{2,1,0:T(8,128)(2,1)S(1)}, u32[]{:S(2)}, u32[]{:S(2)}) collective-permute-start(bf16[2,16,1792]{2,1,0:T(8,128)(2,1)S(1)} %get-tuple-element.57), channel_id=1, source_target_pairs={{0,1},{1,0},{2,3},{3,2},{4,5},{5,4},{6,7},{7,6},{8,9},{9,8},{10,11... | collective-permute-start | bytes 344072 | tf_op jit(solution)/shard_map/ppermute | solution.py:524
  31.6 3.7 %collective-permute-start.10 = (bf16[2,16,1792]{2,1,0:T(8,128)(2,1)S(1)}, bf16[2,16,1792]{2,1,0:T(8,128)(2,1)S(1)}, u32[]{:S(2)}, u32[]{:S(2)}) collective-permute-start(bf16[2,16,1792]{2,1,0:T(8,128)(2,1)S(1)} %get-tuple-element.58), channel_id=1, source_target_pairs={{0,1},{1,0},{2,3},{3,2},{4,5},{5,4},{6,7},{7,6},{8,9},{9,8},{10,11... | collective-permute-start | bytes 344072 | tf_op jit(solution)/shard_map/ppermute | solution.py:524
  35.4 6.1 %collective-permute-start.14 = (bf16[2,16,1792]{2,1,0:T(8,128)(2,1)S(1)}, bf16[2,16,1792]{2,1,0:T(8,128)(2,1)S(1)}, u32[]{:S(2)}, u32[]{:S(2)}) collective-permute-start(bf16[2,16,1792]{2,1,0:T(8,128)(2,1)S(1)} %get-tuple-element.60), channel_id=1, source_target_pairs={{0,2},{1,3},{2,0},{3,1},{4,6},{5,7},{6,4},{7,5},{8,10},{9,11},{10,... | collective-permute-start | bytes 344072 | tf_op jit(solution)/shard_map/ppermute | solution.py:524
  37.0 6.9 %collective-permute-start.20 = (bf16[2,16,1792]{2,1,0:T(8,128)(2,1)S(1)}, bf16[2,16,1792]{2,1,0:T(8,128)(2,1)S(1)}, u32[]{:S(2)}, u32[]{:S(2)}) collective-permute-start(bf16[2,16,1792]{2,1,0:T(8,128)(2,1)S(1)} %get-tuple-element.66), channel_id=1, source_target_pairs={{0,2},{1,3},{2,0},{3,1},{4,6},{5,7},{6,4},{7,5},{8,10},{9,11},{10,... | collective-permute-start | bytes 344072 | tf_op jit(solution)/shard_map/ppermute | solution.py:524
  38.0 8.1 %collective-permute-start.11 = (bf16[16,3584]{1,0:T(8,128)(2,1)S(1)}, bf16[16,3584]{1,0:T(8,128)(2,1)S(1)}, u32[]{:S(2)}, u32[]{:S(2)}) collective-permute-start(bf16[16,3584]{1,0:T(8,128)(2,1)S(1)} %activate_near.1.refs_0_), channel_id=1, source_target_pairs={{0,2},{1,3},{2,0},{3,1},{4,6},{5,7},{6,4},{7,5},{8,10},{9,11},{10,... | collective-permute-start | bytes 344072 | tf_op jit(solution)/shard_map/ppermute | solution.py:524
  39.3 8.9 %collective-permute-start.12 = (bf16[16,3584]{1,0:T(8,128)(2,1)S(1)}, bf16[16,3584]{1,0:T(8,128)(2,1)S(1)}, u32[]{:S(2)}, u32[]{:S(2)}) collective-permute-start(bf16[16,3584]{1,0:T(8,128)(2,1)S(1)} %activate_near.1.refs_0_), channel_id=1, source_target_pairs={{0,1},{1,0},{2,3},{3,2},{4,5},{5,4},{6,7},{7,6},{8,9},{9,8},{10,11... | collective-permute-start | bytes 344072 | tf_op jit(solution)/shard_map/ppermute | solution.py:524
  41.5 4.6 %collective-permute-start.16 = (bf16[16,1792]{1,0:T(8,128)(2,1)S(1)}, bf16[16,1792]{1,0:T(8,128)(2,1)S(1)}, u32[]{:S(2)}, u32[]{:S(2)}) collective-permute-start(bf16[16,1792]{1,0:T(8,128)(2,1)S(1)} %activate_far_0.1.refs_4_.refs_1_), channel_id=1, source_target_pairs={{0,1},{1,0},{2,3},{3,2},{4,5},{5,4},{6,7},{7,6},{8,9},{9,8},{10,11... | collective-permute-start | bytes 172040 | tf_op jit(solution)/shard_map/ppermute | solution.py:524
  41.6 5.7 %collective-permute-start.15 = (bf16[16,1792]{1,0:T(8,128)(2,1)S(1)}, bf16[16,1792]{1,0:T(8,128)(2,1)S(1)}, u32[]{:S(2)}, u32[]{:S(2)}) collective-permute-start(bf16[16,1792]{1,0:T(8,128)(2,1)S(1)} %activate_far_0.1.refs_4_.refs_1_), channel_id=1, source_target_pairs={{0,2},{1,3},{2,0},{3,1},{4,6},{5,7},{6,4},{7,5},{8,10},{9,11},{10,... | collective-permute-start | bytes 172040 | tf_op jit(solution)/shard_map/ppermute | solution.py:524
  44.0 4.2 %collective-permute-start.21 = (bf16[16,1792]{1,0:T(8,128)(2,1)S(1)}, bf16[16,1792]{1,0:T(8,128)(2,1)S(1)}, u32[]{:S(2)}, u32[]{:S(2)}) collective-permute-start(bf16[16,1792]{1,0:T(8,128)(2,1)S(1)} %activate_far_1.1.refs_8_.refs_2_), channel_id=1, source_target_pairs={{0,2},{1,3},{2,0},{3,1},{4,6},{5,7},{6,4},{7,5},{8,10},{9,11},{10,... | collective-permute-start | bytes 172040 | tf_op jit(solution)/shard_map/ppermute | solution.py:524
  46.1 3.3 %collective-permute-start.13 = (bf16[16,3584]{1,0:T(8,128)(2,1)S(1)}, bf16[16,3584]{1,0:T(8,128)(2,1)S(1)}, u32[]{:S(2)}, u32[]{:S(2)}) collective-permute-start(bf16[16,3584]{1,0:T(8,128)(2,1)S(1)} %collective-permute-done.11.refs_1_), channel_id=1, source_target_pairs={{0,1},{1,0},{2,3},{3,2},{4,5},{5,4},{6,7},{7,6},{8,9},{9,8},{10,11... | collective-permute-start | bytes 344072 | tf_op jit(solution)/shard_map/ppermute | solution.py:524
  52.4 7.5 %collective-permute-start.28 = (bf16[16,2048]{1,0:T(8,128)(2,1)S(1)}, bf16[16,2048]{1,0:T(8,128)(2,1)S(1)}, u32[]{:S(2)}, u32[]{:S(2)}) collective-permute-start(bf16[16,2048]{1,0:T(8,128)(2,1)S(1)} %get-tuple-element.78), channel_id=1, source_target_pairs={{0,4},{4,8},{8,12},{12,0},{1,5},{5,9},{9,13},{13,1},{2,6},{6,10},{... | collective-permute-start | bytes 196616 | tf_op jit(solution)/shard_map/ppermute | solution.py:528
  52.5 10.2 %collective-permute-start.29 = (bf16[16,2048]{1,0:T(8,128)(2,1)S(1)}, bf16[16,2048]{1,0:T(8,128)(2,1)S(1)}, u32[]{:S(2)}, u32[]{:S(2)}) collective-permute-start(bf16[16,2048]{1,0:T(8,128)(2,1)S(1)} %get-tuple-element.79), channel_id=1, source_target_pairs={{0,8},{4,12},{8,0},{12,4},{1,9},{5,13},{9,1},{13,5},{2,10},{6,14},... | collective-permute-start | bytes 196616 | tf_op jit(solution)/shard_map/ppermute | solution.py:528
  56.5 6.2 %collective-permute-start.30 = (bf16[16,2048]{1,0:T(8,128)(2,1)S(1)}, bf16[16,2048]{1,0:T(8,128)(2,1)S(1)}, u32[]{:S(2)}, u32[]{:S(2)}) collective-permute-start(bf16[16,2048]{1,0:T(8,128)(2,1)S(1)} %get-tuple-element.80), channel_id=1, source_target_pairs={{0,12},{4,0},{8,4},{12,8},{1,13},{5,1},{9,5},{13,9},{2,14},{6,2},{... | collective-permute-start | bytes 196616 | tf_op jit(solution)/shard_map/ppermute | solution.py:528
  57.9 6.8 %collective-permute-start.25 = (bf16[2,8,2048]{2,1,0:T(8,128)(2,1)S(1)}, bf16[2,8,2048]{2,1,0:T(8,128)(2,1)S(1)}, u32[]{:S(2)}, u32[]{:S(2)}) collective-permute-start(bf16[2,8,2048]{2,1,0:T(8,128)(2,1)S(1)} %get-tuple-element.74), channel_id=1, source_target_pairs={{0,4},{4,8},{8,12},{12,0},{1,5},{5,9},{9,13},{13,1},{2,6},{6,10},{... | collective-permute-start | bytes 196616 | tf_op jit(solution)/shard_map/ppermute | solution.py:528
  59.9 7.0 %collective-permute-start.26 = (bf16[2,8,2048]{2,1,0:T(8,128)(2,1)S(1)}, bf16[2,8,2048]{2,1,0:T(8,128)(2,1)S(1)}, u32[]{:S(2)}, u32[]{:S(2)}) collective-permute-start(bf16[2,8,2048]{2,1,0:T(8,128)(2,1)S(1)} %get-tuple-element.75), channel_id=1, source_target_pairs={{0,8},{4,12},{8,0},{12,4},{1,9},{5,13},{9,1},{13,5},{2,10},{6,14},... | collective-permute-start | bytes 196616 | tf_op jit(solution)/shard_map/ppermute | solution.py:528
  60.0 7.0 %collective-permute-start.27 = (bf16[2,8,2048]{2,1,0:T(8,128)(2,1)S(1)}, bf16[2,8,2048]{2,1,0:T(8,128)(2,1)S(1)}, u32[]{:S(2)}, u32[]{:S(2)}) collective-permute-start(bf16[2,8,2048]{2,1,0:T(8,128)(2,1)S(1)} %get-tuple-element.76), channel_id=1, source_target_pairs={{0,12},{4,0},{8,4},{12,8},{1,13},{5,1},{9,5},{13,9},{2,14},{6,2},{... | collective-permute-start | bytes 196616 | tf_op jit(solution)/shard_map/ppermute | solution.py:528
  62.7 4.3 %collective-permute-start.32 = (bf16[8,2048]{1,0:T(8,128)(2,1)S(1)}, bf16[8,2048]{1,0:T(8,128)(2,1)S(1)}, u32[]{:S(2)}, u32[]{:S(2)}) collective-permute-start(bf16[8,2048]{1,0:T(8,128)(2,1)S(1)} %get-tuple-element.84), channel_id=1, source_target_pairs={{0,3},{1,2},{2,1},{3,0},{4,7},{5,6},{6,5},{7,4},{8,11},{9,10},{10,... | collective-permute-start | bytes 98312 | tf_op jit(solution)/shard_map/ppermute | solution.py:524
  63.2 4.0 %collective-permute-start.31 = (bf16[8,2048]{1,0:T(8,128)(2,1)S(1)}, bf16[8,2048]{1,0:T(8,128)(2,1)S(1)}, u32[]{:S(2)}, u32[]{:S(2)}) collective-permute-start(bf16[8,2048]{1,0:T(8,128)(2,1)S(1)} %get-tuple-element.81.refs_4_), channel_id=1, source_target_pairs={{0,2},{1,3},{2,0},{3,1},{4,6},{5,7},{6,4},{7,5},{8,10},{9,11},{10,... | collective-permute-start | bytes 98312 | tf_op jit(solution)/shard_map/ppermute | solution.py:524
  (17 other events, 131.5 us)

commit v6 on v5

--- a/solution.py
+++ b/solution.py
@@ -587,7 +587,7 @@
     blocks = [[collect(part) for part in group] for group in hiddens]
     served, placed = serve(batches, rows, hiddens)
     mine, peers, other = down(cols, "down", batches, rows, partner_table, blocks, down_weight, [])
-    other = [other[0]] + [turn(other[s], ffn, s) for s in range(1, ffn)]
+    other = [other[0]] + [turn(other[s], ffn, s) for s in sorted(range(1, ffn), key=lambda s: [2, 1, 3].index(s) if s < 4 else s)]
     same = merge(
         mine, [to_column(cols, peer, dr + 1, 0) for dr, peer in enumerate(peers)], [placed]
     )

time: 68.1 us -> 68 us (level)
  starting transfers between devices: 28.2 us -> 26.5 us
  waiting for transfers between devices: 18.1 us -> 19.6 us
    ppermute x9, waiting for transfers between devices: 7.79 us -> 9.55 us  [turn(): lax.ppermute(value, 'ffn', [(i, (i + shift) % ffn) for i in range(ffn)])]
    ppermute x9, starting transfers between devices: 13.5 us -> 12.2 us  [turn(): lax.ppermute(value, 'ffn', [(i, (i + shift) % ffn) for i in range(ffn)])]
where the time goes in v6:
time: 68 us; the launch traced here: 67.8 us
  starting transfers between devices  26.5 us (39%)
  Pallas kernels  20.9 us (31%)
  waiting for transfers between devices  19.6 us (29%)
  between operations  0.87 us (1%)
    ppermute x24, starting transfers between devices, to_column(): return lax.ppermute(value, ('pair', 'rep'), route)  14.3 us
    ppermute x9, starting transfers between devices, turn(): lax.ppermute(value, 'ffn', [(i, (i + shift) % ffn) for i in range(ffn)])  12.2 us
    pallas_call x4, Pallas kernels, gate_up(): pl.pallas_call(functools.partial(gate_up_kernel, pairs * reps, len(packs)...  10.5 us
    ppermute x24, waiting for transfers between devices, to_column(): return lax.ppermute(value, ('pair', 'rep'), route)  10 us
    ppermute x9, waiting for transfers between devices, turn(): lax.ppermute(value, 'ffn', [(i, (i + shift) % ffn) for i in range(ffn)])  9.55 us
    pallas_call x1, Pallas kernels, attend(): pl.pallas_call(functools.partial(attend_kernel, cols, kvh, heads_per_step...  4.69 us
    pallas_call x1, Pallas kernels, down(): pl.pallas_call(functools.partial(down_kernel, cols, batches, rows, sizes,...  2.94 us
  transfers between devices with their start and end apart: 33, of which 15 were waited for; matrix products, arithmetic and copies ran while one was open for 0% of the time, Pallas kernels for 17%

profile of v6, /device:TPU:0, one launch (start us, length us, event | category | flops | bytes accessed | tf_op | source)
XLA Modules:
  0.0 67.8 jit_solution(12413773994654908109)
XLA Ops:
  0.7 4.7 %attend.1 = (f32[8,8192]{1,0:T(8,128)S(1)}, bf16[8,2048]{1,0:T(8,128)(2,1)S(1)}, bf16[8,2048]{1,0:T(8,128)(2,1)S(1)}, bf16[8,2048]{1,0:T(8,128)(2,1)S(1)}, bf16[8,2048]{1,0:T(8,128)(2,1)S(1)}) custom-call(s32[2,1,4]{2,1,0:T(1,128)} %len_ref.1, bf16[2,4,8192]{2,1,0:T(4,128)(2,1)} %bitcast.10, bf16[1024,1024]{1,0:T(8,128)(2,1)} %bitcast.7, ...), custom_call_target="tpu_custom_call" | custom-call | flops 99999997952 | bytes 100000000 | tf_op jit(solution)/shard_map/attend/pallas_call | solution.py:134
  5.4 3.0 %collective-permute-start = (bf16[8,2048]{1,0:T(8,128)(2,1)S(1)}, bf16[8,2048]{1,0:T(8,128)(2,1)S(1)}, u32[]{:S(2)}, u32[]{:S(2)}) collective-permute-start(bf16[8,2048]{1,0:T(8,128)(2,1)S(1)} %get-tuple-element.46), channel_id=1, source_target_pairs={{0,2},{1,3},{2,0},{3,1},{4,6},{5,7},{6,4},{7,5},{8,10},{9,11},{10,... | collective-permute-start | bytes 98312 | tf_op jit(solution)/shard_map/ppermute | solution.py:524
  8.6 1.7 %collective-permute-done.refs_1_ = bf16[8,2048]{1,0:T(8,128)(2,1)S(1)} collective-permute-done((bf16[8,2048]{1,0:T(8,128)(2,1)S(1)}, bf16[8,2048]{1,0:T(8,128)(2,1)S(1)}, u32[]{:S(2)}, u32[]{:S(2)}) %collective-permute-start) | collective-permute-done | bytes 32800 | tf_op jit(solution)/shard_map/ppermute | solution.py:524
  10.3 1.4 %collective-permute-done.2.refs_3_ = bf16[8,2048]{1,0:T(8,128)(2,1)S(1)} collective-permute-done((bf16[8,2048]{1,0:T(8,128)(2,1)S(1)}, bf16[8,2048]{1,0:T(8,128)(2,1)S(1)}, u32[]{:S(2)}, u32[]{:S(2)}) %collective-permute-start.2) | collective-permute-done | bytes 32800 | tf_op jit(solution)/shard_map/ppermute | solution.py:524
  12.4 3.6 %collective-permute-start.3 = (bf16[32,2048]{1,0:T(8,128)(2,1)S(1)}, bf16[32,2048]{1,0:T(8,128)(2,1)S(1)}, u32[]{:S(2)}, u32[]{:S(2)}) collective-permute-start(bf16[32,2048]{1,0:T(8,128)(2,1)S(1)} %pack.1.refs_0_), channel_id=1, source_target_pairs={{0,12},{4,0},{8,4},{12,8},{1,13},{5,1},{9,5},{13,9},{2,14},{6,2},{... | collective-permute-start | bytes 393224 | tf_op jit(solution)/shard_map/ppermute | solution.py:528
  16.0 1.0 %collective-permute-start.6 = (bf16[32,2048]{1,0:T(8,128)(2,1)S(1)}, bf16[32,2048]{1,0:T(8,128)(2,1)S(1)}, u32[]{:S(2)}, u32[]{:S(2)}) collective-permute-start(bf16[32,2048]{1,0:T(8,128)(2,1)S(1)} %pack.1.refs_0_), channel_id=1, source_target_pairs={{0,8},{4,12},{8,0},{12,4},{1,9},{5,13},{9,1},{13,5},{2,10},{6,14},... | collective-permute-start | bytes 393224 | tf_op jit(solution)/shard_map/ppermute | solution.py:528
  17.0 2.8 %collective-permute-done.3.refs_1_ = bf16[32,2048]{1,0:T(8,128)(2,1)S(1)} collective-permute-done((bf16[32,2048]{1,0:T(8,128)(2,1)S(1)}, bf16[32,2048]{1,0:T(8,128)(2,1)S(1)}, u32[]{:S(2)}, u32[]{:S(2)}) %collective-permute-start.3) | collective-permute-done | bytes 131104 | tf_op jit(solution)/shard_map/ppermute | solution.py:528
  19.9 2.6 %gate_up_near_0.1 = (bf16[64,2048]{1,0:T(8,128)(2,1)S(1)}, f32[2,32,1792]{2,1,0:T(8,128)S(1)}, bf16[2,32,1792]{2,1,0:T(8,128)(2,1)S(1)}) custom-call(bf16[2048,3584]{1,0:T(8,128)(2,1)S(1)} %copy-done, bf16[2048,3584]{1,0:T(8,128)(2,1)S(1)} %copy-done.1, bf16[32,2048]{1,0:T(8,128)(2,1)S(1)} %pack.1.refs_0_, bf16[32,2048]{1,0:T(8,128)(2,1)S(1)} %collective-permute-done.3.refs_1_), custom_call_target="tpu_custom_call" | custom-call | flops 49999998976 | bytes 50000000 | tf_op jit(solution)/shard_map/gate_up_near_0/pallas_call | solution.py:226
  22.6 2.6 %gate_up_near_1.1 = (f32[2,32,1792]{2,1,0:T(8,128)S(1)}, bf16[2,32,1792]{2,1,0:T(8,128)(2,1)S(1)}) custom-call(bf16[2048,3584]{1,0:T(8,128)(2,1)S(1)} %copy-done, bf16[2048,3584]{1,0:T(8,128)(2,1)S(1)} %copy-done.1, bf16[64,2048]{1,0:T(8,128)(2,1)S(1)} %get-tuple-element.51.refs_0_), custom_call_target="tpu_custom_call" | custom-call | flops 49999998976 | bytes 50000000 | tf_op jit(solution)/shard_map/gate_up_near_1/pallas_call | solution.py:226
  25.8 2.4 %collective-permute-done.6.refs_0_ = bf16[32,2048]{1,0:T(8,128)(2,1)S(1)} collective-permute-done((bf16[32,2048]{1,0:T(8,128)(2,1)S(1)}, bf16[32,2048]{1,0:T(8,128)(2,1)S(1)}, u32[]{:S(2)}, u32[]{:S(2)}) %collective-permute-start.6) | collective-permute-done | bytes 131104 | tf_op jit(solution)/shard_map/ppermute | solution.py:528
  28.9 2.6 %gate_up_far_0.1 = (bf16[64,2048]{1,0:T(8,128)(2,1)S(1)}, f32[2,32,1792]{2,1,0:T(8,128)S(1)}, bf16[2,16,1792]{2,1,0:T(8,128)(2,1)S(1)}, bf16[2,16,1792]{2,1,0:T(8,128)(2,1)S(1)}) custom-call(bf16[2048,3584]{1,0:T(8,128)(2,1)S(1)} %copy-done, bf16[2048,3584]{1,0:T(8,128)(2,1)S(1)} %copy-done.1, bf16[32,2048]{1,0:T(8,128)(2,1)S(1)} %collective-permute-done.6.refs_0_, ...), custom_call_target="tpu_custom_call" | custom-call | flops 49999998976 | bytes 50000000 | tf_op jit(solution)/shard_map/gate_up_far_0/pallas_call | solution.py:226
  32.1 2.6 %gate_up_far_1.1 = (f32[2,32,1792]{2,1,0:T(8,128)S(1)}, bf16[2,16,1792]{2,1,0:T(8,128)(2,1)S(1)}, bf16[2,16,1792]{2,1,0:T(8,128)(2,1)S(1)}) custom-call(bf16[2048,3584]{1,0:T(8,128)(2,1)S(1)} %copy-done, bf16[2048,3584]{1,0:T(8,128)(2,1)S(1)} %copy-done.1, bf16[64,2048]{1,0:T(8,128)(2,1)S(1)} %get-tuple-element.61.refs_0_), custom_call_target="tpu_custom_call" | custom-call | flops 1000000 | bytes 1000 | tf_op jit(solution)/shard_map/gate_up_far_1/pallas_call | solution.py:226
  35.4 1.5 %collective-permute-start.14 = (bf16[2,16,1792]{2,1,0:T(8,128)(2,1)S(1)}, bf16[2,16,1792]{2,1,0:T(8,128)(2,1)S(1)}, u32[]{:S(2)}, u32[]{:S(2)}) collective-permute-start(bf16[2,16,1792]{2,1,0:T(8,128)(2,1)S(1)} %get-tuple-element.60), channel_id=1, source_target_pairs={{0,2},{1,3},{2,0},{3,1},{4,6},{5,7},{6,4},{7,5},{8,10},{9,11},{10,... | collective-permute-start | bytes 344072 | tf_op jit(solution)/shard_map/ppermute | solution.py:524
  38.0 1.2 %collective-permute-start.11 = (bf16[16,3584]{1,0:T(8,128)(2,1)S(1)}, bf16[16,3584]{1,0:T(8,128)(2,1)S(1)}, u32[]{:S(2)}, u32[]{:S(2)}) collective-permute-start(bf16[16,3584]{1,0:T(8,128)(2,1)S(1)} %activate_near.1.refs_0_), channel_id=1, source_target_pairs={{0,2},{1,3},{2,0},{3,1},{4,6},{5,7},{6,4},{7,5},{8,10},{9,11},{10,... | collective-permute-start | bytes 344072 | tf_op jit(solution)/shard_map/ppermute | solution.py:524
  39.3 2.2 %collective-permute-done.14.refs_0_ = bf16[2,16,1792]{2,1,0:T(8,128)(2,1)S(1)} collective-permute-done((bf16[2,16,1792]{2,1,0:T(8,128)(2,1)S(1)}, bf16[2,16,1792]{2,1,0:T(8,128)(2,1)S(1)}, u32[]{:S(2)}, u32[]{:S(2)}) %collective-permute-start.14) | collective-permute-done | bytes 114720 | tf_op jit(solution)/shard_map/ppermute | solution.py:524
  41.6 1.5 %collective-permute-start.15 = (bf16[16,1792]{1,0:T(8,128)(2,1)S(1)}, bf16[16,1792]{1,0:T(8,128)(2,1)S(1)}, u32[]{:S(2)}, u32[]{:S(2)}) collective-permute-start(bf16[16,1792]{1,0:T(8,128)(2,1)S(1)} %activate_far_0.1.refs_4_.refs_1_), channel_id=1, source_target_pairs={{0,2},{1,3},{2,0},{3,1},{4,6},{5,7},{6,4},{7,5},{8,10},{9,11},{10,... | collective-permute-start | bytes 172040 | tf_op jit(solution)/shard_map/ppermute | solution.py:524
  44.0 1.5 %collective-permute-start.21 = (bf16[16,1792]{1,0:T(8,128)(2,1)S(1)}, bf16[16,1792]{1,0:T(8,128)(2,1)S(1)}, u32[]{:S(2)}, u32[]{:S(2)}) collective-permute-start(bf16[16,1792]{1,0:T(8,128)(2,1)S(1)} %activate_far_1.1.refs_8_.refs_2_), channel_id=1, source_target_pairs={{0,2},{1,3},{2,0},{3,1},{4,6},{5,7},{6,4},{7,5},{8,10},{9,11},{10,... | collective-permute-start | bytes 172040 | tf_op jit(solution)/shard_map/ppermute | solution.py:524
  49.5 2.9 %down.1 = (bf16[8,2048]{1,0:T(8,128)(2,1)S(1)}, bf16[8,2048]{1,0:T(8,128)(2,1)S(1)}, bf16[8,2048]{1,0:T(8,128)(2,1)S(1)}, bf16[8,2048]{1,0:T(8,128)(2,1)S(1)}, b...) custom-call(s32[2,4]{1,0:T(2,128)S(1)} %copy-done.3, ...), custom_call_target="tpu_custom_call" | custom-call | flops 49999998976 | bytes 50000000 | tf_op jit(solution)/shard_map/down/pallas_call | solution.py:429
  52.9 3.6 %collective-permute-start.29 = (bf16[16,2048]{1,0:T(8,128)(2,1)S(1)}, bf16[16,2048]{1,0:T(8,128)(2,1)S(1)}, u32[]{:S(2)}, u32[]{:S(2)}) collective-permute-start(bf16[16,2048]{1,0:T(8,128)(2,1)S(1)} %get-tuple-element.79), channel_id=1, source_target_pairs={{0,4},{4,8},{8,12},{12,0},{1,5},{5,9},{9,13},{13,1},{2,6},{6,10},{... | collective-permute-start | bytes 196616 | tf_op jit(solution)/shard_map/ppermute | solution.py:528
  58.1 1.8 %collective-permute-start.25 = (bf16[2,8,2048]{2,1,0:T(8,128)(2,1)S(1)}, bf16[2,8,2048]{2,1,0:T(8,128)(2,1)S(1)}, u32[]{:S(2)}, u32[]{:S(2)}) collective-permute-start(bf16[2,8,2048]{2,1,0:T(8,128)(2,1)S(1)} %get-tuple-element.74), channel_id=1, source_target_pairs={{0,4},{4,8},{8,12},{12,0},{1,5},{5,9},{9,13},{13,1},{2,6},{6,10},{... | collective-permute-start | bytes 196616 | tf_op jit(solution)/shard_map/ppermute | solution.py:528
  60.0 1.1 %collective-permute-done.28.refs_1_ = bf16[16,2048]{1,0:T(8,128)(2,1)S(1)} collective-permute-done((bf16[16,2048]{1,0:T(8,128)(2,1)S(1)}, bf16[16,2048]{1,0:T(8,128)(2,1)S(1)}, u32[]{:S(2)}, u32[]{:S(2)}) %collective-permute-start.28) | collective-permute-done | bytes 65568 | tf_op jit(solution)/shard_map/ppermute | solution.py:528
  61.1 1.3 %collective-permute-start.27 = (bf16[2,8,2048]{2,1,0:T(8,128)(2,1)S(1)}, bf16[2,8,2048]{2,1,0:T(8,128)(2,1)S(1)}, u32[]{:S(2)}, u32[]{:S(2)}) collective-permute-start(bf16[2,8,2048]{2,1,0:T(8,128)(2,1)S(1)} %get-tuple-element.76), channel_id=1, source_target_pairs={{0,12},{4,0},{8,4},{12,8},{1,13},{5,1},{9,5},{13,9},{2,14},{6,2},{... | collective-permute-start | bytes 196616 | tf_op jit(solution)/shard_map/ppermute | solution.py:528
  63.7 1.2 %collective-permute-done.25.refs_1_ = bf16[2,8,2048]{2,1,0:T(8,128)(2,1)S(1)} collective-permute-done((bf16[2,8,2048]{2,1,0:T(8,128)(2,1)S(1)}, bf16[2,8,2048]{2,1,0:T(8,128)(2,1)S(1)}, u32[]{:S(2)}, u32[]{:S(2)}) %collective-permute-start.25) | collective-permute-done | bytes 65568 | tf_op jit(solution)/shard_map/ppermute | solution.py:528
  64.9 2.1 %collective-permute-done.26.refs_2_ = bf16[2,8,2048]{2,1,0:T(8,128)(2,1)S(1)} collective-permute-done((bf16[2,8,2048]{2,1,0:T(8,128)(2,1)S(1)}, bf16[2,8,2048]{2,1,0:T(8,128)(2,1)S(1)}, u32[]{:S(2)}, u32[]{:S(2)}) %collective-permute-start.26) | collective-permute-done | bytes 65568 | tf_op jit(solution)/shard_map/ppermute | solution.py:528
  (78 shorter events, 13.7 us)
Async XLA Ops:
  5.4 4.9 %collective-permute-start = (bf16[8,2048]{1,0:T(8,128)(2,1)S(1)}, bf16[8,2048]{1,0:T(8,128)(2,1)S(1)}, u32[]{:S(2)}, u32[]{:S(2)}) collective-permute-start(bf16[8,2048]{1,0:T(8,128)(2,1)S(1)} %get-tuple-element.46), channel_id=1, source_target_pairs={{0,2},{1,3},{2,0},{3,1},{4,6},{5,7},{6,4},{7,5},{8,10},{9,11},{10,... | collective-permute-start | bytes 98312 | tf_op jit(solution)/shard_map/ppermute | solution.py:524
  12.4 7.5 %collective-permute-start.3 = (bf16[32,2048]{1,0:T(8,128)(2,1)S(1)}, bf16[32,2048]{1,0:T(8,128)(2,1)S(1)}, u32[]{:S(2)}, u32[]{:S(2)}) collective-permute-start(bf16[32,2048]{1,0:T(8,128)(2,1)S(1)} %pack.1.refs_0_), channel_id=1, source_target_pairs={{0,12},{4,0},{8,4},{12,8},{1,13},{5,1},{9,5},{13,9},{2,14},{6,2},{... | collective-permute-start | bytes 393224 | tf_op jit(solution)/shard_map/ppermute | solution.py:528
  16.0 9.8 %collective-permute-start.7 = (bf16[32,2048]{1,0:T(8,128)(2,1)S(1)}, bf16[32,2048]{1,0:T(8,128)(2,1)S(1)}, u32[]{:S(2)}, u32[]{:S(2)}) collective-permute-start(bf16[32,2048]{1,0:T(8,128)(2,1)S(1)} %pack.1.refs_0_), channel_id=1, source_target_pairs={{0,4},{4,8},{8,12},{12,0},{1,5},{5,9},{9,13},{13,1},{2,6},{6,10},{... | collective-permute-start | bytes 393224 | tf_op jit(solution)/shard_map/ppermute | solution.py:528
  16.0 12.1 %collective-permute-start.6 = (bf16[32,2048]{1,0:T(8,128)(2,1)S(1)}, bf16[32,2048]{1,0:T(8,128)(2,1)S(1)}, u32[]{:S(2)}, u32[]{:S(2)}) collective-permute-start(bf16[32,2048]{1,0:T(8,128)(2,1)S(1)} %pack.1.refs_0_), channel_id=1, source_target_pairs={{0,8},{4,12},{8,0},{12,4},{1,9},{5,13},{9,1},{13,5},{2,10},{6,14},... | collective-permute-start | bytes 393224 | tf_op jit(solution)/shard_map/ppermute | solution.py:528
  22.5 5.7 %collective-permute-start.4 = (bf16[2,32,1792]{2,1,0:T(8,128)(2,1)S(1)}, bf16[2,32,1792]{2,1,0:T(8,128)(2,1)S(1)}, u32[]{:S(2)}, u32[]{:S(2)}) collective-permute-start(bf16[2,32,1792]{2,1,0:T(8,128)(2,1)S(1)} %get-tuple-element.50), channel_id=1, source_target_pairs={{0,1},{1,0},{2,3},{3,2},{4,5},{5,4},{6,7},{7,6},{8,9},{9,8},{10,11... | collective-permute-start | bytes 688136 | tf_op jit(solution)/shard_map/ppermute | solution.py:524
  28.3 9.6 %collective-permute-start.8 = (bf16[2,16,3584]{2,1,0:T(8,128)(2,1)S(1)}, bf16[2,16,3584]{2,1,0:T(8,128)(2,1)S(1)}, u32[]{:S(2)}, u32[]{:S(2)}) collective-permute-start(bf16[2,16,3584]{2,1,0:T(8,128)(2,1)S(1)} %get-tuple-element.55), channel_id=1, source_target_pairs={{0,2},{1,3},{2,0},{3,1},{4,6},{5,7},{6,4},{7,5},{8,10},{9,11},{10,... | collective-permute-start | bytes 688136 | tf_op jit(solution)/shard_map/ppermute | solution.py:524
  31.5 3.8 %collective-permute-start.9 = (bf16[2,16,1792]{2,1,0:T(8,128)(2,1)S(1)}, bf16[2,16,1792]{2,1,0:T(8,128)(2,1)S(1)}, u32[]{:S(2)}, u32[]{:S(2)}) collective-permute-start(bf16[2,16,1792]{2,1,0:T(8,128)(2,1)S(1)} %get-tuple-element.57), channel_id=1, source_target_pairs={{0,1},{1,0},{2,3},{3,2},{4,5},{5,4},{6,7},{7,6},{8,9},{9,8},{10,11... | collective-permute-start | bytes 344072 | tf_op jit(solution)/shard_map/ppermute | solution.py:524
  31.6 3.7 %collective-permute-start.10 = (bf16[2,16,1792]{2,1,0:T(8,128)(2,1)S(1)}, bf16[2,16,1792]{2,1,0:T(8,128)(2,1)S(1)}, u32[]{:S(2)}, u32[]{:S(2)}) collective-permute-start(bf16[2,16,1792]{2,1,0:T(8,128)(2,1)S(1)} %get-tuple-element.58), channel_id=1, source_target_pairs={{0,1},{1,0},{2,3},{3,2},{4,5},{5,4},{6,7},{7,6},{8,9},{9,8},{10,11... | collective-permute-start | bytes 344072 | tf_op jit(solution)/shard_map/ppermute | solution.py:524
  35.4 6.1 %collective-permute-start.14 = (bf16[2,16,1792]{2,1,0:T(8,128)(2,1)S(1)}, bf16[2,16,1792]{2,1,0:T(8,128)(2,1)S(1)}, u32[]{:S(2)}, u32[]{:S(2)}) collective-permute-start(bf16[2,16,1792]{2,1,0:T(8,128)(2,1)S(1)} %get-tuple-element.60), channel_id=1, source_target_pairs={{0,2},{1,3},{2,0},{3,1},{4,6},{5,7},{6,4},{7,5},{8,10},{9,11},{10,... | collective-permute-start | bytes 344072 | tf_op jit(solution)/shard_map/ppermute | solution.py:524
  37.0 6.9 %collective-permute-start.20 = (bf16[2,16,1792]{2,1,0:T(8,128)(2,1)S(1)}, bf16[2,16,1792]{2,1,0:T(8,128)(2,1)S(1)}, u32[]{:S(2)}, u32[]{:S(2)}) collective-permute-start(bf16[2,16,1792]{2,1,0:T(8,128)(2,1)S(1)} %get-tuple-element.66), channel_id=1, source_target_pairs={{0,2},{1,3},{2,0},{3,1},{4,6},{5,7},{6,4},{7,5},{8,10},{9,11},{10,... | collective-permute-start | bytes 344072 | tf_op jit(solution)/shard_map/ppermute | solution.py:524
  38.0 8.1 %collective-permute-start.11 = (bf16[16,3584]{1,0:T(8,128)(2,1)S(1)}, bf16[16,3584]{1,0:T(8,128)(2,1)S(1)}, u32[]{:S(2)}, u32[]{:S(2)}) collective-permute-start(bf16[16,3584]{1,0:T(8,128)(2,1)S(1)} %activate_near.1.refs_0_), channel_id=1, source_target_pairs={{0,2},{1,3},{2,0},{3,1},{4,6},{5,7},{6,4},{7,5},{8,10},{9,11},{10,... | collective-permute-start | bytes 344072 | tf_op jit(solution)/shard_map/ppermute | solution.py:524
  39.3 8.9 %collective-permute-start.12 = (bf16[16,3584]{1,0:T(8,128)(2,1)S(1)}, bf16[16,3584]{1,0:T(8,128)(2,1)S(1)}, u32[]{:S(2)}, u32[]{:S(2)}) collective-permute-start(bf16[16,3584]{1,0:T(8,128)(2,1)S(1)} %activate_near.1.refs_0_), channel_id=1, source_target_pairs={{0,1},{1,0},{2,3},{3,2},{4,5},{5,4},{6,7},{7,6},{8,9},{9,8},{10,11... | collective-permute-start | bytes 344072 | tf_op jit(solution)/shard_map/ppermute | solution.py:524
  41.5 4.6 %collective-permute-start.16 = (bf16[16,1792]{1,0:T(8,128)(2,1)S(1)}, bf16[16,1792]{1,0:T(8,128)(2,1)S(1)}, u32[]{:S(2)}, u32[]{:S(2)}) collective-permute-start(bf16[16,1792]{1,0:T(8,128)(2,1)S(1)} %activate_far_0.1.refs_4_.refs_1_), channel_id=1, source_target_pairs={{0,1},{1,0},{2,3},{3,2},{4,5},{5,4},{6,7},{7,6},{8,9},{9,8},{10,11... | collective-permute-start | bytes 172040 | tf_op jit(solution)/shard_map/ppermute | solution.py:524
  41.6 5.7 %collective-permute-start.15 = (bf16[16,1792]{1,0:T(8,128)(2,1)S(1)}, bf16[16,1792]{1,0:T(8,128)(2,1)S(1)}, u32[]{:S(2)}, u32[]{:S(2)}) collective-permute-start(bf16[16,1792]{1,0:T(8,128)(2,1)S(1)} %activate_far_0.1.refs_4_.refs_1_), channel_id=1, source_target_pairs={{0,2},{1,3},{2,0},{3,1},{4,6},{5,7},{6,4},{7,5},{8,10},{9,11},{10,... | collective-permute-start | bytes 172040 | tf_op jit(solution)/shard_map/ppermute | solution.py:524
  44.0 4.2 %collective-permute-start.21 = (bf16[16,1792]{1,0:T(8,128)(2,1)S(1)}, bf16[16,1792]{1,0:T(8,128)(2,1)S(1)}, u32[]{:S(2)}, u32[]{:S(2)}) collective-permute-start(bf16[16,1792]{1,0:T(8,128)(2,1)S(1)} %activate_far_1.1.refs_8_.refs_2_), channel_id=1, source_target_pairs={{0,2},{1,3},{2,0},{3,1},{4,6},{5,7},{6,4},{7,5},{8,10},{9,11},{10,... | collective-permute-start | bytes 172040 | tf_op jit(solution)/shard_map/ppermute | solution.py:524
  46.1 3.3 %collective-permute-start.13 = (bf16[16,3584]{1,0:T(8,128)(2,1)S(1)}, bf16[16,3584]{1,0:T(8,128)(2,1)S(1)}, u32[]{:S(2)}, u32[]{:S(2)}) collective-permute-start(bf16[16,3584]{1,0:T(8,128)(2,1)S(1)} %collective-permute-done.11.refs_1_), channel_id=1, source_target_pairs={{0,1},{1,0},{2,3},{3,2},{4,5},{5,4},{6,7},{7,6},{8,9},{9,8},{10,11... | collective-permute-start | bytes 344072 | tf_op jit(solution)/shard_map/ppermute | solution.py:524
  52.4 8.6 %collective-permute-start.28 = (bf16[16,2048]{1,0:T(8,128)(2,1)S(1)}, bf16[16,2048]{1,0:T(8,128)(2,1)S(1)}, u32[]{:S(2)}, u32[]{:S(2)}) collective-permute-start(bf16[16,2048]{1,0:T(8,128)(2,1)S(1)} %get-tuple-element.78), channel_id=1, source_target_pairs={{0,8},{4,12},{8,0},{12,4},{1,9},{5,13},{9,1},{13,5},{2,10},{6,14},... | collective-permute-start | bytes 196616 | tf_op jit(solution)/shard_map/ppermute | solution.py:528
  52.9 9.5 %collective-permute-start.29 = (bf16[16,2048]{1,0:T(8,128)(2,1)S(1)}, bf16[16,2048]{1,0:T(8,128)(2,1)S(1)}, u32[]{:S(2)}, u32[]{:S(2)}) collective-permute-start(bf16[16,2048]{1,0:T(8,128)(2,1)S(1)} %get-tuple-element.79), channel_id=1, source_target_pairs={{0,4},{4,8},{8,12},{12,0},{1,5},{5,9},{9,13},{13,1},{2,6},{6,10},{... | collective-permute-start | bytes 196616 | tf_op jit(solution)/shard_map/ppermute | solution.py:528
  56.5 5.9 %collective-permute-start.30 = (bf16[16,2048]{1,0:T(8,128)(2,1)S(1)}, bf16[16,2048]{1,0:T(8,128)(2,1)S(1)}, u32[]{:S(2)}, u32[]{:S(2)}) collective-permute-start(bf16[16,2048]{1,0:T(8,128)(2,1)S(1)} %get-tuple-element.80), channel_id=1, source_target_pairs={{0,12},{4,0},{8,4},{12,8},{1,13},{5,1},{9,5},{13,9},{2,14},{6,2},{... | collective-permute-start | bytes 196616 | tf_op jit(solution)/shard_map/ppermute | solution.py:528
  58.1 6.8 %collective-permute-start.25 = (bf16[2,8,2048]{2,1,0:T(8,128)(2,1)S(1)}, bf16[2,8,2048]{2,1,0:T(8,128)(2,1)S(1)}, u32[]{:S(2)}, u32[]{:S(2)}) collective-permute-start(bf16[2,8,2048]{2,1,0:T(8,128)(2,1)S(1)} %get-tuple-element.74), channel_id=1, source_target_pairs={{0,4},{4,8},{8,12},{12,0},{1,5},{5,9},{9,13},{13,1},{2,6},{6,10},{... | collective-permute-start | bytes 196616 | tf_op jit(solution)/shard_map/ppermute | solution.py:528
  60.0 7.1 %collective-permute-start.26 = (bf16[2,8,2048]{2,1,0:T(8,128)(2,1)S(1)}, bf16[2,8,2048]{2,1,0:T(8,128)(2,1)S(1)}, u32[]{:S(2)}, u32[]{:S(2)}) collective-permute-start(bf16[2,8,2048]{2,1,0:T(8,128)(2,1)S(1)} %get-tuple-element.75), channel_id=1, source_target_pairs={{0,8},{4,12},{8,0},{12,4},{1,9},{5,13},{9,1},{13,5},{2,10},{6,14},... | collective-permute-start | bytes 196616 | tf_op jit(solution)/shard_map/ppermute | solution.py:528
  61.1 6.0 %collective-permute-start.27 = (bf16[2,8,2048]{2,1,0:T(8,128)(2,1)S(1)}, bf16[2,8,2048]{2,1,0:T(8,128)(2,1)S(1)}, u32[]{:S(2)}, u32[]{:S(2)}) collective-permute-start(bf16[2,8,2048]{2,1,0:T(8,128)(2,1)S(1)} %get-tuple-element.76), channel_id=1, source_target_pairs={{0,12},{4,0},{8,4},{12,8},{1,13},{5,1},{9,5},{13,9},{2,14},{6,2},{... | collective-permute-start | bytes 196616 | tf_op jit(solution)/shard_map/ppermute | solution.py:528
  62.4 4.6 %collective-permute-start.32 = (bf16[8,2048]{1,0:T(8,128)(2,1)S(1)}, bf16[8,2048]{1,0:T(8,128)(2,1)S(1)}, u32[]{:S(2)}, u32[]{:S(2)}) collective-permute-start(bf16[8,2048]{1,0:T(8,128)(2,1)S(1)} %get-tuple-element.84), channel_id=1, source_target_pairs={{0,3},{1,2},{2,1},{3,0},{4,7},{5,6},{6,5},{7,4},{8,11},{9,10},{10,... | collective-permute-start | bytes 98312 | tf_op jit(solution)/shard_map/ppermute | solution.py:524
  62.8 4.3 %collective-permute-start.31 = (bf16[8,2048]{1,0:T(8,128)(2,1)S(1)}, bf16[8,2048]{1,0:T(8,128)(2,1)S(1)}, u32[]{:S(2)}, u32[]{:S(2)}) collective-permute-start(bf16[8,2048]{1,0:T(8,128)(2,1)S(1)} %get-tuple-element.81.refs_4_), channel_id=1, source_target_pairs={{0,2},{1,3},{2,0},{3,1},{4,6},{5,7},{6,4},{7,5},{8,10},{9,11},{10,... | collective-permute-start | bytes 98312 | tf_op jit(solution)/shard_map/ppermute | solution.py:524
  (17 other events, 131.5 us)
